TPU v7x, 128 devices: a whole 4x4x4 slice. The times are simulated.
128 devices in a mesh: dp: 16 (over y, z), seq: 8 (over x, core).
Axes of the slice: x: 4, y: 4, z: 4, core: 2. Of those that a mesh axis runs over, the one named last changes fastest.
Arguments:
- tokens: bfloat16 [16, 1024, 2048], P('dp', 'seq'), may hold values from -6 to 6
- gain_attn: bfloat16 [2048], P(('dp', 'seq')), may hold values from 0.5 to 1.5
- w_query: bfloat16 [2048, 2048], P(('dp', 'seq')), may hold values from -0.125 to 0.125
- key_weight: bfloat16 [2048, 1024], P(('dp', 'seq')), may hold values from -0.125 to 0.125
- value_weight: bfloat16 [2048, 1024], P(('dp', 'seq')), may hold values from -0.125 to 0.125
- w_out: bfloat16 [2048, 2048], P(('dp', 'seq')), may hold values from -1 to 1
- gain_query: bfloat16 [128], P(('dp', 'seq')), may hold values from 0.5 to 1.5
- key_norm_gain: bfloat16 [128], P(('dp', 'seq')), may hold values from 0.5 to 1.5
- gain_mlp: bfloat16 [2048], P(('dp', 'seq')), may hold values from 0.5 to 1.5
- w_gate: bfloat16 [2048, 6144], P(('dp', 'seq')), may hold values from -0.125 to 0.125
- w_up: bfloat16 [2048, 6144], P(('dp', 'seq')), may hold values from -0.125 to 0.125
- w_down: bfloat16 [6144, 2048], P(('dp', 'seq')), may hold values from -0.078125 to 0.078125
- cotangent: bfloat16 [16, 1024, 2048], P('dp', 'seq'), may hold values from -6 to 6
Outputs:
- block_out: bfloat16 [16, 1024, 2048], P('dp', 'seq')
- grad_tokens: float32 [16, 1024, 2048], P('dp', 'seq')
- grad_gain_attn: float32 [2048], P(('dp', 'seq'))
- grad_w_query: float32 [2048, 2048], P(('dp', 'seq'))
- grad_w_key: float32 [2048, 1024], P(('dp', 'seq'))
- grad_w_value: float32 [2048, 1024], P(('dp', 'seq'))
- grad_w_out: float32 [2048, 2048], P(('dp', 'seq'))
- grad_gain_query: float32 [128], P(('dp', 'seq'))
- grad_gain_key: float32 [128], P(('dp', 'seq'))
- grad_gain_mlp: float32 [2048], P(('dp', 'seq'))
- grad_w_gate: float32 [2048, 6144], P(('dp', 'seq'))
- grad_w_up: float32 [2048, 6144], P(('dp', 'seq'))
- grad_w_down: float32 [6144, 2048], P(('dp', 'seq'))
All inputs are finite; a program needn't handle non-finite values.
Results may differ from a plain program's by a relative error of at most 0.035.
Values may be sent and summed in bfloat16 or wider, within the bound.
A program may use at most 512 MiB of HBM per device.

v0:
```python
import math

import jax
import jax.numpy as jnp
from jax import lax
from jax.sharding import PartitionSpec as P

QUERY_HEADS = 16
KEY_VALUE_HEADS = 8
HEAD_DIM = 128


eps_norm = 1e-06
rope_base = 1000000.0


def rope_tables(positions, half_dim):
    freqs = rope_base ** (-(jnp.arange(half_dim, dtype=jnp.float32) * 2.0 / (2 * half_dim)))
    angles = positions.astype(jnp.float32)[:, None] * freqs[None, :]
    return (jnp.cos(angles), jnp.sin(angles))


def rotate_halves(values, cosine_table, sine_table):
    half_dim = values.shape[-1] // 2
    first = values[..., :half_dim]
    second = values[..., half_dim:]
    cosine_table = cosine_table[:, None, :]
    sine_table = sine_table[:, None, :]
    return jnp.concatenate(
        [first * cosine_table - second * sine_table, second * cosine_table + first * sine_table],
        axis=-1,
    )


def inverse_rotation(grads, cosine_table, sine_table):
    half_dim = grads.shape[-1] // 2
    first = grads[..., :half_dim]
    second = grads[..., half_dim:]
    cosine_table = cosine_table[:, None, :]
    sine_table = sine_table[:, None, :]
    return jnp.concatenate(
        [first * cosine_table + second * sine_table, second * cosine_table - first * sine_table],
        axis=-1,
    )


def root_mean_square_norm(values, gain_vec):
    inv_rms = lax.rsqrt(jnp.mean(values * values, axis=-1, keepdims=True) + eps_norm)
    unit = values * inv_rms
    return (unit * gain_vec, unit, inv_rms)


def rms_back(grad_out, gain_vec, unit, inv_rms):
    grad_unit = grad_out * gain_vec
    grad_in = inv_rms * (grad_unit - unit * jnp.mean(grad_unit * unit, axis=-1, keepdims=True))
    grad_gain = jnp.sum(grad_out * unit, axis=tuple(range(grad_out.ndim - 1)))
    return (grad_in, grad_gain)


def shards(
    tokens,
    gain_attn,
    w_query,
    key_weight,
    value_weight,
    w_out,
    gain_query,
    key_norm_gain,
    gain_mlp,
    w_gate,
    w_up,
    w_down,
    cotangent,
):
    sequence_count, span_length, model_width = tokens.shape
    count_of_rows = sequence_count * span_length
    query_groups = QUERY_HEADS // KEY_VALUE_HEADS
    score_scale = 1.0 / math.sqrt(HEAD_DIM)
    f32 = jnp.float32
    brain_float_half = jnp.bfloat16
    attn_set = (
        lax.all_gather(gain_attn, ("dp", "seq"), axis=0, tiled=True),
        lax.all_gather(w_query, ("dp", "seq"), axis=0, tiled=True),
        lax.all_gather(key_weight, ("dp", "seq"), axis=0, tiled=True),
        lax.all_gather(value_weight, ("dp", "seq"), axis=0, tiled=True),
        lax.all_gather(w_out, ("dp", "seq"), axis=0, tiled=True),
        lax.all_gather(gain_query, ("dp", "seq"), axis=0, tiled=True),
        lax.all_gather(key_norm_gain, ("dp", "seq"), axis=0, tiled=True),
    )
    gain_one, query_mat, key_mat, value_mat, out_mat, gain_qn, gain_kn = attn_set
    x_flat = tokens.reshape(count_of_rows, model_width).astype(f32)
    normed_f, unit_one, inv_one = root_mean_square_norm(x_flat, gain_one.astype(f32))
    normalized_input = normed_f.astype(brain_float_half)
    query_pre = jnp.dot(normalized_input, query_mat, preferred_element_type=f32).reshape(
        sequence_count, span_length, QUERY_HEADS, HEAD_DIM
    )
    prenorm_key = jnp.dot(normalized_input, key_mat, preferred_element_type=f32).reshape(
        sequence_count, span_length, KEY_VALUE_HEADS, HEAD_DIM
    )
    value_loc = (
        jnp.dot(normalized_input, value_mat, preferred_element_type=f32)
        .astype(brain_float_half)
        .reshape(sequence_count, span_length, KEY_VALUE_HEADS * HEAD_DIM)
    )
    span_start = lax.axis_index("seq") * span_length
    cosine_table, sine_table = rope_tables(
        span_start + jnp.arange(span_length, dtype=jnp.int32), HEAD_DIM // 2
    )
    query_normed, unit_query, inv_query = root_mean_square_norm(query_pre, gain_qn.astype(f32))
    normalized_key, unit_key, inv_key = root_mean_square_norm(prenorm_key, gain_kn.astype(f32))
    local_query = rotate_halves(query_normed, cosine_table, sine_table).astype(brain_float_half)
    key_loc = (
        rotate_halves(normalized_key, cosine_table, sine_table)
        .astype(brain_float_half)
        .reshape(sequence_count, span_length, KEY_VALUE_HEADS * HEAD_DIM)
    )
    complete_keys, complete_values = (
        lax.all_gather(key_loc, "seq", axis=1, tiled=True),
        lax.all_gather(value_loc, "seq", axis=1, tiled=True),
    )
    sequence_length = complete_keys.shape[1]
    key_four_axes = complete_keys.reshape(
        sequence_count, sequence_length, KEY_VALUE_HEADS, HEAD_DIM
    )
    value_four_axes = complete_values.reshape(
        sequence_count, sequence_length, KEY_VALUE_HEADS, HEAD_DIM
    )
    query_five_axes = local_query.reshape(
        sequence_count, span_length, KEY_VALUE_HEADS, query_groups, HEAD_DIM
    )
    allowed = (
        jnp.arange(sequence_length, dtype=jnp.int32)[None, :]
        <= (span_start + jnp.arange(span_length, dtype=jnp.int32))[:, None]
    )
    scores = (
        jnp.einsum("sqhgd,skhd->shgqk", query_five_axes, key_four_axes, preferred_element_type=f32)
        * score_scale
    )
    scores = jnp.where(allowed, scores, -1e30)
    top_val = jnp.max(scores, axis=-1, keepdims=True)
    expon = jnp.exp(scores - top_val)
    totals = jnp.sum(expon, axis=-1, keepdims=True)
    log_total = top_val + jnp.log(totals)
    prob_low = (expon / totals).astype(brain_float_half)
    attn_flat = (
        jnp.einsum("shgqk,skhd->sqhgd", prob_low, value_four_axes, preferred_element_type=f32)
        .astype(brain_float_half)
        .reshape(count_of_rows, QUERY_HEADS * HEAD_DIM)
    )
    after_attn = x_flat + jnp.dot(attn_flat, out_mat, preferred_element_type=f32)
    mlp_set = (
        lax.all_gather(gain_mlp, ("dp", "seq"), axis=0, tiled=True),
        lax.all_gather(w_gate, ("dp", "seq"), axis=0, tiled=True),
        lax.all_gather(w_up, ("dp", "seq"), axis=0, tiled=True),
        lax.all_gather(w_down, ("dp", "seq"), axis=0, tiled=True),
    )
    gain_two, gate_mat, up_mat, down_mat = mlp_set
    normed_two_f, unit_two, inv_two = root_mean_square_norm(after_attn, gain_two.astype(f32))
    normed_two = normed_two_f.astype(brain_float_half)
    gate_val = jnp.dot(normed_two, gate_mat, preferred_element_type=f32)
    up_val = jnp.dot(normed_two, up_mat, preferred_element_type=f32)
    sigmoid_gate = jax.nn.sigmoid(gate_val)
    silu_gate = gate_val * sigmoid_gate
    hidden = (silu_gate * up_val).astype(brain_float_half)
    block_out = (
        (after_attn + jnp.dot(hidden, down_mat, preferred_element_type=f32))
        .astype(brain_float_half)
        .reshape(sequence_count, span_length, model_width)
    )
    gain_two, gate_mat, up_mat, down_mat = (
        lax.all_gather(gain_mlp, ("dp", "seq"), axis=0, tiled=True),
        lax.all_gather(w_gate, ("dp", "seq"), axis=0, tiled=True),
        lax.all_gather(w_up, ("dp", "seq"), axis=0, tiled=True),
        lax.all_gather(w_down, ("dp", "seq"), axis=0, tiled=True),
    )
    grad_out_f = cotangent.reshape(count_of_rows, model_width).astype(f32)
    grad_out_low = grad_out_f.astype(brain_float_half)
    grad_down = jnp.einsum("rf,rd->fd", hidden, grad_out_low, preferred_element_type=f32)
    grad_hidden = jnp.einsum("rd,fd->rf", grad_out_low, down_mat, preferred_element_type=f32)
    grad_gate_val = (
        grad_hidden * up_val * (sigmoid_gate * (1.0 + gate_val * (1.0 - sigmoid_gate)))
    ).astype(brain_float_half)
    grad_up_val = (grad_hidden * silu_gate).astype(brain_float_half)
    grad_gate = jnp.einsum("rd,rf->df", normed_two, grad_gate_val, preferred_element_type=f32)
    grad_up = jnp.einsum("rd,rf->df", normed_two, grad_up_val, preferred_element_type=f32)
    grad_normed_two = jnp.einsum(
        "rf,df->rd", grad_gate_val, gate_mat, preferred_element_type=f32
    ) + jnp.einsum("rf,df->rd", grad_up_val, up_mat, preferred_element_type=f32)
    grad_mid, grad_gain_two = rms_back(grad_normed_two, gain_two.astype(f32), unit_two, inv_two)
    grad_after = grad_out_f + grad_mid
    mlp_sums = (
        lax.psum_scatter(grad_gain_two, ("dp", "seq"), scatter_dimension=0, tiled=True),
        lax.psum_scatter(grad_gate, ("dp", "seq"), scatter_dimension=0, tiled=True),
        lax.psum_scatter(grad_up, ("dp", "seq"), scatter_dimension=0, tiled=True),
        lax.psum_scatter(grad_down, ("dp", "seq"), scatter_dimension=0, tiled=True),
    )
    gain_one, query_mat, key_mat, value_mat, out_mat, gain_qn, gain_kn = (
        lax.all_gather(gain_attn, ("dp", "seq"), axis=0, tiled=True),
        lax.all_gather(w_query, ("dp", "seq"), axis=0, tiled=True),
        lax.all_gather(key_weight, ("dp", "seq"), axis=0, tiled=True),
        lax.all_gather(value_weight, ("dp", "seq"), axis=0, tiled=True),
        lax.all_gather(w_out, ("dp", "seq"), axis=0, tiled=True),
        lax.all_gather(gain_query, ("dp", "seq"), axis=0, tiled=True),
        lax.all_gather(key_norm_gain, ("dp", "seq"), axis=0, tiled=True),
    )
    grad_after_low = grad_after.astype(brain_float_half)
    grad_out_proj = jnp.einsum("re,rd->ed", attn_flat, grad_after_low, preferred_element_type=f32)
    grad_attn = (
        jnp.einsum("rd,ed->re", grad_after_low, out_mat, preferred_element_type=f32)
        .astype(brain_float_half)
        .reshape(sequence_count, span_length, KEY_VALUE_HEADS, query_groups, HEAD_DIM)
    )
    scores_again = (
        jnp.einsum("sqhgd,skhd->shgqk", query_five_axes, key_four_axes, preferred_element_type=f32)
        * score_scale
    )
    prob_again = jnp.where(allowed, jnp.exp(scores_again - log_total), 0.0)
    prob_again_low = prob_again.astype(brain_float_half)
    grad_prob = jnp.einsum(
        "sqhgd,skhd->shgqk", grad_attn, value_four_axes, preferred_element_type=f32
    )
    row_delta = jnp.sum(prob_again * grad_prob, axis=-1, keepdims=True)
    grad_scores = (prob_again * (grad_prob - row_delta)).astype(brain_float_half)
    grad_query = (
        jnp.einsum("shgqk,skhd->sqhgd", grad_scores, key_four_axes, preferred_element_type=f32)
        * score_scale
    )
    full_key_gradient = (
        jnp.einsum("shgqk,sqhgd->skhd", grad_scores, query_five_axes, preferred_element_type=f32)
        * score_scale
    )
    full_value_gradient = jnp.einsum(
        "shgqk,sqhgd->skhd", prob_again_low, grad_attn, preferred_element_type=f32
    )
    local_key_gradient, local_value_gradient = (
        lax.psum_scatter(
            full_key_gradient.reshape(
                sequence_count, sequence_length, KEY_VALUE_HEADS * HEAD_DIM
            ).astype(jnp.bfloat16),
            "seq",
            scatter_dimension=1,
            tiled=True,
        ).astype(jnp.float32),
        lax.psum_scatter(
            full_value_gradient.reshape(
                sequence_count, sequence_length, KEY_VALUE_HEADS * HEAD_DIM
            ).astype(jnp.bfloat16),
            "seq",
            scatter_dimension=1,
            tiled=True,
        ).astype(jnp.float32),
    )
    narrow_value_gradient = local_value_gradient.astype(brain_float_half).reshape(
        count_of_rows, KEY_VALUE_HEADS * HEAD_DIM
    )
    grad_query_rot = inverse_rotation(
        grad_query.reshape(sequence_count, span_length, QUERY_HEADS, HEAD_DIM),
        cosine_table,
        sine_table,
    )
    grad_query_pre, grad_gain_qn = rms_back(
        grad_query_rot, gain_qn.astype(f32), unit_query, inv_query
    )
    rotated_key_gradient = inverse_rotation(
        local_key_gradient.reshape(sequence_count, span_length, KEY_VALUE_HEADS, HEAD_DIM),
        cosine_table,
        sine_table,
    )
    prenorm_key_gradient, grad_gain_kn = rms_back(
        rotated_key_gradient, gain_kn.astype(f32), unit_key, inv_key
    )
    grad_query_low = grad_query_pre.reshape(count_of_rows, QUERY_HEADS * HEAD_DIM).astype(
        brain_float_half
    )
    narrow_key_gradient = prenorm_key_gradient.reshape(
        count_of_rows, KEY_VALUE_HEADS * HEAD_DIM
    ).astype(brain_float_half)
    grad_query_mat = jnp.einsum(
        "rd,re->de", normalized_input, grad_query_low, preferred_element_type=f32
    )
    grad_key_mat = jnp.einsum(
        "rd,re->de", normalized_input, narrow_key_gradient, preferred_element_type=f32
    )
    grad_value_mat = jnp.einsum(
        "rd,re->de", normalized_input, narrow_value_gradient, preferred_element_type=f32
    )
    grad_normed = jnp.einsum("re,de->rd", grad_query_low, query_mat, preferred_element_type=f32)
    grad_normed = grad_normed + jnp.einsum(
        "re,de->rd", narrow_key_gradient, key_mat, preferred_element_type=f32
    )
    grad_normed = grad_normed + jnp.einsum(
        "re,de->rd", narrow_value_gradient, value_mat, preferred_element_type=f32
    )
    grad_input_norm, grad_gain_one = rms_back(grad_normed, gain_one.astype(f32), unit_one, inv_one)
    grad_input = (grad_after + grad_input_norm).reshape(sequence_count, span_length, model_width)
    attn_sums = (
        lax.psum_scatter(grad_gain_one, ("dp", "seq"), scatter_dimension=0, tiled=True),
        lax.psum_scatter(grad_query_mat, ("dp", "seq"), scatter_dimension=0, tiled=True),
        lax.psum_scatter(grad_key_mat, ("dp", "seq"), scatter_dimension=0, tiled=True),
        lax.psum_scatter(grad_value_mat, ("dp", "seq"), scatter_dimension=0, tiled=True),
        lax.psum_scatter(grad_out_proj, ("dp", "seq"), scatter_dimension=0, tiled=True),
        lax.psum_scatter(grad_gain_qn, ("dp", "seq"), scatter_dimension=0, tiled=True),
        lax.psum_scatter(grad_gain_kn, ("dp", "seq"), scatter_dimension=0, tiled=True),
    )
    return (
        block_out,
        grad_input,
        attn_sums[0],
        attn_sums[1],
        attn_sums[2],
        attn_sums[3],
        attn_sums[4],
        attn_sums[5],
        attn_sums[6],
        mlp_sums[0],
        mlp_sums[1],
        mlp_sums[2],
        mlp_sums[3],
    )


def solution(mesh):
    in_specs = (
        P("dp", "seq", None),
        P(("dp", "seq")),
        P(("dp", "seq"), None),
        P(("dp", "seq"), None),
        P(("dp", "seq"), None),
        P(("dp", "seq"), None),
        P(("dp", "seq")),
        P(("dp", "seq")),
        P(("dp", "seq")),
        P(("dp", "seq"), None),
        P(("dp", "seq"), None),
        P(("dp", "seq"), None),
        P("dp", "seq", None),
    )
    out_specs = (
        P("dp", "seq", None),
        P("dp", "seq", None),
        P(("dp", "seq")),
        P(("dp", "seq"), None),
        P(("dp", "seq"), None),
        P(("dp", "seq"), None),
        P(("dp", "seq"), None),
        P(("dp", "seq")),
        P(("dp", "seq")),
        P(("dp", "seq")),
        P(("dp", "seq"), None),
        P(("dp", "seq"), None),
        P(("dp", "seq"), None),
    )
    return jax.shard_map(shards, mesh=mesh, in_specs=in_specs, out_specs=out_specs, check_vma=False)
```

profile of v0, /device:TPU:0, one launch (start us, length us, event | category | flops | bytes accessed | tf_op | source)
XLA Modules:
  0.0 4353.3 jit_solution(10876943741793703502)
XLA Ops:
  11.9 69.4 %all-reduce.9 = (bf16[2048]{0:T(1024)(128)(2,1)S(1)}, bf16[128]{0:T(256)(128)(2,1)S(1)}, bf16[128]{0:T(256)(128)(2,1)S(1)}, bf16[2048]{0:T(1024)(128)(2,1)S(1)}) all-reduce(bf16[2048]{0:T(1024)(128)(2,1)S(1)} %dynamic-update-slice, bf16[128]{0:T(256)(128)(2,1)S(1)} %dynamic-update-slice.1, ...), channel_id=1, replica_groups=mesh['dp'=16,'seq'=8] {'dp','seq'}, use_global_device_ids=true, to_apply=%add | all-reduce | flops 4352 | bytes 17408
  82.6 3.8 convolution_convert_fusion.1
  87.5 60.6 %all-gather.13.cloned.1.call-done = bf16[2048,1024]{1,0:T(8,128)(2,1)} async-done(((bf16[16,1024]{1,0:T(8,128)(2,1)}), bf16[2048,1024]{1,0:T(8,128)(2,1)}) %all-gather.13.cloned.1.call-update) | async-done | bytes 4194320 | tf_op jit(solution)/shard_map/all_gather | solution.py:84
  148.1 3.1 fusion.89
  157.0 16.1 all-gather.27.cloned.1.call-done
  173.0 3.6 copy.119
  176.6 69.7 %all-gather.17.cloned.1.call-done = bf16[2048,2048]{1,0:T(8,128)(2,1)} async-done(((bf16[16,2048]{1,0:T(8,128)(2,1)}), bf16[2048,2048]{1,0:T(8,128)(2,1)}) %all-gather.17.cloned.1.call-update) | async-done | bytes 8388624 | tf_op jit(solution)/shard_map/all_gather | solution.py:83
  246.4 4.7 fusion.87
  252.9 20.3 all-gather.15.cloned.1.call-done
  273.2 3.6 fusion.5
  276.9 1.8 fusion.6
  278.7 1.4 copy-done
  280.1 2.9 fusion.34
  283.1 64.2 %all-gather.19.cloned.1.call-done = bf16[2048,2048]{1,0:T(8,128)(2,1)} async-done(((bf16[16,2048]{1,0:T(8,128)(2,1)}), bf16[2048,2048]{1,0:T(8,128)(2,1)}) %all-gather.19.cloned.1.call-update) | async-done | bytes 8388624 | tf_op jit(solution)/shard_map/all_gather | solution.py:86
  347.2 4.7 multiply_reduce_fusion.3
  352.2 88.8 %all-gather.21.cloned.1.call-done = bf16[2048,6144]{1,0:T(8,128)(2,1)} async-done(((bf16[16,6144]{1,0:T(8,128)(2,1)}), bf16[2048,6144]{1,0:T(8,128)(2,1)}) %all-gather.21.cloned.1.call-update) | async-done | bytes 25165840 | tf_op jit(solution)/shard_map/all_gather | solution.py:153
  441.0 13.2 fusion.94
  454.2 82.4 %all-gather.23.cloned.1.call-done = bf16[2048,6144]{1,0:T(8,128)(2,1)} async-done(((bf16[16,6144]{1,0:T(8,128)(2,1)}), bf16[2048,6144]{1,0:T(8,128)(2,1)}) %all-gather.23.cloned.1.call-update) | async-done | bytes 25165840 | tf_op jit(solution)/shard_map/all_gather | solution.py:154
  536.6 13.3 fusion.95
  549.9 82.4 %all-gather.25.cloned.1.call-done = bf16[6144,2048]{1,0:T(8,128)(2,1)} async-done(((bf16[48,2048]{1,0:T(8,128)(2,1)}), bf16[6144,2048]{1,0:T(8,128)(2,1)}) %all-gather.25.cloned.1.call-update) | async-done | bytes 25165840 | tf_op jit(solution)/shard_map/all_gather | solution.py:155
  632.3 17.2 multiply_convert_fusion
  649.5 14.3 fusion.96
  663.8 15.2 multiply_reduce_fusion
  679.0 1.7 multiply_add_fusion.1
  681.7 6.3 convolution_convert_fusion
  688.2 6.0 fusion
  694.3 4.9 fusion.11
  699.2 2.0 copy-done.2
  701.3 3.1 fusion.12
  704.4 10.9 copy.108
  715.3 4.4 copy.149
  719.7 6.5 bitcast_convert_fusion
  726.3 10.9 copy.110
  737.2 4.5 copy.148
  742.3 10.5 reduce-scatter.28.cloned.1.call-done
  752.8 2.0 reshape_bitcast_fusion.1
  757.0 2.0 copy.117
  758.9 2.0 copy.116
  766.0 4.6 fusion.83
  770.6 17.1 reduce-scatter.30.cloned.1.call-done
  789.8 4.7 fusion.56
  795.2 3.6 convolution_multiply_fusion
  799.8 2.4 copy.115
  802.3 2.5 copy.114
  804.8 1.8 multiply_add_fusion
  806.6 1.9 multiply_reduce_fusion.1
  809.2 1.6 fusion.52
  810.8 8.2 fusion.85
  820.4 8.1 fusion.72
  828.5 20.9 fusion.98
  849.5 20.9 fusion.99
  871.4 21.0 fusion.63
  893.5 6.2 fusion.97
  899.8 11.1 fusion.22
  910.9 1.5 convolution_add_fusion.1
  912.5 1.8 fusion.45
  914.3 66.4 %all-reduce.8 = (f32[2048]{0:T(1024)S(1)}, f32[128]{0:T(128)S(1)}, f32[128]{0:T(128)S(1)}, f32[2048]{0:T(1024)S(1)}) all-reduce(f32[2048]{0:T(1024)S(1)} %get-tuple-element.15, f32[128]{0:T(128)S(1)} %bitcast_reduce_fusion, f32[128]{0:T(128)S(1)} %bitcast_reduce_fusion.1, ...), channel_id=5, replica_groups=mesh['dp'=16,'seq'=8] {'dp','seq'}, use_global_device_ids=true, to_apply=%region_14.15.clone | all-reduce | flops 4352 | bytes 34816
  984.3 455.8 %reduce-scatter.16.cloned.1.call-done = f32[16,1024]{1,0:T(8,128)} async-done(((f32[2048,1024]{1,0:T(8,128)}), f32[16,1024]{1,0:T(8,128)}) %reduce-scatter.16.cloned.1.call-update) | async-done | bytes 65552 | tf_op jit(solution)/shard_map/reduce_scatter | solution.py:299
  1440.1 647.1 %reduce-scatter.18.cloned.1.call-done = f32[16,1024]{1,0:T(8,128)} async-done(((f32[2048,1024]{1,0:T(8,128)}), f32[16,1024]{1,0:T(8,128)}) %reduce-scatter.18.cloned.1.call-update) | async-done | bytes 65552 | tf_op jit(solution)/shard_map/reduce_scatter | solution.py:300
  2087.2 661.6 %reduce-scatter.14.cloned.1.call-done = f32[16,2048]{1,0:T(8,128)} async-done(((f32[2048,2048]{1,0:T(8,128)}), f32[16,2048]{1,0:T(8,128)}) %reduce-scatter.14.cloned.1.call-update) | async-done | bytes 131088 | tf_op jit(solution)/shard_map/reduce_scatter | solution.py:298
  2748.8 661.6 %reduce-scatter.20.cloned.1.call-done = f32[16,2048]{1,0:T(8,128)} async-done(((f32[2048,2048]{1,0:T(8,128)}), f32[16,2048]{1,0:T(8,128)}) %reduce-scatter.20.cloned.1.call-update) | async-done | bytes 131088 | tf_op jit(solution)/shard_map/reduce_scatter | solution.py:301
  3410.4 309.3 %reduce-scatter.22.cloned.1.call-done = f32[16,6144]{1,0:T(8,128)} async-done(((f32[2048,6144]{1,0:T(8,128)}), f32[16,6144]{1,0:T(8,128)}) %reduce-scatter.22.cloned.1.call-update) | async-done | bytes 393232 | tf_op jit(solution)/shard_map/reduce_scatter | solution.py:193
  3719.7 313.3 %reduce-scatter.24.cloned.1.call-done = f32[16,6144]{1,0:T(8,128)} async-done(((f32[2048,6144]{1,0:T(8,128)}), f32[16,6144]{1,0:T(8,128)}) %reduce-scatter.24.cloned.1.call-update) | async-done | bytes 393232 | tf_op jit(solution)/shard_map/reduce_scatter | solution.py:194
  4033.0 313.2 %reduce-scatter.26.cloned.1.call-done = f32[48,2048]{1,0:T(8,128)} async-done(((f32[6144,2048]{1,0:T(8,128)}), f32[48,2048]{1,0:T(8,128)}) %reduce-scatter.26.cloned.1.call-update) | async-done | bytes 393232 | tf_op jit(solution)/shard_map/reduce_scatter | solution.py:195
  (175 shorter events, 34.0 us)
Async XLA Ops:
  7.2 75.4 %all-gather.11.cloned.1.call-start = ((), (), s32[]{:S(2)}) async-start(), calls=%async_computation.9 | async-start | bytes 4227072 | tf_op jit(solution)/shard_map/all_gather | solution.py:85
  7.9 140.1 %all-gather.13.cloned.1.call-start = ((), (), s32[]{:S(2)}) async-start(), calls=%async_computation.10 | async-start | bytes 4227072 | tf_op jit(solution)/shard_map/all_gather | solution.py:84
  8.7 164.4 %all-gather.27.cloned.1.call-start = ((), (), s32[]{:S(2)}) async-start(), calls=%async_computation.24 | async-start | bytes 2359296 | tf_op jit(solution)/shard_map/all_gather | solution.py:119
  82.6 163.8 %copy-start.31 = (f32[128]{0:T(128)}, f32[128]{0:T(128)S(1)}, u32[]{:S(2)}) copy-start(f32[128]{0:T(128)S(1)} %add_rsqrt_fusion.3) | copy-start | bytes 1540
  86.5 159.9 %copy-start.1 = (bf16[1,128,2048]{2,1,0:T(8,128)(2,1)S(1)}, bf16[1,128,2048]{2,1,0:T(8,128)(2,1)}, u32[]{:S(2)}) copy-start(bf16[1,128,2048]{2,1,0:T(8,128)(2,1)} %param.13) | copy-start | bytes 1572868
  86.5 159.9 %all-gather.17.cloned.1.call-start = ((), (), s32[]{:S(2)}) async-start(), calls=%async_computation.12 | async-start | bytes 8454144 | tf_op jit(solution)/shard_map/all_gather | solution.py:83
  87.0 186.2 %all-gather.15.cloned.1.call-start = ((), (), s32[]{:S(2)}) async-start(), calls=%async_computation.11 | async-start | bytes 2359296 | tf_op jit(solution)/shard_map/all_gather | solution.py:118
  87.1 164.0 %copy-start.35 = (f32[128]{0:T(128)}, f32[128]{0:T(128)S(1)}, u32[]{:S(2)}) copy-start(f32[128]{0:T(128)S(1)} %convert_element_type.159) | copy-start | bytes 1540
  151.2 1.5 copy-start.21
  151.3 0.9 copy-start.13
  151.5 1.1 copy-start.30
  153.8 193.5 %all-gather.19.cloned.1.call-start = ((), (), s32[]{:S(2)}) async-start(), calls=%async_computation.13 | async-start | bytes 8454144 | tf_op jit(solution)/shard_map/all_gather | solution.py:86
  154.4 286.6 %all-gather.21.cloned.1.call-start = ((), (), s32[]{:S(2)}) async-start(), calls=%async_computation.14 | async-start | bytes 25362432 | tf_op jit(solution)/shard_map/all_gather | solution.py:153
  155.1 381.5 %all-gather.23.cloned.1.call-start = ((), (), s32[]{:S(2)}) async-start(), calls=%async_computation.15 | async-start | bytes 25362432 | tf_op jit(solution)/shard_map/all_gather | solution.py:154
  155.9 476.4 %all-gather.25.cloned.1.call-start = ((), (), s32[]{:S(2)}) async-start(), calls=%async_computation.16 | async-start | bytes 25362432 | tf_op jit(solution)/shard_map/all_gather | solution.py:155
  156.6 596.2 %reduce-scatter.28.cloned.1.call-start = ((), (), s32[]{:S(2)}) async-start(), calls=%async_computation.25 | async-start | bytes 2359296
  156.8 94.8 %copy-start.37 = (f32[128]{0:T(128)}, f32[128]{0:T(128)S(1)}, u32[]{:S(2)}) copy-start(f32[128]{0:T(128)S(1)} %convert_element_type.162) | copy-start | bytes 1540
  251.1 1.5 copy-start.11
  251.6 25.3 copy-start.28
  252.7 25.9 copy-start.15
  252.9 25.8 copy-start.17
  273.2 6.9 copy-start.9
  276.9 3.2 copy-start
  283.1 68.9 %copy-start.23 = (bf16[8,128,2,128]{3,1,2,0:T(8,128)(2,1)}, bf16[8,128,2,128]{3,1,2,0:T(8,128)(2,1)S(1)}, u32[]{:S(2)}) copy-start(bf16[8,128,2,128]{3,1,2,0:T(8,128)(2,1)S(1)} %fusion.34) | copy-start | bytes 1572868
  352.0 327.1 %copy-start.3 = (f32[128,2048]{1,0:T(8,128)}, f32[128,2048]{1,0:T(8,128)S(1)}, u32[]{:S(2)}) copy-start(f32[128,2048]{1,0:T(8,128)S(1)} %get-tuple-element.53) | copy-start | bytes 3145732
  680.7 1.0 copy-start.7
  694.3 7.0 copy-start.16
  694.3 7.0 copy-start.18
  699.2 2.1 copy-start.2
  719.7 68.0 %reduce-scatter.30.cloned.1.call-start = ((), (), s32[]{:S(2)}) async-start(), calls=%async_computation.26 | async-start | bytes 2359296
  726.3 15.4 copy-start.36
  737.2 25.0 copy-start.14
  737.2 27.7 copy-start.22
  741.6 24.3 copy-start.32
  741.7 698.4 %reduce-scatter.16.cloned.1.call-start = ((), (), s32[]{:S(2)}) async-start(), calls=%async_computation.18 | async-start | bytes 8454144 | tf_op jit(solution)/shard_map/reduce_scatter | solution.py:299
  770.6 1316.6 %reduce-scatter.18.cloned.1.call-start = ((), (), s32[]{:S(2)}) async-start(), calls=%async_computation.19 | async-start | bytes 8454144 | tf_op jit(solution)/shard_map/reduce_scatter | solution.py:300
  789.8 4.7 copy-start.25
  789.8 4.8 copy-start.38
  794.5 1954.3 %reduce-scatter.14.cloned.1.call-start = ((), (), s32[]{:S(2)}) async-start(), calls=%async_computation.17 | async-start | bytes 16908288 | tf_op jit(solution)/shard_map/reduce_scatter | solution.py:298
  798.8 10.4 copy-start.12
  804.8 3.7 copy-start.29
  804.8 4.4 copy-start.34
  810.8 8.2 copy-start.19
  819.0 1.2 copy-start.8
  819.0 1.4 copy-start.24
  819.0 2591.4 %reduce-scatter.20.cloned.1.call-start = ((), (), s32[]{:S(2)}) async-start(), calls=%async_computation.20 | async-start | bytes 16908288 | tf_op jit(solution)/shard_map/reduce_scatter | solution.py:301
  828.5 2891.3 %reduce-scatter.22.cloned.1.call-start = ((), (), s32[]{:S(2)}) async-start(), calls=%async_computation.21 | async-start | bytes 50724864 | tf_op jit(solution)/shard_map/reduce_scatter | solution.py:193
  849.4 3183.6 %reduce-scatter.24.cloned.1.call-start = ((), (), s32[]{:S(2)}) async-start(), calls=%async_computation.22 | async-start | bytes 50724864 | tf_op jit(solution)/shard_map/reduce_scatter | solution.py:194
  870.4 1.0 copy-start.27
  870.4 3475.8 %reduce-scatter.26.cloned.1.call-start = ((), (), s32[]{:S(2)}) async-start(), calls=%async_computation.23 | async-start | bytes 50724864 | tf_op jit(solution)/shard_map/reduce_scatter | solution.py:195
  892.5 1.0 copy-start.20
  892.5 7.3 copy-start.4
  892.5 7.3 copy-start.10
  899.8 11.1 copy-start.6
  899.8 12.6 copy-start.5
  899.8 12.6 copy-start.26
  910.9 3.4 copy-start.33
Sparse Core Ops, SparseCore 0:
  11.2 69.3 all-gather.10
  83.7 64.2 all-gather.12
  150.3 22.6 all-gather.26
  175.9 70.4 all-gather.16
  248.5 24.7 all-gather.14
  276.1 71.1 all-gather.18
  350.3 90.6 all-gather.20
  444.1 92.4 all-gather.22
  539.7 92.4 all-gather.24
  719.8 32.9 reduce-scatter.27
  755.2 32.4 reduce-scatter.29
  790.5 649.5 reduce-scatter.15
  1443.2 643.9 reduce-scatter.17
  2090.0 658.7 reduce-scatter.13
  2751.6 658.7 reduce-scatter.19
  3416.2 303.4 reduce-scatter.21
  3725.6 307.3 reduce-scatter.23
  4038.9 307.3 reduce-scatter.25
where the time goes:
time: 4360 us; the launch traced here: 4350 us
  waiting for transfers between devices  3880 us (89%)
  matrix products  231 us (5%)
  blocking collectives  136 us (3%)
  local copies, waits for them, and re-layouts  67.8 us (2%)
    reduce_scatter x1, waiting for transfers between devices, shards(): lax.psum_scatter(grad_query_mat, ('dp', 'seq'), scatter_dimension=0, tile...  662 us
    reduce_scatter x1, waiting for transfers between devices, shards(): lax.psum_scatter(grad_out_proj, ('dp', 'seq'), scatter_dimension=0, tiled...  662 us
    reduce_scatter x1, waiting for transfers between devices, shards(): lax.psum_scatter(grad_value_mat, ('dp', 'seq'), scatter_dimension=0, tile...  647 us
    reduce_scatter x1, waiting for transfers between devices, shards(): lax.psum_scatter(grad_key_mat, ('dp', 'seq'), scatter_dimension=0, tiled=...  456 us
    reduce_scatter x1, waiting for transfers between devices, shards(): lax.psum_scatter(grad_up, ('dp', 'seq'), scatter_dimension=0, tiled=True)  313 us
    reduce_scatter x1, waiting for transfers between devices, shards(): lax.psum_scatter(grad_down, ('dp', 'seq'), scatter_dimension=0, tiled=True)  313 us
    reduce_scatter x1, waiting for transfers between devices, shards(): lax.psum_scatter(grad_gate, ('dp', 'seq'), scatter_dimension=0, tiled=True)  309 us
    unnamed x2, blocking collectives  136 us
  transfers between devices with their start and end apart: 18, of which 17 were waited for; matrix products, arithmetic and copies ran while one was open for 5% of the time, Pallas kernels for 0%

commit v1 on v0

v1 whole, which is shorter than its diff:
```python
import math

import jax
import jax.numpy as jnp
from jax import lax
from jax.sharding import PartitionSpec as P

QUERY_HEADS = 16
KEY_VALUE_HEADS = 8
HEAD_DIM = 128

eps_norm = 1e-06
rope_base = 1000000.0

f32 = jnp.float32
bf16 = jnp.bfloat16


def rope_tables(positions, half_dim):
    freqs = rope_base ** (-(jnp.arange(half_dim, dtype=f32) * 2.0 / (2 * half_dim)))
    angles = positions.astype(f32)[:, None] * freqs[None, :]
    return (jnp.cos(angles), jnp.sin(angles))


def rotate(values, cos, sin):
    half = values.shape[-1] // 2
    a, b = values[..., :half], values[..., half:]
    cos, sin = cos[:, None, :], sin[:, None, :]
    return jnp.concatenate([a * cos - b * sin, b * cos + a * sin], axis=-1)


def unrotate(grads, cos, sin):
    half = grads.shape[-1] // 2
    a, b = grads[..., :half], grads[..., half:]
    cos, sin = cos[:, None, :], sin[:, None, :]
    return jnp.concatenate([a * cos + b * sin, b * cos - a * sin], axis=-1)


def rms(values):
    return lax.rsqrt(jnp.mean(values * values, axis=-1, keepdims=True) + eps_norm)


def rms_back(grad_out, gain, unit, inv):
    grad_unit = grad_out * gain
    return inv * (grad_unit - unit * jnp.mean(grad_unit * unit, axis=-1, keepdims=True))


def dot(a, b):
    return jnp.dot(a, b, preferred_element_type=f32)


def dot_tn(a, b):
    return lax.dot_general(a, b, (((0,), (0,)), ((), ())), preferred_element_type=f32)


def dot_nt(a, b):
    return lax.dot_general(a, b, (((1,), (1,)), ((), ())), preferred_element_type=f32)


def shards(
    tokens, gain_attn, w_query, key_weight, value_weight, w_out, gain_query,
    key_norm_gain, gain_mlp, w_gate, w_up, w_down, cotangent,
):
    nd, ns = lax.axis_size("dp"), lax.axis_size("seq")
    _, span, width = tokens.shape
    length = span * ns
    wr = w_query.shape[0]
    heads = QUERY_HEADS // ns
    qw, kw = w_query.shape[1] // ns, key_weight.shape[1] // ns
    ff = w_gate.shape[1] // ns
    fr = w_down.shape[0]
    scale = 1.0 / math.sqrt(HEAD_DIM)

    gains = jnp.concatenate([gain_attn, gain_mlp, gain_query, key_norm_gain])
    gains = jnp.broadcast_to(jnp.pad(gains, (0, 128 - gains.shape[0]))[None, :], (16, 128))
    gains = lax.all_gather(gains, ("dp", "seq"), axis=0, tiled=True).reshape(-1, 16, 128)[:, 0]
    gains = gains.astype(f32)
    gain_one = gains[:, :wr].reshape(1, width)
    gain_two = gains[:, wr : 2 * wr].reshape(1, width)
    gain_q = gains[:, 2 * wr].reshape(1, HEAD_DIM)
    gain_k = gains[:, 2 * wr + 1].reshape(1, HEAD_DIM)

    qkv_blk = jnp.concatenate(
        [
            w_query.reshape(wr, ns, qw),
            key_weight.reshape(wr, ns, kw),
            value_weight.reshape(wr, ns, kw),
        ],
        axis=2,
    )
    mlp_blk = jnp.concatenate(
        [
            w.reshape(wr, nd, ns, fr).transpose(0, 2, 1, 3).reshape(wr, ns, nd * fr)
            for w in (w_gate, w_up)
        ],
        axis=2,
    )
    qkv_blk = lax.all_to_all(qkv_blk, "seq", 1, 0, tiled=True).reshape(ns * wr, -1)
    qkv_mat = lax.all_gather(qkv_blk, "dp", axis=0, tiled=True)
    mlp_blk = lax.all_to_all(mlp_blk, "seq", 1, 0, tiled=True).reshape(ns * wr, -1)
    cw = width // nd
    out_blk = lax.all_to_all(w_out, "dp", 1, 0, tiled=True)
    out_blk = lax.all_to_all(out_blk, "seq", 0, 1, tiled=True)
    d2 = nd // ns
    out_blk = (
        out_blk.reshape(d2, wr, ns, cw).transpose(0, 2, 1, 3).reshape(d2 * ns * wr, cw)
    )
    out_mat = lax.all_gather(out_blk, "dp", axis=1, tiled=True)
    mlp_mat = lax.all_gather(mlp_blk, "dp", axis=0, tiled=True)
    gate_mat, up_mat = mlp_mat[:, :ff], mlp_mat[:, ff:]
    down_mat = lax.all_gather(w_down, "dp", axis=0, tiled=True)

    x_loc = tokens[0].astype(f32)
    x_all = lax.all_gather(tokens[0], "seq", axis=0, tiled=True).astype(f32)
    unit_one = x_all * rms(x_all)
    h1 = (unit_one * gain_one).astype(bf16)
    qkv = dot(h1, qkv_mat)
    q_pre = qkv[:, :qw].reshape(length, heads, HEAD_DIM)
    k_pre = qkv[:, qw : qw + kw].reshape(length, 1, HEAD_DIM)
    vb = qkv[:, qw + kw :].astype(bf16)
    cos, sin = rope_tables(jnp.arange(length, dtype=jnp.int32), HEAD_DIM // 2)
    inv_q, inv_k = rms(q_pre), rms(k_pre)
    unit_q, unit_k = q_pre * inv_q, k_pre * inv_k
    qb = rotate(unit_q * gain_q, cos, sin).astype(bf16)
    kb = rotate(unit_k * gain_k, cos, sin).astype(bf16)[:, 0]
    allowed = (
        jnp.arange(length, dtype=jnp.int32)[None, :]
        <= jnp.arange(length, dtype=jnp.int32)[:, None]
    )
    score = jnp.einsum("qhd,kd->hqk", qb, kb, preferred_element_type=f32) * scale
    score = jnp.where(allowed, score, -1e30)
    top = jnp.max(score, axis=-1, keepdims=True)
    expo = jnp.exp(score - top)
    prob = expo / jnp.sum(expo, axis=-1, keepdims=True)
    pb = prob.astype(bf16)
    ob = jnp.einsum("hqk,kd->qhd", pb, vb, preferred_element_type=f32)
    ob = ob.astype(bf16).reshape(length, qw)
    part = dot(ob, out_mat).astype(bf16)
    x1 = x_loc + lax.psum_scatter(part, "seq", scatter_dimension=0, tiled=True).astype(f32)

    inv_two = rms(x1)
    unit_two = x1 * inv_two
    h2_loc = (unit_two * gain_two).astype(bf16)
    h2 = lax.all_gather(h2_loc, "seq", axis=0, tiled=True)
    dy = cotangent[0].astype(f32)
    dyb = lax.all_gather(cotangent[0], "seq", axis=0, tiled=True)
    gate = dot(h2, gate_mat)
    up = dot(h2, up_mat)
    sig = jax.nn.sigmoid(gate)
    silu = gate * sig
    hid = (silu * up).astype(bf16)
    dhid = dot_nt(dyb, down_mat)
    dgate = (dhid * up * (sig * (1.0 + gate * (1.0 - sig)))).astype(bf16)
    dup = (dhid * silu).astype(bf16)
    dh2 = (dot_nt(dgate, gate_mat) + dot_nt(dup, up_mat)).astype(bf16)
    dh2 = lax.psum_scatter(dh2, "seq", scatter_dimension=0, tiled=True).astype(f32)
    dx1 = dy + rms_back(dh2, gain_two, unit_two, inv_two)
    g_gain_two = jnp.sum(dh2 * unit_two, axis=0)
    part = dot(hid, down_mat).astype(bf16)
    block = x1 + lax.psum_scatter(part, "seq", scatter_dimension=0, tiled=True).astype(f32)
    block_out = block.astype(bf16)[None]
    g_down = dot_tn(hid, dyb).astype(bf16)
    g_mlp = jnp.concatenate([dot_tn(h2, dgate), dot_tn(h2, dup)], axis=1).astype(bf16)
    g_down = lax.psum_scatter(g_down, "dp", scatter_dimension=0, tiled=True).astype(f32)
    g_mlp = lax.psum_scatter(g_mlp, "dp", scatter_dimension=0, tiled=True)
    g_mlp = lax.all_to_all(g_mlp.reshape(ns, wr, 2 * ff), "seq", 0, 0, tiled=True)
    g_mlp = g_mlp.astype(f32).reshape(ns, wr, 2, nd, fr).transpose(2, 1, 3, 0, 4)
    g_mlp = g_mlp.reshape(2, wr, nd * ns * fr)

    dab = lax.all_gather(dx1.astype(bf16), "seq", axis=0, tiled=True)
    g_out = dot_tn(ob, dab).astype(bf16)
    dob = dot_nt(dab, out_mat).astype(bf16).reshape(length, heads, HEAD_DIM)
    dprob = jnp.einsum("qhd,kd->hqk", dob, vb, preferred_element_type=f32)
    delta = jnp.sum(prob * dprob, axis=-1, keepdims=True)
    dscore = (prob * (dprob - delta)).astype(bf16)
    dq = jnp.einsum("hqk,kd->qhd", dscore, kb, preferred_element_type=f32) * scale
    dk = jnp.einsum("hqk,qhd->kd", dscore, qb, preferred_element_type=f32) * scale
    dv = jnp.einsum("hqk,qhd->kd", pb, dob, preferred_element_type=f32)
    dq = unrotate(dq, cos, sin)
    dk = unrotate(dk[:, None], cos, sin)
    g_gain_q = jnp.sum(dq * unit_q, axis=(0, 1))
    g_gain_k = jnp.sum(dk * unit_k, axis=(0, 1))
    dqp = rms_back(dq, gain_q, unit_q, inv_q).reshape(length, qw)
    dkp = rms_back(dk, gain_k, unit_k, inv_k).reshape(length, kw)
    dqkv = jnp.concatenate([dqp, dkp, dv], axis=1).astype(bf16)
    dh1 = dot_nt(dqkv, qkv_mat).astype(bf16)
    dh1 = lax.psum_scatter(dh1, "seq", scatter_dimension=0, tiled=True).astype(f32)
    inv_one = rms(x_loc)
    unit_loc = x_loc * inv_one
    grad_tokens = (dx1 + rms_back(dh1, gain_one, unit_loc, inv_one))[None]
    g_gain_one = jnp.sum(dh1 * unit_loc, axis=0)
    g_qkv = dot_tn(h1, dqkv).astype(bf16)
    g_qkv = lax.psum_scatter(g_qkv, "dp", scatter_dimension=0, tiled=True)
    g_qkv = lax.all_to_all(g_qkv.reshape(ns, wr, -1), "seq", 0, 0, tiled=True).astype(f32)
    g_q = g_qkv[:, :, :qw].transpose(1, 0, 2).reshape(wr, -1)
    g_k = g_qkv[:, :, qw : qw + kw].transpose(1, 0, 2).reshape(wr, -1)
    g_v = g_qkv[:, :, qw + kw :].transpose(1, 0, 2).reshape(wr, -1)
    g_out = lax.psum_scatter(g_out, "dp", scatter_dimension=1, tiled=True)
    g_out = g_out.reshape(d2, ns, wr, cw).transpose(0, 2, 1, 3).reshape(d2 * wr, ns * cw)
    g_out = lax.all_to_all(g_out, "seq", 1, 0, tiled=True)
    g_out = lax.all_to_all(g_out, "dp", 0, 1, tiled=True).astype(f32)

    gg = jnp.concatenate(
        [
            g_gain_one.reshape(nd * ns, wr),
            g_gain_two.reshape(nd * ns, wr),
            g_gain_q[:, None],
            g_gain_k[:, None],
        ],
        axis=1,
    )
    gg = jnp.pad(gg, ((0, 0), (0, 128 - gg.shape[1])))
    gg = lax.psum_scatter(gg, "dp", scatter_dimension=0, tiled=True)
    gg = jnp.sum(lax.all_to_all(gg[:, None], "seq", 0, 1, tiled=True)[0], axis=0)
    return (
        block_out, grad_tokens, gg[:wr], g_q, g_k, g_v, g_out,
        gg[2 * wr : 2 * wr + 1], gg[2 * wr + 1 : 2 * wr + 2], gg[wr : 2 * wr],
        g_mlp[0], g_mlp[1], g_down,
    )


def solution(mesh):
    both = P(("dp", "seq"))
    rows = P(("dp", "seq"), None)
    act = P("dp", "seq", None)
    in_specs = (act, both, rows, rows, rows, rows, both, both, both, rows, rows, rows, act)
    out_specs = (act, act, both, rows, rows, rows, rows, both, both, both, rows, rows, rows)
    return jax.shard_map(
        shards, mesh=mesh, in_specs=in_specs, out_specs=out_specs, check_vma=False
    )
```

time: 4360 us -> 986 us (0.23)
  waiting for transfers between devices: 3880 us -> 665 us
  matrix products: 231 us -> 116 us
  blocking collectives: 136 us -> 63.1 us
    reduce_scatter x7, waiting for transfers between devices: 3360 us -> 289 us  [the longest x1 71.6 us: shards(): lax.psum_scatter(g_down, 'dp', scatter_dimension=0, tiled=True).astype(f32)]
    all_gather x9 -> x8, waiting for transfers between devices: 484 us -> 218 us  [the longest x1 57.7 us: shards(): mlp_mat = lax.all_gather(mlp_blk, 'dp', axis=0, tiled=True)]
    unnamed x2 -> x0, blocking collectives: 136 us -> none
    dot_general x27 -> x20, matrix products: 231 us -> 107 us  [the longest x5 34.1 us: dot_nt(): lax.dot_general(a, b, (((1,), (1,)), ((), ())), preferred_element_type=f32)]
    unnamed x20 -> x19, waiting for transfers between devices: 32.2 us -> 146 us
  transfers between devices with their start and end apart: 18 -> 24, of which waited for: 17 -> 18; matrix products, arithmetic and copies ran while one was open for 5% -> 14% of each run, Pallas kernels for 0% -> 0%
where the time goes in v1:
time: 986 us; the launch traced here: 981 us
  waiting for transfers between devices  665 us (67%)
  matrix products  116 us (12%)
  blocking collectives  63.1 us (6%)
  local copies, waits for them, and re-layouts  44.9 us (5%)
  other arithmetic  39.6 us (4%)
  starting transfers between devices  35.2 us (4%)
  between operations  17 us (2%)
    unnamed x19, waiting for transfers between devices  146 us
    reduce_scatter x1, waiting for transfers between devices, shards(): lax.psum_scatter(g_down, 'dp', scatter_dimension=0, tiled=True).astype(f32)  71.6 us
    reduce_scatter x1, waiting for transfers between devices, shards(): g_mlp = lax.psum_scatter(g_mlp, 'dp', scatter_dimension=0, tiled=True)  68 us
    reduce_scatter x1, waiting for transfers between devices, shards(): g_qkv = lax.psum_scatter(g_qkv, 'dp', scatter_dimension=0, tiled=True)  61.1 us
    all_gather x1, waiting for transfers between devices, shards(): mlp_mat = lax.all_gather(mlp_blk, 'dp', axis=0, tiled=True)  57.7 us
    reduce_scatter x2, waiting for transfers between devices, shards(): lax.psum_scatter(part, 'seq', scatter_dimension=0, tiled=True).astype(f32)  50 us
    reduce_scatter x1, waiting for transfers between devices, shards(): lax.psum_scatter(dh2, 'seq', scatter_dimension=0, tiled=True).astype(f32)  38 us
    all_gather x1, blocking collectives, shards(): lax.all_gather(gains, ('dp', 'seq'), axis=0, tiled=True)  37.3 us
  transfers between devices with their start and end apart: 24, of which 18 were waited for; matrix products, arithmetic and copies ran while one was open for 14% of the time, Pallas kernels for 0%

profile of v1, /device:TPU:0, one launch (start us, length us, event | category | flops | bytes accessed | tf_op | source)
XLA Modules:
  0.0 980.6 jit_solution(11664671516360723979)
XLA Ops:
  10.4 10.4 %all_to_all.110 = bf16[16,8,512]{2,0,1:T(8,128)(2,1)} all-to-all(bf16[16,8,512]{2,0,1:T(8,128)(2,1)S(1)} %copy.160), channel_id=1, replica_groups=mesh['dp'=16,'seq'=8] {'seq'}, dimensions={1} | all-to-all | bytes 262144 | tf_op jit(solution)/shard_map/all_to_all | solution.py:98
  21.5 8.1 all-to-all-start.1
  31.8 37.3 %all_gather.28 = bf16[2048,128]{1,0:T(8,128)(2,1)S(1)} all-gather(bf16[16,128]{1,0:T(8,128)(2,1)S(1)} %broadcast_in_dim.22), channel_id=1, replica_groups=mesh['dp'=16,'seq'=8] {'dp','seq'}, dimensions={0}, use_global_device_ids=true | all-gather | bytes 528384 | tf_op jit(solution)/shard_map/all_gather | solution.py:76
  69.8 3.1 multiply_cosine_fusion
  74.1 3.4 all-to-all-start.2
  77.8 5.2 all-to-all-done.2
  83.9 3.1 fusion.1
  87.0 4.8 all-gather.11.cloned.1.call-done
  91.8 5.4 fusion.46
  98.5 1.6 copy.161
  103.2 8.5 fusion.105
  111.7 4.1 fusion.34
  115.9 21.4 %all-gather.13.cloned.1.call-done = bf16[256,2048]{1,0:T(8,128)(2,1)} async-done(((bf16[256,128]{1,0:T(8,128)(2,1)}), bf16[256,2048]{1,0:T(8,128)(2,1)}) %all-gather.13.cloned.1.call-update) | async-done | bytes 1048592 | tf_op jit(solution)/shard_map/all_gather | solution.py:108
  137.3 4.6 convolution_convert_fusion.1
  145.4 2.2 reshape.361
  151.0 15.4 %all_to_all.111 = bf16[16,8,1536]{2,0,1:T(8,128)(2,1)} all-to-all(bf16[16,8,1536]{2,0,1:T(8,128)(2,1)S(1)} %copy.168), channel_id=1, replica_groups=mesh['dp'=16,'seq'=8] {'seq'}, dimensions={1} | all-to-all | bytes 786432 | tf_op jit(solution)/shard_map/all_to_all | solution.py:100
  166.6 15.9 %reduce-scatter.13.cloned.1.call-done = bf16[128,2048]{1,0:T(8,128)(2,1)} async-done(((bf16[1024,2048]{1,0:T(8,128)(2,1)}), bf16[128,2048]{1,0:T(8,128)(2,1)}) %reduce-scatter.13.cloned.1.call-update) | async-done | bytes 524304 | tf_op jit(solution)/shard_map/reduce_scatter | solution.py:139
  183.9 2.0 multiply_convert_fusion.3
  187.5 57.7 %all-gather.17.cloned.1.call-done = bf16[2048,1536]{1,0:T(8,128)(2,1)} async-done(((bf16[128,1536]{1,0:T(8,128)(2,1)}), bf16[2048,1536]{1,0:T(8,128)(2,1)}) %all-gather.17.cloned.1.call-update) | async-done | bytes 6291472 | tf_op jit(solution)/shard_map/all_gather | solution.py:109
  245.1 33.8 %all-gather.15.cloned.1.call-done = bf16[1024,2048]{1,0:T(8,128)(2,1)} async-done(((bf16[128,2048]{1,0:T(8,128)(2,1)}), bf16[1024,2048]{1,0:T(8,128)(2,1)}) %all-gather.15.cloned.1.call-update) | async-done | bytes 4194320 | tf_op jit(solution)/shard_map/all_gather | solution.py:144
  279.0 8.3 fusion.20
  287.3 5.2 fusion.24
  292.5 36.8 %all-gather.19.cloned.1.call-done = bf16[768,2048]{1,0:T(8,128)(2,1)} async-done(((bf16[48,2048]{1,0:T(8,128)(2,1)}), bf16[768,2048]{1,0:T(8,128)(2,1)}) %all-gather.19.cloned.1.call-update) | async-done | bytes 3145744 | tf_op jit(solution)/shard_map/all_gather | solution.py:111
  329.3 32.6 %all-gather.25.cloned.1.call-done = bf16[1,1024,2048]{2,1,0:T(8,128)(2,1)} async-done(((bf16[1,128,2048]{2,1,0:T(8,128)(2,1)}), bf16[1,1024,2048]{2,1,0:T(8,128)(2,1)}) %all-gather.25.cloned.1.call-update) | async-done | bytes 4194320 | tf_op jit(solution)/shard_map/all_gather | solution.py:146
  361.9 10.5 %multiply_convert_fusion = (bf16[1024,768]{1,0:T(8,128)(2,1)S(1)}, bf16[1024,768]{1,0:T(8,128)(2,1)S(1)}, bf16[1024,768]{1,0:T(8,128)(2,1)}) fusion(f32[1024,768]{1,0:T(8,128)} %fusion.24, f32[1024,768]{1,0:T(8,128)} %fusion.20, bf16[768,2048]{1,0:T(8,128)(2,1)} %all-gather.19.cloned.1.call-done, bf16[1,1024,2048]{2,1,0:T(8,128)(2,1)} %all-gather.25.cloned.1.call-done), kind=kOutput, calls=%fused_computation.31 | convolution fusion | flops 3233021952 | bytes 18350080 | tf_op jit(solution)/shard_map/dot_general | solution.py:57
  372.4 6.5 fusion.22
  378.9 7.1 add_convert_fusion
  386.1 38.0 %reduce-scatter.17.cloned.1.call-done = bf16[128,2048]{1,0:T(8,128)(2,1)} async-done(((bf16[1024,2048]{1,0:T(8,128)(2,1)}), bf16[128,2048]{1,0:T(8,128)(2,1)}) %reduce-scatter.17.cloned.1.call-update) | async-done | bytes 524304 | tf_op jit(solution)/shard_map/reduce_scatter | solution.py:156
  424.1 2.2 fusion.57
  426.8 2.4 fusion.100
  429.4 31.1 %all-gather.21.cloned.1.call-done = bf16[1024,2048]{1,0:T(8,128)(2,1)} async-done(((bf16[128,2048]{1,0:T(8,128)(2,1)}), bf16[1024,2048]{1,0:T(8,128)(2,1)}) %all-gather.21.cloned.1.call-update) | async-done | bytes 4194320 | tf_op jit(solution)/shard_map/all_gather | solution.py:170
  460.5 3.9 convolution_convert_fusion.7
  464.4 5.8 fusion.48
  471.5 2.5 fusion.6
  474.0 1.6 fusion.44
  475.7 1.8 fusion.33
  479.3 1.6 multiply_reduce_fusion
  481.2 2.5 copy.174
  483.8 1.5 fusion.63
  486.1 6.1 convolution_convert_fusion
  492.6 6.3 convolution_convert_fusion.3
  499.0 3.8 convolution_convert_fusion.4
  502.7 3.8 pad_maximum_fusion
  506.5 8.7 copy.203
  516.3 3.5 convolution_convert_fusion.6
  521.3 8.0 fusion.15
  529.6 6.6 convolution_convert_fusion.5
  539.1 6.8 convolution_convert_fusion.2
  546.0 68.0 %reduce-scatter.27.cloned.1.call-done = bf16[128,1536]{1,0:T(8,128)(2,1)} async-done(((bf16[2048,1536]{1,0:T(8,128)(2,1)}), bf16[128,1536]{1,0:T(8,128)(2,1)}) %reduce-scatter.27.cloned.1.call-update) | async-done | bytes 393232 | tf_op jit(solution)/shard_map/reduce_scatter | solution.py:165
  614.0 4.2 all-to-all-start.8
  618.2 71.8 %reduce-scatter.25.cloned.1.call-done = bf16[128,256]{1,0:T(8,128)(2,1)} async-done(((bf16[2048,256]{1,0:T(8,128)(2,1)}), bf16[128,256]{1,0:T(8,128)(2,1)}) %reduce-scatter.25.cloned.1.call-update) | async-done | bytes 65552
  691.7 4.3 all-to-all-start.6
  697.2 71.6 %reduce-scatter.23.cloned.1.call-done = bf16[48,2048]{1,0:T(8,128)(2,1)} async-done(((bf16[768,2048]{1,0:T(8,128)(2,1)}), bf16[48,2048]{1,0:T(8,128)(2,1)}) %reduce-scatter.23.cloned.1.call-update) | async-done | bytes 196624 | tf_op jit(solution)/shard_map/reduce_scatter | solution.py:164
  768.8 1.7 convert_element_type.182
  770.5 2.0 reshape.376
  772.5 4.8 all-to-all-start.7
  780.5 1.9 copy.188
  785.0 61.1 %reduce-scatter.21.cloned.1.call-done = bf16[128,512]{1,0:T(8,128)(2,1)} async-done(((bf16[2048,512]{1,0:T(8,128)(2,1)}), bf16[128,512]{1,0:T(8,128)(2,1)}) %reduce-scatter.21.cloned.1.call-update) | async-done | bytes 131088 | tf_op jit(solution)/shard_map/reduce_scatter | solution.py:193
  846.1 4.3 all-to-all-start.5
  851.1 5.5 all-to-all-done.5
  857.9 72.0 %all-reduce.5.cloned.1.call-done = f32[128,128]{1,0:T(8,128)} async-done(((f32[128,128]{1,0:T(8,128)}), f32[128,128]{1,0:T(8,128)}) %all-reduce.5.cloned.1.call-update) | async-done | bytes 65552
  931.2 4.3 all-to-all-start.4
  935.5 34.0 %reduce-scatter.15.cloned.1.call-done = bf16[128,2048]{1,0:T(8,128)(2,1)} async-done(((bf16[1024,2048]{1,0:T(8,128)(2,1)}), bf16[128,2048]{1,0:T(8,128)(2,1)}) %reduce-scatter.15.cloned.1.call-update) | async-done | bytes 524304 | tf_op jit(solution)/shard_map/reduce_scatter | solution.py:160
  969.5 3.2 fusion.53
  (225 shorter events, 45.3 us)
Async XLA Ops:
  7.2 13.7 %copy-start = (bf16[16,2048]{1,0:T(8,128)(2,1)S(1)}, bf16[16,2048]{1,0:T(8,128)(2,1)}, u32[]{:S(2)}) copy-start(bf16[16,2048]{1,0:T(8,128)(2,1)} %param.18) | copy-start | bytes 196612
  7.2 76.7 %all-gather.23.cloned.1.call-start = ((), (), s32[]{:S(2)}) async-start(), calls=%async_computation.29 | async-start | bytes 4718592 | tf_op jit(solution)/shard_map/all_gather | solution.py:114
  7.9 83.9 %all-gather.11.cloned.1.call-start = ((), (), s32[]{:S(2)}) async-start(), calls=%async_computation.17 | async-start | bytes 2228224 | tf_op jit(solution)/shard_map/all_gather | solution.py:99
  21.5 52.6 %all-to-all-start.1 = ((bf16[16,16,128]{2,0,1:T(8,128)(2,1)}), bf16[16,16,128]{2,0,1:T(8,128)(2,1)}, u32[]{:S(2)}, u32[]{:S(2)}) async-start(bf16[16,16,128]{2,0,1:T(8,128)(2,1)} %copy_bitcast_fusion.5), calls=%async_computation.1 | async-start | bytes 131072 | tf_op jit(solution)/shard_map/all_to_all | solution.py:102
  31.0 69.6 %copy-start.38 = (f32[64]{0:T(128)}, f32[64]{0:T(128)S(1)}, u32[]{:S(2)}) copy-start(f32[64]{0:T(128)S(1)} %negate_power_fusion) | copy-start | bytes 772
  31.7 68.8 %copy-start.25 = (f32[1024]{0:T(1024)}, f32[1024]{0:T(1024)S(1)}, u32[]{:S(2)}) copy-start(f32[1024]{0:T(1024)S(1)} %iota_convert_fusion) | copy-start | bytes 12292
  74.1 8.9 all-to-all-start.2
  77.5 59.8 %all-gather.13.cloned.1.call-start = ((), (), s32[]{:S(2)}) async-start(), calls=%async_computation.18 | async-start | bytes 1114112 | tf_op jit(solution)/shard_map/all_gather | solution.py:108
  77.7 22.4 %copy-start.32 = (f32[128]{0:T(128)}, f32[128]{0:T(128)S(1)}, u32[]{:S(2)}) copy-start(f32[128]{0:T(128)S(1)} %get-tuple-element.21) | copy-start | bytes 1540
  77.7 22.5 %copy-start.36 = (f32[128]{0:T(128)}, f32[128]{0:T(128)S(1)}, u32[]{:S(2)}) copy-start(f32[128]{0:T(128)S(1)} %get-tuple-element.20) | copy-start | bytes 1540
  77.8 19.4 %copy-start.23 = (f32[2048]{0:T(1024)}, f32[2048]{0:T(1024)S(1)}, u32[]{:S(2)}) copy-start(f32[2048]{0:T(1024)S(1)} %mul.492) | copy-start | bytes 24580
  83.7 98.9 %reduce-scatter.13.cloned.1.call-start = ((), (), s32[]{:S(2)}) async-start(), calls=%async_computation.19 | async-start | bytes 4718592 | tf_op jit(solution)/shard_map/reduce_scatter | solution.py:139
  87.0 10.2 %copy-start.40 = (f32[1024]{0:T(1024)}, f32[1024]{0:T(1024)S(1)}, u32[]{:S(2)}) copy-start(f32[1024]{0:T(1024)S(1)} %add_rsqrt_fusion.2) | copy-start | bytes 12292
  98.4 4.7 copy-start.27
  100.0 11.7 %copy-start.4 = (f32[1024,2,128]{2,0,1:T(8,128)}, f32[1024,2,128]{2,0,1:T(8,128)S(1)}, u32[]{:S(2)}) copy-start(f32[1024,2,128]{2,0,1:T(8,128)S(1)} %copy.161) | copy-start | bytes 3145732
  101.7 10.0 %copy-start.17 = (bf16[1024,64]{0,1:T(8,128)(2,1)}, bf16[1024,64]{0,1:T(8,128)(2,1)S(1)}, u32[]{:S(2)}) copy-start(bf16[1024,64]{0,1:T(8,128)(2,1)S(1)} %get-tuple-element.40) | copy-start | bytes 393220
  111.7 4.1 copy-start.34
  115.9 26.1 %copy-start.15 = (bf16[128,2,1024]{2,0,1:T(8,128)(2,1)}, bf16[128,2,1024]{2,0,1:T(8,128)(2,1)S(1)}, u32[]{:S(2)}) copy-start(bf16[128,2,1024]{2,0,1:T(8,128)(2,1)S(1)} %fusion.34) | copy-start | bytes 1572868
  137.3 5.1 copy-start.22
  141.9 24.6 %copy-start.21 = (f32[128,16]{1,0:T(8,128)S(1)}, f32[128,16]{1,0:T(8,128)}, u32[]{:S(2)}) copy-start(f32[128,16]{1,0:T(8,128)} %get-tuple-element.43) | copy-start | bytes 24580
  142.0 40.6 %copy-start.2 = (bf16[1,128,2048]{2,1,0:T(8,128)(2,1)S(1)}, bf16[1,128,2048]{2,1,0:T(8,128)(2,1)}, u32[]{:S(2)}) copy-start(bf16[1,128,2048]{2,1,0:T(8,128)(2,1)} %param.13) | copy-start | bytes 1572868
  142.0 103.2 %all-gather.17.cloned.1.call-start = ((), (), s32[]{:S(2)}) async-start(), calls=%async_computation.21 | async-start | bytes 6684672 | tf_op jit(solution)/shard_map/all_gather | solution.py:109
  166.5 112.5 %all-gather.15.cloned.1.call-start = ((), (), s32[]{:S(2)}) async-start(), calls=%async_computation.20 | async-start | bytes 4718592 | tf_op jit(solution)/shard_map/all_gather | solution.py:144
  183.8 242.4 %copy-start.30 = (f32[128]{0:T(128)}, f32[128]{0:T(128)S(1)}, u32[]{:S(2)}) copy-start(f32[128]{0:T(128)S(1)} %add_rsqrt_fusion.4) | copy-start | bytes 1540
  185.9 143.4 %all-gather.19.cloned.1.call-start = ((), (), s32[]{:S(2)}) async-start(), calls=%async_computation.22 | async-start | bytes 3342336 | tf_op jit(solution)/shard_map/all_gather | solution.py:111
  186.7 175.2 %all-gather.25.cloned.1.call-start = ((), (), s32[]{:S(2)}) async-start(), calls=%async_computation.30 | async-start | bytes 4718592 | tf_op jit(solution)/shard_map/all_gather | solution.py:146
  187.4 236.7 %reduce-scatter.17.cloned.1.call-start = ((), (), s32[]{:S(2)}) async-start(), calls=%async_computation.24 | async-start | bytes 4718592 | tf_op jit(solution)/shard_map/reduce_scatter | solution.py:156
  279.0 8.3 copy-start.45
  279.0 8.3 copy-start.46
  372.4 6.5 copy-start.50
  372.4 6.5 copy-start.52
  386.0 38.1 %copy-start.3 = (bf16[128,2048]{1,0:T(8,128)(2,1)S(1)}, bf16[128,2048]{1,0:T(8,128)(2,1)}, u32[]{:S(2)}) copy-start(bf16[128,2048]{1,0:T(8,128)(2,1)} %reduce-scatter.13.cloned.1.call-done) | copy-start | bytes 1572868
  386.0 43.4 %copy-start.37 = (f32[128]{0:T(128)S(1)}, f32[128]{0:T(128)}, u32[]{:S(2)}) copy-start(f32[128]{0:T(128)} %copy-done.36) | copy-start | bytes 1540
  386.0 74.4 %all-gather.21.cloned.1.call-start = ((), (), s32[]{:S(2)}) async-start(), calls=%async_computation.25 | async-start | bytes 4718592 | tf_op jit(solution)/shard_map/all_gather | solution.py:170
  429.3 35.1 %copy-start.35 = (f32[2,1024]{1,0:T(2,128)S(1)}, f32[2,1024]{1,0:T(2,128)}, u32[]{:S(2)}) copy-start(f32[2,1024]{1,0:T(2,128)} %copy-done.34) | copy-start | bytes 24580
  429.3 107.4 %reduce-scatter.19.cloned.1.call-start = ((), (), s32[]{:S(2)}) async-start(), calls=%async_computation.26 | async-start | bytes 4718592 | tf_op jit(solution)/shard_map/reduce_scatter | solution.py:187
  460.5 9.7 slice-start
  464.4 5.8 slice-start.1
  492.2 121.8 %reduce-scatter.27.cloned.1.call-start = ((), (), s32[]{:S(2)}) async-start(), calls=%async_computation.32 | async-start | bytes 6684672 | tf_op jit(solution)/shard_map/reduce_scatter | solution.py:165
  492.6 6.3 copy-start.47
  492.6 6.3 copy-start.51
  515.3 174.7 %reduce-scatter.25.cloned.1.call-start = ((), (), s32[]{:S(2)}) async-start(), calls=%async_computation.31 | async-start | bytes 1114112
  521.2 247.6 %reduce-scatter.23.cloned.1.call-start = ((), (), s32[]{:S(2)}) async-start(), calls=%async_computation.28 | async-start | bytes 3342336 | tf_op jit(solution)/shard_map/reduce_scatter | solution.py:164
  521.3 8.4 copy-start.20
  521.3 8.4 copy-start.24
  521.3 8.4 copy-start.41
  529.4 7.0 copy-start.29
  529.4 7.1 copy-start.44
  529.4 9.7 copy-start.49
  529.4 316.7 %reduce-scatter.21.cloned.1.call-start = ((), (), s32[]{:S(2)}) async-start(), calls=%async_computation.27 | async-start | bytes 2228224 | tf_op jit(solution)/shard_map/reduce_scatter | solution.py:193
  536.3 393.6 %all-reduce.5.cloned.1.call-start = ((), (), s32[]{:S(2)}) async-start(), calls=%async_computation.33 | async-start | bytes 131072
  539.1 430.4 %reduce-scatter.15.cloned.1.call-start = ((), (), s32[]{:S(2)}) async-start(), calls=%async_computation.23 | async-start | bytes 4718592 | tf_op jit(solution)/shard_map/reduce_scatter | solution.py:160
  546.0 150.0 %copy-start.48 = (u32[128]{0:T(128)S(1)}, u32[128]{0:T(128)}, u32[]{:S(2)}) copy-start(u32[128]{0:T(128)} %constant.62) | copy-start | bytes 1540
  614.0 77.7 %all-to-all-start.8 = ((bf16[8,16,1536]{2,1,0:T(8,128)(2,1)}), bf16[8,16,1536]{2,1,0:T(8,128)(2,1)S(1)}, u32[]{:S(2)}, u32[]{:S(2)}) async-start(bf16[8,16,1536]{2,1,0:T(8,128)(2,1)} %bitcast.262), calls=%async_computation.13 | async-start | bytes 786432 | tf_op jit(solution)/shard_map/all_to_all | solution.py:166
  691.7 77.2 %copy-start.14 = (bf16[8,16,1536]{2,1,0:T(8,128)(2,1)}, bf16[8,16,1536]{2,1,0:T(8,128)(2,1)S(1)}, u32[]{:S(2)}) copy-start(bf16[8,16,1536]{2,1,0:T(8,128)(2,1)S(1)} %all-to-all-done.8) | copy-start | bytes 1179652
  691.7 80.8 %all-to-all-start.6 = ((bf16[32,8,128]{2,0,1:T(8,128)(2,1)}), bf16[32,8,128]{2,0,1:T(8,128)(2,1)}, u32[]{:S(2)}, u32[]{:S(2)}) async-start(bf16[32,8,128]{2,0,1:T(8,128)(2,1)} %copy.185), calls=%async_computation.11 | async-start | bytes 131072 | tf_op jit(solution)/shard_map/all_to_all | solution.py:200
  772.5 12.5 %all-to-all-start.7 = ((bf16[16,16,128]{2,1,0:T(8,128)(2,1)}), bf16[16,16,128]{2,1,0:T(8,128)(2,1)S(1)}, u32[]{:S(2)}, u32[]{:S(2)}) async-start(bf16[16,16,128]{2,1,0:T(8,128)(2,1)} %bitcast.61), calls=%async_computation.12 | async-start | bytes 131072 | tf_op jit(solution)/shard_map/all_to_all | solution.py:201
  778.5 191.0 %copy-start.6 = (bf16[128,2048]{1,0:T(8,128)(2,1)S(1)}, bf16[128,2048]{1,0:T(8,128)(2,1)}, u32[]{:S(2)}) copy-start(bf16[128,2048]{1,0:T(8,128)(2,1)} %reduce-scatter.17.cloned.1.call-done) | copy-start | bytes 1572868
  778.5 191.0 %copy-start.7 = (bf16[1,128,2048]{2,1,0:T(8,128)(2,1)S(1)}, bf16[1,128,2048]{2,1,0:T(8,128)(2,1)}, u32[]{:S(2)}) copy-start(bf16[1,128,2048]{2,1,0:T(8,128)(2,1)} %param.25) | copy-start | bytes 1572868
  778.5 191.0 %copy-start.31 = (f32[128]{0:T(128)S(1)}, f32[128]{0:T(128)}, u32[]{:S(2)}) copy-start(f32[128]{0:T(128)} %copy-done.30) | copy-start | bytes 1540
  778.5 191.0 %copy-start.43 = (f32[128]{0:T(128)S(1)}, f32[128]{0:T(128)}, u32[]{:S(2)}) copy-start(f32[128]{0:T(128)} %copy-done.42) | copy-start | bytes 1540
  780.5 193.4 %copy-start.1 = (bf16[16,2048]{1,0:T(8,128)(2,1)S(1)}, bf16[16,2048]{1,0:T(8,128)(2,1)}, u32[]{:S(2)}) copy-start(bf16[16,2048]{1,0:T(8,128)(2,1)} %param.18) | copy-start | bytes 196612
  846.1 10.4 %all-to-all-start.5 = ((bf16[8,16,512]{2,1,0:T(8,128)(2,1)}), bf16[8,16,512]{2,1,0:T(8,128)(2,1)S(1)}, u32[]{:S(2)}, u32[]{:S(2)}) async-start(bf16[8,16,512]{2,1,0:T(8,128)(2,1)} %bitcast.268), calls=%async_computation.10 | async-start | bytes 262144 | tf_op jit(solution)/shard_map/all_to_all | solution.py:194
  931.2 41.5 %all-to-all-start.4 = ((f32[8,1,128]{2,1,0:T(1,128)}), f32[8,1,128]{2,1,0:T(1,128)S(1)}, u32[]{:S(2)}, u32[]{:S(2)}) async-start(f32[8,1,128]{2,1,0:T(1,128)} %bitcast.51), calls=%async_computation.8 | async-start | bytes 8192 | tf_op jit(solution)/shard_map/all_to_all | solution.py:214
  (15 other events, 28.3 us)
Sparse Core Ops, SparseCore 0:
  9.7 34.5 all-gather.22
  46.5 45.3 all-gather.10
  94.5 42.7 all-gather.12
  142.1 40.4 reduce-scatter.12
  184.6 60.5 all-gather.16
  247.3 31.6 all-gather.14
  281.2 48.0 all-gather.18
  331.0 30.8 all-gather.24
  386.1 37.9 reduce-scatter.16
  429.4 30.9 all-gather.20
  492.3 37.7 reduce-scatter.18
  533.4 80.4 reduce-scatter.26
  617.7 72.2 reduce-scatter.24
  693.6 75.1 reduce-scatter.22
  772.3 73.8 reduce-scatter.20
  849.8 80.1 all-reduce.4
  932.3 37.1 reduce-scatter.14

commit v2 on v1

v2 whole, which is shorter than its diff:
```python
import functools
import math

import jax
import jax.numpy as jnp
import numpy as np
from jax import lax
from jax.experimental import pallas as pl
from jax.experimental.pallas import tpu as pltpu
from jax.sharding import PartitionSpec as P

QUERY_HEADS = 16
KEY_VALUE_HEADS = 8
HEAD_DIM = 128

eps_norm = 1e-06
rope_base = 1000000.0
score_scale = 1.0 / math.sqrt(HEAD_DIM)

f32 = jnp.float32
bf16 = jnp.bfloat16

AXIS = 4
ND, NS = 16, 8
SPAN = 128
WIDTH = 2048
LENGTH = SPAN * NS
WR = 16
FR = 48
FFS = ND * FR
QKV = 512
GCOL = 128
VMEM_LIMIT = 60 * 2**20
MESH = pl.DeviceIdType.MESH


def dot(a, b):
    return jnp.dot(a, b, preferred_element_type=f32)


def dot_tn(a, b):
    return lax.dot_general(a, b, (((0,), (0,)), ((), ())), preferred_element_type=f32)


def dot_nt(a, b):
    return lax.dot_general(a, b, (((1,), (1,)), ((), ())), preferred_element_type=f32)


def rms(values):
    return lax.rsqrt(jnp.mean(values * values, axis=-1, keepdims=True) + eps_norm)


def rms_back(grad_out, gain, unit, inv):
    grad_unit = grad_out * gain
    return inv * (grad_unit - unit * jnp.mean(grad_unit * unit, axis=-1, keepdims=True))


def rope_constants():
    half = HEAD_DIM // 2
    freqs = np.float32(rope_base) ** (
        -(np.arange(half, dtype=np.float32) * np.float32(2.0) / np.float32(2 * half))
    )
    angles = np.arange(LENGTH, dtype=np.float32)[:, None] * freqs.astype(np.float32)[None, :]
    cos, sin = np.cos(angles), np.sin(angles)
    return (
        np.concatenate([cos, cos], axis=1).astype(np.float32),
        np.concatenate([-sin, sin], axis=1).astype(np.float32),
    )


def coords():
    dp, sq = lax.axis_index("dp"), lax.axis_index("seq")
    return dp // AXIS, dp % AXIS, sq // 2, sq % 2


def device(y, z, x, c):
    return (y * AXIS + z, x * 2 + c)


def seq_peers(y, z, x, c):
    return [
        (k, j, device(y, z, (x + k) % AXIS, (c + j) % 2))
        for k in range(AXIS)
        for j in range(2)
        if (k, j) != (0, 0)
    ]


def barrier(peers):
    sem = pltpu.get_barrier_semaphore()
    for peer in peers:
        pl.semaphore_signal(sem, inc=1, device_id=peer, device_id_type=MESH)
    pl.semaphore_wait(sem, len(peers))


class Copies:
    def __init__(self, send, recv, local):
        self.send, self.recv, self.local = send, recv, local
        self.n, self.n_local = 0, 0
        self.sent = []

    def to(self, src, dst, dev):
        copy = pltpu.make_async_remote_copy(
            src_ref=src, dst_ref=dst, send_sem=self.send.at[self.n], recv_sem=self.recv.at[self.n],
            device_id=dev, device_id_type=MESH,
        )
        self.n += 1
        copy.start()
        self.sent.append(copy)
        return copy

    def here(self, src, dst):
        copy = pltpu.make_async_copy(src, dst, self.local.at[self.n_local])
        self.n_local += 1
        copy.start()
        return copy

    def finish(self):
        for copy in self.sent:
            copy.wait_send()
        self.sent = []


class SeqGather:
    def __init__(self, cm, own, buf, co):
        self.cm, self.own, self.buf, self.co = cm, own, buf, co
        self.half = buf.shape[1] // 2

    def slot(self, k):
        y, z, x, c = self.co
        return self.buf.at[((x + k) % AXIS) * 2 + c]

    def start(self):
        y, z, x, c = self.co
        self.sib = device(y, z, x, 1 - c)
        self.plus, self.minus = device(y, z, (x + 1) % AXIS, c), device(y, z, (x + 3) % AXIS, c)
        self.a = self.cm.to(self.own, self.slot(0), self.plus)
        self.b = self.cm.to(self.own, self.slot(0), self.minus)
        self.s0 = self.cm.to(self.own, self.slot(0), self.sib)
        self.l = self.cm.here(self.own, self.slot(0))

    def forward(self):
        h = self.half
        lo, hi = pl.ds(0, h), pl.ds(h, h)
        self.a.wait_recv()
        left = self.slot(3)
        self.fa = self.cm.to(left.at[lo], left.at[lo], self.plus)
        self.s1 = self.cm.to(left, left, self.sib)
        self.b.wait_recv()
        right = self.slot(1)
        self.fb = self.cm.to(right.at[hi], right.at[hi], self.minus)
        self.s2 = self.cm.to(right, right, self.sib)

    def last(self):
        h = self.half
        lo, hi = pl.ds(0, h), pl.ds(h, h)
        opp = self.slot(2)
        self.fa.wait_recv()
        self.s3 = self.cm.to(opp.at[lo], opp.at[lo], self.sib)
        self.fb.wait_recv()
        self.s4 = self.cm.to(opp.at[hi], opp.at[hi], self.sib)

    def wait_chip(self, k):
        if k == 0:
            self.l.wait()
            self.s0.wait_recv()
        elif k == 3:
            self.s1.wait_recv()
        elif k == 1:
            self.s2.wait_recv()
        else:
            self.s3.wait_recv()
            self.s4.wait_recv()


class DpGather:
    def __init__(self, cm, own, buf, co, axis):
        self.cm, self.own, self.buf, self.co, self.axis = cm, own, buf, co, axis
        n = own.shape[axis]
        self.h, self.q = n // 2, n // 4

    def part(self, ref, half, quarter=None):
        lo = half * self.h + (0 if quarter is None else quarter * self.q)
        size = self.h if quarter is None else self.q
        cut = pl.ds(lo, size)
        lead = len(ref.shape) - 2
        index = (slice(None),) * lead + ((cut, slice(None)) if self.axis == 0 else (slice(None), cut))
        return ref.at[index]

    def both(self, src_p, dst_p, src_m, dst_m, along):
        y, z, x, c = self.co
        if along == 0:
            plus, minus = device((y + 1) % AXIS, z, x, c), device((y + 3) % AXIS, z, x, c)
        else:
            plus, minus = device(y, (z + 1) % AXIS, x, c), device(y, (z + 3) % AXIS, x, c)
        return (self.cm.to(src_p, dst_p, plus), self.cm.to(src_m, dst_m, minus))

    def start(self):
        y, z, _, _ = self.co
        mine = self.buf.at[y, z]
        self.l = self.cm.here(self.own, mine)
        self.one = []
        for half in (0, 1):
            src, dst = self.part(self.own, half), self.part(mine, half)
            self.one.append(self.both(src, dst, src, dst, half))

    def spread(self):
        y, z, _, _ = self.co
        self.two = []
        for half in (0, 1):
            if half == 0:
                left, right = self.buf.at[(y + 3) % AXIS, z], self.buf.at[(y + 1) % AXIS, z]
            else:
                left, right = self.buf.at[y, (z + 3) % AXIS], self.buf.at[y, (z + 1) % AXIS]
            for copy in self.one[half]:
                copy.wait_recv()
            lp, rp = self.part(left, half, 0), self.part(right, half, 1)
            self.two.append(self.both(lp, lp, rp, rp, half))

    def line(self, half, k):
        y, z, _, _ = self.co
        if half == 0:
            return self.buf.at[:, (z + k) % AXIS]
        return self.buf.at[(y + k) % AXIS]

    def turn(self):
        self.l.wait()
        self.three = []
        for half in (0, 1):
            for copy in self.two[half]:
                copy.wait_recv()
            mine = self.part(self.line(half, 0), half)
            self.three.append(self.both(mine, mine, mine, mine, 1 - half))

    def last(self):
        self.four = []
        for half in (0, 1):
            for copy in self.three[half]:
                copy.wait_recv()
            lp = self.part(self.line(half, 3), half, 0)
            rp = self.part(self.line(half, 1), half, 1)
            self.four.append(self.both(lp, lp, rp, rp, 1 - half))

    def wait(self):
        for half in (0, 1):
            for copy in self.four[half]:
                copy.wait_recv()


def off(n):
    return jnp.where(n == 0, 2, jnp.where(n == 1, 1, jnp.where(n == 2, 3, 0)))


class SeqScatter:
    def __init__(self, part, sib_recv, x_recv, sems, co):
        self.part, self.sib_recv, self.x_recv, self.sems, self.co = part, sib_recv, x_recv, sems, co

    def sib_copy(self, n):
        y, z, x, c = self.co
        return pltpu.make_async_remote_copy(
            src_ref=self.part.at[2 * n], dst_ref=self.sib_recv.at[n],
            send_sem=self.sems.at[0, n], recv_sem=self.sems.at[1, n],
            device_id=device(y, z, x, 1 - c), device_id_type=MESH,
        )

    def x_copy(self, n):
        y, z, x, c = self.co
        return pltpu.make_async_remote_copy(
            src_ref=self.part.at[2 * n + 1], dst_ref=self.x_recv.at[n],
            send_sem=self.sems.at[2, n], recv_sem=self.sems.at[3, n],
            device_id=device(y, z, (x + off(n)) % AXIS, c), device_id_type=MESH,
        )

    def combine(self, n):
        self.sib_copy(n).wait_recv()
        rows = self.part.shape[1]

        def add(i, _):
            cut = pl.ds(i * 32, 32)
            total = self.part[2 * n + 1, cut, :].astype(f32) + self.sib_recv[n, cut, :].astype(f32)
            self.part[2 * n + 1, cut, :] = total.astype(bf16)
            return 0

        lax.fori_loop(0, rows // 32, add, 0)

        @pl.when(n < 3)
        def _():
            self.x_copy(n).start()

    def arrive(self):
        for n in range(3):
            self.x_copy(n).wait_recv()

    def rows(self, cut):
        total = self.part[7, cut, :].astype(f32)
        for n in range(3):
            total = total + self.x_recv[n, cut, :].astype(f32)
        return total

    def finish(self):
        for n in range(4):
            self.sib_copy(n).wait_send()
        for n in range(3):
            self.x_copy(n).wait_send()


def scatter_scratch():
    return [
        pltpu.VMEM((8, SPAN, WIDTH), bf16),
        pltpu.VMEM((4, SPAN, WIDTH), bf16),
        pltpu.VMEM((3, SPAN, WIDTH), bf16),
        pltpu.SemaphoreType.DMA((4, 4)),
    ]


def swap(u):
    return pltpu.roll(u, HEAD_DIM // 2, 1)


def attn_forward_kernel(
    tok, cot, pq, pm, wd, wo, cos, sin,
    x1_o, h2_o, h1_o, pre_o, qb, kb, vb, ob, lse, gains, gq_o, gm, gd, wo_o, cot_o,
    xg, a2a_q, a2a_m, wq, wo_b, wo_v, o1, o2, o3, part, sib_recv, x_recv, rs_sems, send, recv, local,
):
    co = y, z, x, c = coords()
    s = x * 2 + c
    peers = seq_peers(*co)
    yp = [device((y + k) % AXIS, z, x, c) for k in (1, 2, 3)]
    zp = [device(y, (z + k) % AXIS, x, c) for k in (1, 2, 3)]
    barrier([p for _, _, p in peers] + yp + zp)
    cm = Copies(send, recv, local)

    aq = []
    for k, j, p in peers:
        t = ((x + k) % AXIS) * 2 + (c + j) % 2
        aq.append(cm.to(pq.at[t], a2a_q.at[s], p))
    lq = cm.here(pq.at[s], a2a_q.at[s])
    g_tok = SeqGather(cm, tok, xg, co)
    g_tok.start()
    o_one = [
        cm.to(wo.at[:, pl.ds(pl.multiple_of(((y + k) % AXIS) * 512, 512), 512)], o1.at[y], yp[k - 1])
        for k in (1, 2, 3)
    ]
    l_one = cm.here(wo.at[:, pl.ds(pl.multiple_of(y * 512, 512), 512)], o1.at[y])
    g_d = DpGather(cm, wd, gd, co, 1)
    g_d.start()
    am = []
    for k, j, p in peers:
        t = ((x + k) % AXIS) * 2 + (c + j) % 2
        am.append(cm.to(pm.at[t], a2a_m.at[s], p))
    lm = cm.here(pm.at[s], a2a_m.at[s])
    lq.wait()
    for copy in aq:
        copy.wait_recv()
    g_q = DpGather(cm, a2a_q.reshape(NS * WR, QKV + GCOL), gq_o, co, 0)
    g_q.start()
    l_one.wait()
    for copy in o_one:
        copy.wait_recv()
    o_two = [
        cm.to(o1.at[:, :, pl.ds(pl.multiple_of(((z + k) % AXIS) * 128, 128), 128)], o2.at[z], zp[k - 1])
        for k in (1, 2, 3)
    ]
    l_two = cm.here(o1.at[:, :, pl.ds(pl.multiple_of(z * 128, 128), 128)], o2.at[z])
    g_tok.forward()
    g_q.spread()
    g_q.turn()
    lm.wait()
    for copy in am:
        copy.wait_recv()
    g_m = DpGather(cm, a2a_m.reshape(NS * WR, 2 * FFS), gm, co, 0)
    g_m.start()
    l_two.wait()
    for copy in o_two:
        copy.wait_recv()
    o_three = []
    for k, j, p in peers:
        t = ((x + k) % AXIS) * 2 + (c + j) % 2
        for h in range(2):
            o_three.append(cm.to(o2.at[(t % 2) * 2 + h, t // 2], o3.at[h, s], p))
    l_three = [cm.here(o2.at[(s % 2) * 2 + h, s // 2], o3.at[h, s]) for h in range(2)]
    g_tok.last()
    g_d.spread()
    g_q.last()
    for copy in l_three:
        copy.wait()
    for copy in o_three:
        copy.wait_recv()
    g_o = DpGather(cm, o3.reshape(2 * SPAN, SPAN), wo_b, co, 0)
    g_o.start()
    g_cot = SeqGather(cm, cot, cot_o, co)
    for k in (0, 1, 3, 2):
        g_tok.wait_chip(k)
    g_cot.start()
    g_m.spread()
    g_o.spread()
    g_q.wait()
    wq_copy = [
        cm.here(gq_o.at[yy], wq.at[pl.ds(yy * AXIS, AXIS)]) for yy in range(AXIS)
    ]
    g_o.turn()
    g_d.turn()
    g_m.turn()
    for copy in wq_copy:
        copy.wait()

    wq2 = wq.reshape(WIDTH, QKV + GCOL)
    gcols = wq2[:, QKV:]
    flat = gcols.astype(f32).T
    gains[...] = flat[:8]
    gain_one, gain_two = flat[0:1], flat[1:2]
    rows = lax.broadcasted_iota(jnp.int32, (WIDTH, HEAD_DIM), 0)
    cols = lax.broadcasted_iota(jnp.int32, (WIDTH, HEAD_DIM), 1)
    pick = (rows == cols * WR).astype(bf16)
    head_gains = dot_tn(gcols, pick)
    gain_q, gain_k = head_gains[2:3], head_gains[3:4]
    gains[2:4, 0:HEAD_DIM] = head_gains[2:4]

    def normed(i, _):
        cut = pl.ds(i * 32, 32)
        v = xg[i // 4, pl.ds((i % 4) * 32, 32), :].astype(f32)
        part[i // 4, pl.ds((i % 4) * 32, 32), :] = (v * rms(v) * gain_one).astype(bf16)
        return 0

    lax.fori_loop(0, LENGTH // 32, normed, 0)
    h1_copy = cm.here(part, h1_o)

    def project(i, _):
        h = part[pl.ds(2 * i, 2)].reshape(2 * SPAN, WIDTH)
        p = dot(h, wq2[:, :QKV])
        cut = pl.ds(pl.multiple_of(i * 256, 256), 256)
        pre_o[cut, :] = p[:, :384]
        vb[cut, :] = p[:, 384:].astype(bf16)
        co_t, si_t = cos[cut, :], sin[cut, :]
        for h_i in range(2):
            u = p[:, h_i * 128 : h_i * 128 + 128]
            u = u * rms(u) * gain_q
            u = (u * co_t + swap(u) * si_t).astype(bf16)
            qb[pl.ds(2 * i, 2), pl.ds(h_i * SPAN, SPAN), :] = u.reshape(2, SPAN, HEAD_DIM)
        u = p[:, 256:384]
        u = u * rms(u) * gain_k
        kb[cut, :] = (u * co_t + swap(u) * si_t).astype(bf16)
        return 0

    lax.fori_loop(0, 4, project, 0)
    g_cot.forward()
    g_o.last()
    h1_copy.wait()
    g_o.wait()
    wo_copy = [
        cm.here(wo_b.at[yy, zz], wo_v.at[:, pl.ds((yy * AXIS + zz) * 128, 128)])
        for yy in range(AXIS)
        for zz in range(AXIS)
    ]
    for copy in wo_copy:
        copy.wait()
    wo_out = cm.here(wo_v, wo_o)

    rs = SeqScatter(part, sib_recv, x_recv, rs_sems, co)

    def attend(i, slot):
        sc = dot_nt(qb[i], kb[...]) * score_scale
        r = lax.broadcasted_iota(jnp.int32, (2 * SPAN, LENGTH), 0) % SPAN + i * SPAN
        k = lax.broadcasted_iota(jnp.int32, (2 * SPAN, LENGTH), 1)
        sc = jnp.where(k <= r, sc, -1e30)
        top = jnp.max(sc, axis=-1, keepdims=True)
        ex = jnp.exp(sc - top)
        tot = jnp.sum(ex, axis=-1, keepdims=True)
        lse[i] = jnp.broadcast_to(top + jnp.log(tot), (2 * SPAN, 128))
        pb = (ex / tot).astype(bf16)
        o = dot(pb, vb[...]).astype(bf16)
        o = jnp.concatenate([o[:SPAN], o[SPAN:]], axis=1)
        ob[pl.ds(pl.multiple_of(i * SPAN, SPAN), SPAN), :] = o
        part[slot] = dot(o, wo_v[...]).astype(bf16)

    def pair(n, _):
        chip = (x + off(n)) % AXIS
        attend(chip * 2 + 1 - c, 2 * n)
        rs.sib_copy(n).start()
        attend(chip * 2 + c, 2 * n + 1)
        rs.combine(n)
        return 0

    lax.fori_loop(0, 4, pair, 0)
    g_cot.last()
    g_d.last()
    g_m.last()
    rs.arrive()

    def residual(i, _):
        cut = pl.ds(i * 32, 32)
        v = xg[s, cut, :].astype(f32) + rs.rows(cut)
        x1_o[cut, :] = v
        h2_o[cut, :] = (v * rms(v) * gains[1:2, :]).astype(bf16)
        return 0

    lax.fori_loop(0, SPAN // 32, residual, 0)
    rs.finish()
    wo_out.wait()
    for k in (0, 1, 3, 2):
        g_cot.wait_chip(k)
    g_d.wait()
    g_m.wait()
    cm.finish()


def attn_forward(tok, cot, pq, pm, wd, wo, cos, sin):
    any_, vm = pl.BlockSpec(memory_space=pl.ANY), pl.BlockSpec(memory_space=pltpu.VMEM)
    sds = jax.ShapeDtypeStruct
    n_copies, n_local = 160, 48
    return pl.pallas_call(
        attn_forward_kernel,
        name="attn_forward",
        out_shape=[
            sds((SPAN, WIDTH), f32), sds((SPAN, WIDTH), bf16), sds((8, SPAN, WIDTH), bf16),
            sds((LENGTH, 384), f32), sds((8, 2 * SPAN, 128), bf16), sds((LENGTH, 128), bf16),
            sds((LENGTH, 128), bf16), sds((LENGTH, 256), bf16), sds((8, 2 * SPAN, 128), f32),
            sds((8, WIDTH), f32), sds((4, 4, 128, QKV + GCOL), bf16), sds((4, 4, 128, 2 * FFS), bf16),
            sds((4, 4, FR, WIDTH), bf16), sds((256, WIDTH), bf16), sds((8, SPAN, WIDTH), bf16),
        ],
        in_specs=[any_] * 6 + [vm] * 2,
        out_specs=[vm, vm, any_, vm, vm, vm, vm, vm, vm, vm, any_, any_, any_, any_, any_],
        scratch_shapes=[
            pltpu.VMEM((8, SPAN, WIDTH), bf16),
            pltpu.VMEM((NS, WR, QKV + GCOL), bf16),
            pltpu.VMEM((NS, WR, 2 * FFS), bf16),
            pltpu.VMEM((ND, 128, QKV + GCOL), bf16),
            pltpu.VMEM((4, 4, 256, 128), bf16),
            pltpu.VMEM((256, WIDTH), bf16),
            pltpu.VMEM((4, WR, 512), bf16),
            pltpu.VMEM((4, 4, WR, 128), bf16),
            pltpu.VMEM((2, NS, WR, 128), bf16),
            *scatter_scratch(),
            pltpu.SemaphoreType.DMA((n_copies,)),
            pltpu.SemaphoreType.DMA((n_copies,)),
            pltpu.SemaphoreType.DMA((n_local,)),
        ],
        compiler_params=pltpu.CompilerParams(
            collective_id=1, has_side_effects=True, vmem_limit_bytes=VMEM_LIMIT
        ),
    )(tok, cot, pq, pm, wd, wo, cos, sin)


def shards(
    tokens, gain_attn, w_query, key_weight, value_weight, w_out, gain_query,
    key_norm_gain, gain_mlp, w_gate, w_up, w_down, cotangent,
):
    qw, kw = 256, 128
    extra = jnp.stack(
        [
            gain_attn,
            gain_mlp,
            jnp.broadcast_to(gain_query, (WR,)),
            jnp.broadcast_to(key_norm_gain, (WR,)),
        ],
        axis=1,
    )
    extra = jnp.broadcast_to(jnp.pad(extra, ((0, 0), (0, GCOL - 4)))[:, None], (WR, NS, GCOL))
    pq = jnp.concatenate(
        [
            w_query.reshape(WR, NS, qw),
            key_weight.reshape(WR, NS, kw),
            value_weight.reshape(WR, NS, kw),
            extra,
        ],
        axis=2,
    ).transpose(1, 0, 2)
    pm = jnp.concatenate(
        [
            w.reshape(WR, ND, NS, FR).transpose(2, 0, 1, 3).reshape(NS, WR, FFS)
            for w in (w_gate, w_up)
        ],
        axis=2,
    )
    cos, sin = rope_constants()
    (x1, h2_loc, h1, pre, qb, kb, vb, ob, lse, gains, gq, gm, gd, wo, dyb) = attn_forward(
        tokens[0], cotangent[0], pq, pm, w_down, w_out, cos, sin
    )
    gain_one, gain_two = gains[0:1], gains[1:2]
    gain_q, gain_k = gains[2:3, :128], gains[3:4, :128]
    qkv_mat = gq.reshape(WIDTH, QKV + GCOL)[:, :QKV]
    mlp_mat = gm.reshape(WIDTH, 2 * FFS)
    gate_mat, up_mat = mlp_mat[:, :FFS], mlp_mat[:, FFS:]
    down_mat = gd.reshape(FFS, WIDTH)
    h1 = h1.reshape(LENGTH, WIDTH)
    dyb = dyb.reshape(LENGTH, WIDTH)
    x_loc = tokens[0].astype(f32)
    heads = 2
    length, ns, nd, wr, ff, fr, out_mat = LENGTH, NS, ND, WR, FFS, FR, wo
    d2, cw = 2, 128
    q_pre = pre[:, :qw].reshape(length, heads, HEAD_DIM)
    k_pre = pre[:, qw:].reshape(length, 1, HEAD_DIM)
    inv_q, inv_k = rms(q_pre), rms(k_pre)
    unit_q, unit_k = q_pre * inv_q, k_pre * inv_k
    qb = qb.reshape(8, 2, SPAN, HEAD_DIM).transpose(0, 2, 1, 3).reshape(length, heads, HEAD_DIM)
    lse = lse[:, :, 0].reshape(8, 2, SPAN).transpose(1, 0, 2).reshape(2, length, 1)
    cos_h, sin_h = jnp.asarray(cos[:, :64]), jnp.asarray(sin[:, 64:])

    def unrotate(grads):
        a, b = grads[..., :64], grads[..., 64:]
        co, si = cos_h[:, None, :], sin_h[:, None, :]
        return jnp.concatenate([a * co + b * si, b * co - a * si], axis=-1)

    inv_two = rms(x1)
    unit_two = x1 * inv_two
    h2 = lax.all_gather(h2_loc, "seq", axis=0, tiled=True)
    dy = cotangent[0].astype(f32)
    gate = dot(h2, gate_mat)
    up = dot(h2, up_mat)
    sig = jax.nn.sigmoid(gate)
    silu = gate * sig
    hid = (silu * up).astype(bf16)
    dhid = dot_nt(dyb, down_mat)
    dgate = (dhid * up * (sig * (1.0 + gate * (1.0 - sig)))).astype(bf16)
    dup = (dhid * silu).astype(bf16)
    dh2 = (dot_nt(dgate, gate_mat) + dot_nt(dup, up_mat)).astype(bf16)
    dh2 = lax.psum_scatter(dh2, "seq", scatter_dimension=0, tiled=True).astype(f32)
    dx1 = dy + rms_back(dh2, gain_two, unit_two, inv_two)
    g_gain_two = jnp.sum(dh2 * unit_two, axis=0)
    part = dot(hid, down_mat).astype(bf16)
    block = x1 + lax.psum_scatter(part, "seq", scatter_dimension=0, tiled=True).astype(f32)
    block_out = block.astype(bf16)[None]
    g_down = dot_tn(hid, dyb).astype(bf16)
    g_mlp = jnp.concatenate([dot_tn(h2, dgate), dot_tn(h2, dup)], axis=1).astype(bf16)
    g_down = lax.psum_scatter(g_down, "dp", scatter_dimension=0, tiled=True).astype(f32)
    g_mlp = lax.psum_scatter(g_mlp, "dp", scatter_dimension=0, tiled=True)
    g_mlp = lax.all_to_all(g_mlp.reshape(ns, wr, 2 * ff), "seq", 0, 0, tiled=True)
    g_mlp = g_mlp.astype(f32).reshape(ns, wr, 2, nd, fr).transpose(2, 1, 3, 0, 4)
    g_mlp = g_mlp.reshape(2, wr, nd * ns * fr)

    allowed = (
        jnp.arange(length, dtype=jnp.int32)[None, :]
        <= jnp.arange(length, dtype=jnp.int32)[:, None]
    )
    score = jnp.einsum("qhd,kd->hqk", qb, kb, preferred_element_type=f32) * score_scale
    prob = jnp.where(allowed, jnp.exp(score - lse), 0.0)
    pb = prob.astype(bf16)
    dab = lax.all_gather(dx1.astype(bf16), "seq", axis=0, tiled=True)
    g_out = dot_tn(ob, dab).astype(bf16)
    dob = dot_nt(dab, out_mat).astype(bf16).reshape(length, heads, HEAD_DIM)
    dprob = jnp.einsum("qhd,kd->hqk", dob, vb, preferred_element_type=f32)
    delta = jnp.sum(prob * dprob, axis=-1, keepdims=True)
    dscore = (prob * (dprob - delta)).astype(bf16)
    dq = jnp.einsum("hqk,kd->qhd", dscore, kb, preferred_element_type=f32) * score_scale
    dk = jnp.einsum("hqk,qhd->kd", dscore, qb, preferred_element_type=f32) * score_scale
    dv = jnp.einsum("hqk,qhd->kd", pb, dob, preferred_element_type=f32)
    dq = unrotate(dq)
    dk = unrotate(dk[:, None])
    g_gain_q = jnp.sum(dq * unit_q, axis=(0, 1))
    g_gain_k = jnp.sum(dk * unit_k, axis=(0, 1))
    dqp = rms_back(dq, gain_q, unit_q, inv_q).reshape(length, qw)
    dkp = rms_back(dk, gain_k, unit_k, inv_k).reshape(length, kw)
    dqkv = jnp.concatenate([dqp, dkp, dv], axis=1).astype(bf16)
    dh1 = dot_nt(dqkv, qkv_mat).astype(bf16)
    dh1 = lax.psum_scatter(dh1, "seq", scatter_dimension=0, tiled=True).astype(f32)
    inv_one = rms(x_loc)
    unit_loc = x_loc * inv_one
    grad_tokens = (dx1 + rms_back(dh1, gain_one, unit_loc, inv_one))[None]
    g_gain_one = jnp.sum(dh1 * unit_loc, axis=0)
    g_qkv = dot_tn(h1, dqkv).astype(bf16)
    g_qkv = lax.psum_scatter(g_qkv, "dp", scatter_dimension=0, tiled=True)
    g_qkv = lax.all_to_all(g_qkv.reshape(ns, wr, -1), "seq", 0, 0, tiled=True).astype(f32)
    g_q = g_qkv[:, :, :qw].transpose(1, 0, 2).reshape(wr, -1)
    g_k = g_qkv[:, :, qw : qw + kw].transpose(1, 0, 2).reshape(wr, -1)
    g_v = g_qkv[:, :, qw + kw :].transpose(1, 0, 2).reshape(wr, -1)
    g_out = lax.psum_scatter(g_out, "dp", scatter_dimension=1, tiled=True)
    g_out = g_out.reshape(d2, ns, wr, cw).transpose(0, 2, 1, 3).reshape(d2 * wr, ns * cw)
    g_out = lax.all_to_all(g_out, "seq", 1, 0, tiled=True)
    g_out = lax.all_to_all(g_out, "dp", 0, 1, tiled=True).astype(f32)

    gg = jnp.concatenate(
        [
            g_gain_one.reshape(nd * ns, wr),
            g_gain_two.reshape(nd * ns, wr),
            g_gain_q[:, None],
            g_gain_k[:, None],
        ],
        axis=1,
    )
    gg = jnp.pad(gg, ((0, 0), (0, 128 - gg.shape[1])))
    gg = lax.psum_scatter(gg, "dp", scatter_dimension=0, tiled=True)
    gg = jnp.sum(lax.all_to_all(gg[:, None], "seq", 0, 1, tiled=True)[0], axis=0)
    return (
        block_out, grad_tokens, gg[:wr], g_q, g_k, g_v, g_out,
        gg[2 * wr : 2 * wr + 1], gg[2 * wr + 1 : 2 * wr + 2], gg[wr : 2 * wr],
        g_mlp[0], g_mlp[1], g_down,
    )


def solution(mesh):
    both = P(("dp", "seq"))
    rows = P(("dp", "seq"), None)
    act = P("dp", "seq", None)
    in_specs = (act, both, rows, rows, rows, rows, both, both, both, rows, rows, rows, act)
    out_specs = (act, act, both, rows, rows, rows, rows, both, both, both, rows, rows, rows)
    return jax.shard_map(
        shards, mesh=mesh, in_specs=in_specs, out_specs=out_specs, check_vma=False
    )
```

time: 986 us -> 788 us (0.80)
  waiting for transfers between devices: 665 us -> 454 us
  Pallas kernels: 0 us -> 114 us
  blocking collectives: 63.1 us -> 0 us
  matrix products: 116 us -> 84.3 us
  local copies, waits for them, and re-layouts: 44.9 us -> 59.4 us
  starting transfers between devices: 35.2 us -> 23.2 us
  other arithmetic: 39.6 us -> 28.2 us
    all_gather x6 -> x0, waiting for transfers between devices: 153 us -> none  [the longest x1 57.7 us: shards(): mlp_mat = lax.all_gather(mlp_blk, 'dp', axis=0, tiled=True)]
    pallas_call x0 -> x1, Pallas kernels: none -> 114 us  [attn_forward(): pl.pallas_call(attn_forward_kernel, name='attn_forward', out_shape=[sds((...]
    all_gather x1 -> x0, blocking collectives: 37.3 us -> none  [shards(): lax.all_gather(gains, ('dp', 'seq'), axis=0, tiled=True)]
    all_to_all x2 -> x0, blocking collectives: 25.8 us -> none  [the longest x1 15.4 us: shards(): lax.all_to_all(mlp_blk, 'seq', 1, 0, tiled=True).reshape(ns * wr, -1)]
    all_gather x1, waiting for transfers between devices: 31.1 us -> 9.38 us  [shards(): dab = lax.all_gather(dx1.astype(bf16), 'seq', axis=0, tiled=True)]
    reduce_scatter x2 -> x1, waiting for transfers between devices: 50 us -> 34.1 us  [shards(): lax.psum_scatter(part, 'seq', scatter_dimension=0, tiled=True).astype(f32)]
    dot_general x5 -> x3, matrix products: 30.3 us -> 17.5 us  [dot(): return jnp.dot(a, b, preferred_element_type=f32)]
    dot_general x5, matrix products: 34.1 us -> 22.4 us  [dot_nt(): lax.dot_general(a, b, (((1,), (1,)), ((), ())), preferred_element_type=f32)]
  transfers between devices with their start and end apart: 24 -> 15, of which waited for: 18 -> 10; matrix products, arithmetic and copies ran while one was open for 14% -> 13% of each run, Pallas kernels for 0% -> 0%
where the time goes in v2:
time: 788 us; the launch traced here: 780 us
  waiting for transfers between devices  454 us (58%)
  Pallas kernels  114 us (14%)
  matrix products  84.3 us (11%)
  local copies, waits for them, and re-layouts  59.4 us (8%)
  other arithmetic  28.2 us (4%)
  starting transfers between devices  23.2 us (3%)
  between operations  17.2 us (2%)
    unnamed x12, waiting for transfers between devices  143 us
    pallas_call x1, Pallas kernels, attn_forward(): pl.pallas_call(attn_forward_kernel, name='attn_forward', out_shape=[sds((...  114 us
    reduce_scatter x1, waiting for transfers between devices, shards(): lax.psum_scatter(g_down, 'dp', scatter_dimension=0, tiled=True).astype(f32)  71.8 us
    reduce_scatter x1, waiting for transfers between devices, shards(): g_mlp = lax.psum_scatter(g_mlp, 'dp', scatter_dimension=0, tiled=True)  67.8 us
    reduce_scatter x1, waiting for transfers between devices, shards(): g_qkv = lax.psum_scatter(g_qkv, 'dp', scatter_dimension=0, tiled=True)  56.1 us
    reduce_scatter x1, waiting for transfers between devices, shards(): lax.psum_scatter(dh2, 'seq', scatter_dimension=0, tiled=True).astype(f32)  35.6 us
    reduce_scatter x1, waiting for transfers between devices, shards(): lax.psum_scatter(part, 'seq', scatter_dimension=0, tiled=True).astype(f32)  34.1 us
    all_gather x1, waiting for transfers between devices, shards(): h2 = lax.all_gather(h2_loc, 'seq', axis=0, tiled=True)  30.3 us
  transfers between devices with their start and end apart: 15, of which 10 were waited for; matrix products, arithmetic and copies ran while one was open for 13% of the time, Pallas kernels for 0%

profile of v2, /device:TPU:0, one launch (start us, length us, event | category | flops | bytes accessed | tf_op | source)
XLA Modules:
  0.0 780.1 jit_solution(3738831822858974457)
XLA Ops:
  10.4 1.4 reshape.223
  12.4 1.4 reshape.225
  15.9 113.8 %attn_forward.1 = (f32[128,2048]{1,0:T(8,128)}, bf16[128,2048]{1,0:T(8,128)(2,1)}, bf16[8,128,2048]{2,1,0:T(8,128)(2,1)}, f32[1024,384]{1,0:T(8,128)}, bf16[8,25...) custom-call(bf16[128,2048]{1,0:T(8,128)(2,1)} %bitcast.214, ...), custom_call_target="tpu_custom_call" | custom-call | tf_op jit(solution)/shard_map/attn_forward/pallas_call | solution.py:511
  130.1 30.3 %all-gather.3.cloned.1.call-done = bf16[1024,2048]{1,0:T(8,128)(2,1)} async-done(((bf16[128,2048]{1,0:T(8,128)(2,1)}), bf16[1024,2048]{1,0:T(8,128)(2,1)}) %all-gather.3.cloned.1.call-update) | async-done | bytes 4194320 | tf_op jit(solution)/shard_map/all_gather | solution.py:606
  160.4 6.3 fusion.11
  166.7 3.4 fusion.15
  170.2 5.6 multiply_convert_fusion
  175.8 3.4 fusion.13
  179.2 5.0 add_convert_fusion
  186.7 35.6 %reduce-scatter.14.cloned.1.call-done = bf16[128,2048]{1,0:T(8,128)(2,1)} async-done(((bf16[1024,2048]{1,0:T(8,128)(2,1)}), bf16[128,2048]{1,0:T(8,128)(2,1)}) %reduce-scatter.14.cloned.1.call-update) | async-done | bytes 524304 | tf_op jit(solution)/shard_map/reduce_scatter | solution.py:617
  222.2 1.4 fusion.38
  223.7 2.2 fusion.55
  226.4 1.6 copy.257
  227.9 2.1 copy.255
  230.0 2.1 reshape.232
  233.2 1.8 reshape.230
  235.0 1.3 copy.262
  236.3 2.0 multiply_reduce_fusion.2
  238.2 1.2 copy.253
  239.6 1.3 copy.288
  240.9 1.3 multiply_reduce_fusion.6
  243.3 4.5 fusion.48
  247.8 9.4 %all-gather.5.cloned.1.call-done = bf16[1024,2048]{1,0:T(8,128)(2,1)} async-done(((bf16[128,2048]{1,0:T(8,128)(2,1)}), bf16[1024,2048]{1,0:T(8,128)(2,1)}) %all-gather.5.cloned.1.call-update) | async-done | bytes 4194320 | tf_op jit(solution)/shard_map/all_gather | solution.py:638
  257.2 3.9 convolution_convert_fusion.7
  261.1 5.9 fusion.29
  267.1 3.3 fusion
  270.4 2.9 fusion.2
  273.2 2.1 fusion.28
  276.7 1.2 pad_maximum_fusion.1
  277.8 2.5 copy.290
  281.4 1.9 add_bitcast_fusion
  284.3 1.2 mul.328
  286.7 4.4 convolution_convert_fusion
  291.2 6.3 convolution_convert_fusion.3
  297.5 4.0 convolution_convert_fusion.4
  301.5 3.7 pad_maximum_fusion
  305.2 8.7 %copy.295 = bf16[2048,1536]{1,0:T(8,128)(2,1)} copy(bf16[2048,1536]{0,1:T(8,128)(2,1)} %pad_maximum_fusion) | data formatting | bytes 12582912
  315.0 3.6 convolution_convert_fusion.6
  318.5 1.3 copy.293
  319.9 8.0 %convolution_convert_fusion.2 = bf16[768,2048]{1,0:T(8,128)(2,1)} fusion(bf16[1024,768]{1,0:T(8,128)(2,1)} %get-tuple-element.51, bf16[1024,2048]{1,0:T(8,128)(2,1)} %bitcast.257), kind=kOutput, calls=%fused_computation.16 | convolution fusion | flops 3222798336 | bytes 8912896 | tf_op jit(solution)/shard_map/dot_general | solution.py:42
  328.1 6.0 convolution_convert_fusion.5
  334.7 1.5 fusion.41
  337.4 7.9 %convolution_convert_fusion.1 = bf16[1024,2048]{1,0:T(8,128)(2,1)} fusion(bf16[1024,768]{1,0:T(8,128)(2,1)} %get-tuple-element.51, bf16[768,2048]{1,0:T(8,128)(2,1)} %bitcast.259), kind=kOutput, calls=%fused_computation.15 | convolution fusion | flops 3223322624 | bytes 8912896 | tf_op jit(solution)/shard_map/dot_general | solution.py:38
  345.3 67.8 %reduce-scatter.24.cloned.1.call-done = bf16[128,1536]{1,0:T(8,128)(2,1)} async-done(((bf16[2048,1536]{1,0:T(8,128)(2,1)}), bf16[128,1536]{1,0:T(8,128)(2,1)}) %reduce-scatter.24.cloned.1.call-update) | async-done | bytes 393232 | tf_op jit(solution)/shard_map/reduce_scatter | solution.py:626
  413.1 4.3 all-to-all-start.4
  417.4 71.8 %reduce-scatter.22.cloned.1.call-done = bf16[128,256]{1,0:T(8,128)(2,1)} async-done(((bf16[2048,256]{1,0:T(8,128)(2,1)}), bf16[128,256]{1,0:T(8,128)(2,1)}) %reduce-scatter.22.cloned.1.call-update) | async-done | bytes 65552
  490.7 4.3 all-to-all-start.2
  496.3 71.8 %reduce-scatter.20.cloned.1.call-done = bf16[48,2048]{1,0:T(8,128)(2,1)} async-done(((bf16[768,2048]{1,0:T(8,128)(2,1)}), bf16[48,2048]{1,0:T(8,128)(2,1)}) %reduce-scatter.20.cloned.1.call-update) | async-done | bytes 196624 | tf_op jit(solution)/shard_map/reduce_scatter | solution.py:625
  568.0 1.7 convert_element_type.102
  569.7 2.3 reshape.246
  572.1 4.8 all-to-all-start.3
  576.9 2.7 fusion.56
  579.6 1.6 copy.279
  581.2 2.6 squeeze.18
  583.8 2.8 copy.278
  586.7 2.6 squeeze.17
  589.3 56.1 %reduce-scatter.18.cloned.1.call-done = bf16[128,512]{1,0:T(8,128)(2,1)} async-done(((bf16[2048,512]{1,0:T(8,128)(2,1)}), bf16[128,512]{1,0:T(8,128)(2,1)}) %reduce-scatter.18.cloned.1.call-update) | async-done | bytes 131088 | tf_op jit(solution)/shard_map/reduce_scatter | solution.py:661
  645.4 4.3 all-to-all-start.1
  650.3 5.5 all-to-all-done.1
  657.8 71.5 %all-reduce.5.cloned.1.call-done = f32[128,128]{1,0:T(8,128)} async-done(((f32[128,128]{1,0:T(8,128)}), f32[128,128]{1,0:T(8,128)}) %all-reduce.5.cloned.1.call-update) | async-done | bytes 65552
  729.3 1.3 constant_dynamic-slice_fusion
  730.6 4.3 all-to-all-start
  734.8 34.1 %reduce-scatter.12.cloned.1.call-done = bf16[128,2048]{1,0:T(8,128)(2,1)} async-done(((bf16[1024,2048]{1,0:T(8,128)(2,1)}), bf16[128,2048]{1,0:T(8,128)(2,1)}) %reduce-scatter.12.cloned.1.call-update) | async-done | bytes 524304 | tf_op jit(solution)/shard_map/reduce_scatter | solution.py:621
  768.9 2.7 fusion.34
  (158 shorter events, 23.4 us)
Async XLA Ops:
  7.2 7.2 copy-start
  7.2 7.2 copy-start.20
  7.2 153.2 %all-gather.3.cloned.1.call-start = ((), (), s32[]{:S(2)}) async-start(), calls=%async_computation.12 | async-start | bytes 4718592 | tf_op jit(solution)/shard_map/all_gather | solution.py:606
  129.8 36.9 %slice-start.2 = ((s8[6291456]{0:T(1024)(128)(4,1)}), s8[2097152]{0:T(1024)(128)(4,1)S(1)}, s32[]{:S(2)}) async-start(s8[6291456]{0:T(1024)(128)(4,1)} %bitcast.251), calls=%async_computation.24 | async-start | bytes 4194304
  129.8 92.4 %reduce-scatter.14.cloned.1.call-start = ((), (), s32[]{:S(2)}) async-start(), calls=%async_computation.14 | async-start | bytes 4718592 | tf_op jit(solution)/shard_map/reduce_scatter | solution.py:617
  160.4 6.3 slice-start.3
  160.4 6.3 copy-start.22
  166.7 3.4 copy-start.21
  166.7 3.4 copy-start.24
  175.8 3.5 copy-start.28
  175.8 3.5 copy-start.32
  184.3 1.2 copy-start.2
  184.3 39.4 %copy-start.6 = (bf16[1,128,2048]{2,1,0:T(8,128)(2,1)S(1)}, bf16[1,128,2048]{2,1,0:T(8,128)(2,1)}, u32[]{:S(2)}) copy-start(bf16[1,128,2048]{2,1,0:T(8,128)(2,1)} %param.29) | copy-start | bytes 1572868
  184.3 72.9 %all-gather.5.cloned.1.call-start = ((), (), s32[]{:S(2)}) async-start(), calls=%async_computation.15 | async-start | bytes 4718592 | tf_op jit(solution)/shard_map/all_gather | solution.py:638
  185.7 46.5 %copy-start.3 = (f32[1024,384]{1,0:T(8,128)S(1)}, f32[1024,384]{1,0:T(8,128)}, u32[]{:S(2)}) copy-start(f32[1024,384]{1,0:T(8,128)} %get-tuple-element.34) | copy-start | bytes 4718596
  225.9 108.8 %reduce-scatter.16.cloned.1.call-start = ((), (), s32[]{:S(2)}) async-start(), calls=%async_computation.16 | async-start | bytes 4718592 | tf_op jit(solution)/shard_map/reduce_scatter | solution.py:655
  235.0 8.3 %copy-start.12 = (bf16[1024,2,128]{0,2,1:T(8,128)(2,1)S(1)}, bf16[1024,2,128]{0,2,1:T(8,128)(2,1)}, u32[]{:S(2)}) copy-start(bf16[1024,2,128]{0,2,1:T(8,128)(2,1)} %reshape.232) | copy-start | bytes 1572868
  235.0 8.3 %copy-start.14 = (bf16[1024,128]{1,0:T(8,128)(2,1)S(1)}, bf16[1024,128]{1,0:T(8,128)(2,1)}, u32[]{:S(2)}) copy-start(bf16[1024,128]{1,0:T(8,128)(2,1)} %get-tuple-element.35) | copy-start | bytes 786436
  257.2 9.9 %slice-start = ((s8[8388608]{0:T(1024)(128)(4,1)}), s8[4194304]{0:T(1024)(128)(4,1)S(1)}, s32[]{:S(2)}) async-start(s8[8388608]{0:T(1024)(128)(4,1)} %bitcast.212), calls=%async_computation.22 | async-start | bytes 8388608
  261.1 5.9 slice-start.1
  261.1 5.9 copy-start.19
  275.3 0.9 copy-start.17
  275.3 1.0 copy-start.18
  275.3 1.4 copy-start.8
  276.7 6.6 copy-start.4
  281.4 2.9 copy-start.13
  281.4 4.2 copy-start.9
  281.4 4.2 copy-start.10
  283.8 2.9 copy-start.25
  283.8 2.9 copy-start.30
  285.9 0.8 copy-start.15
  291.1 122.0 %reduce-scatter.24.cloned.1.call-start = ((), (), s32[]{:S(2)}) async-start(), calls=%async_computation.20 | async-start | bytes 6684672 | tf_op jit(solution)/shard_map/reduce_scatter | solution.py:626
  291.2 6.3 copy-start.23
  291.2 6.3 copy-start.29
  313.9 1.1 copy-start.26
  314.0 175.2 %reduce-scatter.22.cloned.1.call-start = ((), (), s32[]{:S(2)}) async-start(), calls=%async_computation.19 | async-start | bytes 1114112
  319.9 248.2 %reduce-scatter.20.cloned.1.call-start = ((), (), s32[]{:S(2)}) async-start(), calls=%async_computation.18 | async-start | bytes 3342336 | tf_op jit(solution)/shard_map/reduce_scatter | solution.py:625
  319.9 8.1 %copy-start.16 = (bf16[1024,256]{1,0:T(8,128)(2,1)S(1)}, bf16[1024,256]{1,0:T(8,128)(2,1)}, u32[]{:S(2)}) copy-start(bf16[1024,256]{1,0:T(8,128)(2,1)} %copy-done.15) | copy-start | bytes 1572868
  319.9 8.1 %copy-start.31 = (bf16[1024,128]{1,0:T(8,128)(2,1)S(1)}, bf16[1024,128]{1,0:T(8,128)(2,1)}, u32[]{:S(2)}) copy-start(bf16[1024,128]{1,0:T(8,128)(2,1)} %fusion.29) | copy-start | bytes 786436
  328.0 317.4 %reduce-scatter.18.cloned.1.call-start = ((), (), s32[]{:S(2)}) async-start(), calls=%async_computation.17 | async-start | bytes 2228224 | tf_op jit(solution)/shard_map/reduce_scatter | solution.py:661
  328.1 6.1 copy-start.5
  334.1 395.2 %all-reduce.5.cloned.1.call-start = ((), (), s32[]{:S(2)}) async-start(), calls=%async_computation.21 | async-start | bytes 131072
  337.1 431.8 %reduce-scatter.12.cloned.1.call-start = ((), (), s32[]{:S(2)}) async-start(), calls=%async_computation.13 | async-start | bytes 4718592 | tf_op jit(solution)/shard_map/reduce_scatter | solution.py:621
  345.2 149.8 %copy-start.27 = (u32[128]{0:T(128)S(1)}, u32[128]{0:T(128)}, u32[]{:S(2)}) copy-start(u32[128]{0:T(128)} %constant.62) | copy-start | bytes 1540
  413.1 77.7 %all-to-all-start.4 = ((bf16[8,16,1536]{2,1,0:T(8,128)(2,1)}), bf16[8,16,1536]{2,1,0:T(8,128)(2,1)S(1)}, u32[]{:S(2)}, u32[]{:S(2)}) async-start(bf16[8,16,1536]{2,1,0:T(8,128)(2,1)} %bitcast.227), calls=%async_computation.8 | async-start | bytes 786432 | tf_op jit(solution)/shard_map/all_to_all | solution.py:627
  490.7 81.3 %all-to-all-start.2 = ((bf16[32,8,128]{2,0,1:T(8,128)(2,1)}), bf16[32,8,128]{2,0,1:T(8,128)(2,1)}, u32[]{:S(2)}, u32[]{:S(2)}) async-start(bf16[32,8,128]{2,0,1:T(8,128)(2,1)} %copy.275), calls=%async_computation.6 | async-start | bytes 131072 | tf_op jit(solution)/shard_map/all_to_all | solution.py:668
  572.1 17.2 %all-to-all-start.3 = ((bf16[16,16,128]{2,1,0:T(8,128)(2,1)}), bf16[16,16,128]{2,1,0:T(8,128)(2,1)S(1)}, u32[]{:S(2)}, u32[]{:S(2)}) async-start(bf16[16,16,128]{2,1,0:T(8,128)(2,1)} %bitcast.52), calls=%async_computation.7 | async-start | bytes 131072 | tf_op jit(solution)/shard_map/all_to_all | solution.py:669
  579.6 189.3 %copy-start.7 = (bf16[128,2048]{1,0:T(8,128)(2,1)S(1)}, bf16[128,2048]{1,0:T(8,128)(2,1)}, u32[]{:S(2)}) copy-start(bf16[128,2048]{1,0:T(8,128)(2,1)} %reduce-scatter.14.cloned.1.call-done) | copy-start | bytes 1572868
  579.6 189.3 %copy-start.11 = (bf16[128,2048]{1,0:T(8,128)(2,1)S(1)}, bf16[128,2048]{1,0:T(8,128)(2,1)}, u32[]{:S(2)}) copy-start(bf16[128,2048]{1,0:T(8,128)(2,1)} %reduce-scatter.16.cloned.1.call-done) | copy-start | bytes 1572868
  583.8 189.0 %copy-start.1 = (bf16[16,1024]{1,0:T(8,128)(2,1)S(1)}, bf16[16,1024]{1,0:T(8,128)(2,1)}, u32[]{:S(2)}) copy-start(bf16[16,1024]{1,0:T(8,128)(2,1)} %param.20) | copy-start | bytes 98308
  645.4 10.4 %all-to-all-start.1 = ((bf16[8,16,512]{2,1,0:T(8,128)(2,1)}), bf16[8,16,512]{2,1,0:T(8,128)(2,1)S(1)}, u32[]{:S(2)}, u32[]{:S(2)}) async-start(bf16[8,16,512]{2,1,0:T(8,128)(2,1)} %bitcast.234), calls=%async_computation.5 | async-start | bytes 262144 | tf_op jit(solution)/shard_map/all_to_all | solution.py:662
  730.6 41.0 %all-to-all-start = ((f32[8,1,128]{2,1,0:T(1,128)}), f32[8,1,128]{2,1,0:T(1,128)S(1)}, u32[]{:S(2)}, u32[]{:S(2)}) async-start(f32[8,1,128]{2,1,0:T(1,128)} %bitcast.42), calls=%async_computation.3 | async-start | bytes 8192 | tf_op jit(solution)/shard_map/all_to_all | solution.py:682
Sparse Core Ops, SparseCore 0:
  129.9 30.4 all-gather.2
  184.4 37.7 reduce-scatter.13
  226.0 31.1 all-gather.4
  291.2 37.8 reduce-scatter.15
  332.4 80.6 reduce-scatter.23
  416.7 72.3 reduce-scatter.21
  492.8 75.1 reduce-scatter.19
  571.6 73.7 reduce-scatter.17
  649.2 80.0 all-reduce.4
  731.7 37.1 reduce-scatter.11

commit v3 on v2

--- a/solution.py
+++ b/solution.py
@@ -252,8 +252,12 @@
 
 
 class SeqScatter:
-    def __init__(self, part, sib_recv, x_recv, sems, co):
+    def __init__(self, part, sib_recv, x_recv, sems, co, kept=None):
         self.part, self.sib_recv, self.x_recv, self.sems, self.co = part, sib_recv, x_recv, sems, co
+        self.kept = kept
+
+    def ours(self, n):
+        return self.part.at[2 * n + 1] if self.kept is None else self.kept.at[n]
 
     def sib_copy(self, n):
         y, z, x, c = self.co
@@ -266,33 +270,34 @@
     def x_copy(self, n):
         y, z, x, c = self.co
         return pltpu.make_async_remote_copy(
-            src_ref=self.part.at[2 * n + 1], dst_ref=self.x_recv.at[n],
+            src_ref=self.ours(n), dst_ref=self.x_recv.at[n],
             send_sem=self.sems.at[2, n], recv_sem=self.sems.at[3, n],
             device_id=device(y, z, (x + off(n)) % AXIS, c), device_id_type=MESH,
         )
 
-    def combine(self, n):
+    def combine(self, n, go=True):
         self.sib_copy(n).wait_recv()
-        rows = self.part.shape[1]
+        ours = self.ours(n)
 
         def add(i, _):
             cut = pl.ds(i * 32, 32)
-            total = self.part[2 * n + 1, cut, :].astype(f32) + self.sib_recv[n, cut, :].astype(f32)
-            self.part[2 * n + 1, cut, :] = total.astype(bf16)
+            total = ours[cut, :].astype(f32) + self.sib_recv[n, cut, :].astype(f32)
+            ours[cut, :] = total.astype(bf16)
             return 0
 
-        lax.fori_loop(0, rows // 32, add, 0)
-
-        @pl.when(n < 3)
-        def _():
-            self.x_copy(n).start()
+        lax.fori_loop(0, SPAN // 32, add, 0)
+        if go:
+
+            @pl.when(n < 3)
+            def _():
+                self.x_copy(n).start()
 
     def arrive(self):
         for n in range(3):
             self.x_copy(n).wait_recv()
 
     def rows(self, cut):
-        total = self.part[7, cut, :].astype(f32)
+        total = self.ours(3)[cut, :].astype(f32)
         for n in range(3):
             total = total + self.x_recv[n, cut, :].astype(f32)
         return total
@@ -541,6 +546,560 @@
     )(tok, cot, pq, pm, wd, wo, cos, sin)
 
 
+def mlp_kernel(
+    h2_loc, dyg, gm, gd, x1, cot, gains,
+    dx1_o, dab_o, gain_o, ggu_o, gwd_o, pd_o,
+    h2g, dy_v, wgu, wd, hid, dgu, ggu, gwd, pdv,
+    part, sib_recv, x_recv, rs_sems, send, recv, local,
+):
+    co = y, z, x, c = coords()
+    peers = seq_peers(*co)
+    cm = Copies(send, recv, local)
+    loads = [
+        cm.here(gm, wgu),
+        cm.here(dyg, dy_v),
+        cm.here(gd, wd),
+    ]
+    barrier([p for _, _, p in peers])
+    g_h2 = SeqGather(cm, h2_loc, h2g, co)
+    g_h2.start()
+    rs = SeqScatter(part, sib_recv, x_recv, rs_sems, co)
+    wgu2 = wgu.reshape(WIDTH, 2 * FFS)
+    wd2 = wd.reshape(FFS, WIDTH)
+    order = {2: 0, 1: 1, 3: 2, 0: 3}
+    for copy in loads:
+        copy.wait()
+
+    def chip_of(k):
+        return (x + k) % AXIS
+
+    def forward(k):
+        chip = chip_of(k)
+        rows = pl.ds(pl.multiple_of(chip * 256, 256), 256)
+        two = pl.ds(2 * chip, 2)
+
+        def tile(f, _):
+            lo = pl.multiple_of(f * 256, 256)
+            h = h2g[two].reshape(256, WIDTH)
+            gate = dot(h, wgu2[:, pl.ds(lo, 256)])
+            up = dot(h, wgu2[:, pl.ds(pl.multiple_of(lo + FFS, 256), 256)])
+            dh = dot_nt(dy_v[two].reshape(256, WIDTH), wd2[pl.ds(lo, 256), :])
+            sig = jax.nn.sigmoid(gate)
+            silu = gate * sig
+            hid[rows, pl.ds(lo, 256)] = (silu * up).astype(bf16)
+            dgate = dh * up * (sig * (1.0 + gate * (1.0 - sig)))
+            dgu[rows, pl.ds(lo, 256)] = dgate.astype(bf16)
+            dgu[rows, pl.ds(pl.multiple_of(lo + FFS, 256), 256)] = (dh * silu).astype(bf16)
+            return 0
+
+        lax.fori_loop(0, FFS // 256, tile, 0)
+
+    def put(ref, n, cols, o):
+        ref[2 * n + 1 - c, :, cols] = o[:SPAN]
+        ref[2 * n + c, :, cols] = o[SPAN:]
+
+    def back(k):
+        n = order[k]
+        rows = pl.ds(pl.multiple_of(chip_of(k) * 256, 256), 256)
+
+        def tile(m, _):
+            cols = pl.ds(pl.multiple_of(m * 256, 256), 256)
+            put(part, n, cols, dot_nt(dgu[rows, :], wgu2[cols, :]).astype(bf16))
+            return 0
+
+        lax.fori_loop(0, WIDTH // 256, tile, 0)
+        rs.sib_copy(n).start()
+
+    g_h2.wait_chip(0)
+    forward(0)
+    g_h2.forward()
+    back(0)
+    g_h2.wait_chip(3)
+    forward(3)
+    g_h2.last()
+    back(3)
+    g_h2.wait_chip(1)
+    forward(1)
+    rs.combine(order[3])
+    back(1)
+    g_h2.wait_chip(2)
+    forward(2)
+    rs.combine(order[1])
+    back(2)
+    rs.combine(order[0])
+
+    def gate_up(m, _):
+        cols = pl.ds(pl.multiple_of(m * 256, 256), 256)
+        ggu[cols, :] = dot_tn(h2g[:, :, cols].reshape(LENGTH, 256), dgu[...]).astype(bf16)
+        return 0
+
+    lax.fori_loop(0, 1, gate_up, 0)
+    rs.combine(order[2])
+    lax.fori_loop(1, WIDTH // 256, gate_up, 0)
+    outs = [cm.here(ggu, ggu_o)]
+
+    for k in range(4):
+        n = order[k]
+        rows = pl.ds(pl.multiple_of(chip_of(k) * 256, 256), 256)
+
+        def down(m, _):
+            cols = pl.ds(pl.multiple_of(m * 512, 512), 512)
+            put(pdv, n, cols, dot(hid[rows, :], wd2[:, cols]).astype(bf16))
+            return 0
+
+        lax.fori_loop(0, WIDTH // 512, down, 0)
+    outs.append(cm.here(pdv, pd_o))
+
+    def down_grad(m, _):
+        cols = pl.ds(pl.multiple_of(m * 256, 256), 256)
+        gwd[cols, :] = dot_tn(hid[:, cols], dy_v[...].reshape(LENGTH, WIDTH)).astype(bf16)
+        return 0
+
+    lax.fori_loop(0, FFS // 256, down_grad, 0)
+    outs.append(cm.here(gwd, gwd_o))
+    rs.arrive()
+    gain_two = gains[1:2, :]
+
+    def residual(i, acc):
+        cut = pl.ds(i * 32, 32)
+        v = x1[cut, :]
+        inv = rms(v)
+        unit = v * inv
+        dh2 = rs.rows(cut)
+        dx1 = cot[cut, :].astype(f32) + rms_back(dh2, gain_two, unit, inv)
+        dx1_o[cut, :] = dx1
+        dab_o[cut, :] = dx1.astype(bf16)
+        return acc + jnp.sum(dh2 * unit, axis=0, keepdims=True)
+
+    acc = lax.fori_loop(0, SPAN // 32, residual, jnp.zeros((1, WIDTH), f32))
+    gain_o[...] = jnp.broadcast_to(acc, (8, WIDTH))
+    rs.finish()
+    for copy in outs:
+        copy.wait()
+    cm.finish()
+
+
+def mlp(h2_loc, dyg, gm, gd, x1, cot, gains):
+    any_, vm = pl.BlockSpec(memory_space=pl.ANY), pl.BlockSpec(memory_space=pltpu.VMEM)
+    sds = jax.ShapeDtypeStruct
+    n_copies, n_local = 9, 8
+    return pl.pallas_call(
+        mlp_kernel,
+        name="feed_forward",
+        out_shape=[
+            sds((SPAN, WIDTH), f32), sds((SPAN, WIDTH), bf16), sds((8, WIDTH), f32),
+            sds((WIDTH, 2 * FFS), bf16), sds((FFS, WIDTH), bf16), sds((8, SPAN, WIDTH), bf16),
+        ],
+        in_specs=[any_] * 4 + [vm] * 3,
+        out_specs=[vm, vm, vm, any_, any_, any_],
+        scratch_shapes=[
+            pltpu.VMEM((8, SPAN, WIDTH), bf16),
+            pltpu.VMEM((8, SPAN, WIDTH), bf16),
+            pltpu.VMEM((4, 4, 128, 2 * FFS), bf16),
+            pltpu.VMEM((4, 4, FR, WIDTH), bf16),
+            pltpu.VMEM((LENGTH, FFS), bf16),
+            pltpu.VMEM((LENGTH, 2 * FFS), bf16),
+            pltpu.VMEM((WIDTH, 2 * FFS), bf16),
+            pltpu.VMEM((FFS, WIDTH), bf16),
+            pltpu.VMEM((8, SPAN, WIDTH), bf16),
+            *scatter_scratch(),
+            pltpu.SemaphoreType.DMA((n_copies,)),
+            pltpu.SemaphoreType.DMA((n_copies,)),
+            pltpu.SemaphoreType.DMA((n_local,)),
+        ],
+        compiler_params=pltpu.CompilerParams(
+            collective_id=2, has_side_effects=True, vmem_limit_bytes=VMEM_LIMIT
+        ),
+    )(h2_loc, dyg, gm, gd, x1, cot, gains)
+
+
+class DpScatter:
+    def __init__(self, cm, grad, acc, one, two, co, axis, tile):
+        self.cm, self.grad, self.acc, self.r1, self.r2 = cm, grad, acc, one, two
+        self.co, self.axis, self.tile = co, axis, tile
+        self.h = grad.shape[2 + axis] // 2
+
+    def part(self, ref, half):
+        cut = pl.ds(half * self.h, self.h)
+        lead = (slice(None),) * (len(ref.shape) - 2)
+        return ref.at[lead + ((cut, slice(None)) if self.axis == 0 else (slice(None), cut))]
+
+    def line(self, half, k):
+        y, z, _, _ = self.co
+        if half == 0:
+            return self.part(self.grad.at[(y + k) % AXIS], half)
+        return self.part(self.grad.at[:, (z + k) % AXIS], half)
+
+    def away(self, along, k):
+        y, z, x, c = self.co
+        if along == 0:
+            return device((y + k) % AXIS, z, x, c)
+        return device(y, (z + k) % AXIS, x, c)
+
+    def start(self):
+        self.own = [self.cm.here(self.line(h, 0), self.acc.at[h]) for h in (0, 1)]
+        self.first = [[], []]
+        for k in (2, 1, 3):
+            for h in (0, 1):
+                self.first[h].append(
+                    self.cm.to(self.line(h, k), self.r1.at[h, k - 1], self.away(h, k))
+                )
+
+    def mid(self):
+        y, z, _, _ = self.co
+        rows = self.acc.shape[2]
+        self.second = [[], []]
+        for h in (0, 1):
+            self.own[h].wait()
+            for copy in self.first[h]:
+                copy.wait_recv()
+
+            def add(t, _, h=h):
+                q = t // (rows // self.tile)
+                cut = pl.ds((t % (rows // self.tile)) * self.tile, self.tile)
+                total = self.acc[h, q, cut, :].astype(f32)
+                for k in range(3):
+                    total = total + self.r1[h, k, q, cut, :].astype(f32)
+                self.acc[h, q, cut, :] = total.astype(bf16)
+                return 0
+
+            lax.fori_loop(0, AXIS * (rows // self.tile), add, 0)
+            mine = z if h == 0 else y
+            for k in (2, 1, 3):
+                self.second[h].append(
+                    self.cm.to(self.acc.at[h, (mine + k) % AXIS], self.r2.at[h, k - 1], self.away(1 - h, k))
+                )
+
+    def last(self, out):
+        y, z, _, _ = self.co
+        rows, cols = self.acc.shape[2:]
+        for h in (0, 1):
+            for copy in self.second[h]:
+                copy.wait_recv()
+            mine = z if h == 0 else y
+
+            def add(t, _, h=h, mine=mine):
+                cut = pl.ds(t * self.tile, self.tile)
+                total = self.acc[h, mine, cut, :].astype(f32)
+                for k in range(3):
+                    total = total + self.r2[h, k, cut, :].astype(f32)
+                if self.axis == 0:
+                    out[pl.ds(h * self.h + t * self.tile, self.tile), :] = total.astype(out.dtype)
+                else:
+                    out[cut, pl.ds(h * self.h, self.h)] = total.astype(out.dtype)
+                return 0
+
+            lax.fori_loop(0, rows // self.tile, add, 0)
+
+
+def dp_scatter_scratch(rows, cols):
+    return [
+        pltpu.VMEM((2, AXIS, rows, cols), bf16),
+        pltpu.VMEM((2, 3, AXIS, rows, cols), bf16),
+        pltpu.VMEM((2, 3, rows, cols), bf16),
+    ]
+
+
+def attn_backward_kernel(
+    dab_loc, pd, ggu, gwd, h1, gq, wo,
+    dx1, tok, x1, gain2, pre, qb, kb, vb, ob, lse, gains, cos, sin,
+    gt_o, block_o, gu_o, gwd_o, gqkv_o, gwo_o, gg_o,
+    dab, h1_v, wq, wo_v, pbuf, dob, dk, dv, dqkv, gacc,
+    part, sib_recv, x_recv, rs_sems, kept, sib2, x2, rs2_sems,
+    m_acc, m_one, m_two, d_acc, d_one, d_two, o_acc, o_one, o_two, q_acc, q_one, q_two,
+    mo, go, oo, o2g, o1g, ow, gqk, qo, gg, g_one, g_two, g_all, g_sum,
+    send, recv, local,
+):
+    co = y, z, x, c = coords()
+    s = x * 2 + c
+    peers = seq_peers(*co)
+    yp = [device((y + k) % AXIS, z, x, c) for k in (1, 2, 3)]
+    zp = [device(y, (z + k) % AXIS, x, c) for k in (1, 2, 3)]
+    cm = Copies(send, recv, local)
+    l_wo = cm.here(wo, wo_v)
+    l_pd = [cm.here(pd.at[2 * n + 1], kept.at[n]) for n in range(4)]
+    l_wq = cm.here(gq.at[:, :, :, pl.ds(0, QKV)], wq)
+
+    def h1_load(m):
+        return cm.here(h1.at[:, :, pl.ds(m * 256, 256)], h1_v.at[m % 2])
+
+    l_h1 = [h1_load(0), h1_load(1)]
+    barrier([p for _, _, p in peers] + yp + zp)
+    g_dab = SeqGather(cm, dab_loc, dab, co)
+    g_dab.start()
+    r_m = DpScatter(cm, ggu, m_acc, m_one, m_two, co, 0, 16)
+    r_d = DpScatter(cm, gwd, d_acc, d_one, d_two, co, 1, 16)
+    r_m.start()
+    r_d.start()
+    rs2 = SeqScatter(pd, sib2, x2, rs2_sems, co, kept)
+    for n in range(4):
+        l_pd[n].wait()
+        rs2.sib_copy(n).start()
+
+    def probs(i, _):
+        sc = dot_nt(qb[i], kb[...]) * score_scale
+        r = lax.broadcasted_iota(jnp.int32, (2 * SPAN, LENGTH), 0) % SPAN + i * SPAN
+        k = lax.broadcasted_iota(jnp.int32, (2 * SPAN, LENGTH), 1)
+        p = jnp.where(k <= r, jnp.exp(sc - lse[i][:, 0:1]), 0.0)
+        pbuf[i] = p.astype(bf16)
+        return 0
+
+    lax.fori_loop(0, 4, probs, 0)
+    g_dab.forward()
+    lax.fori_loop(4, 8, probs, 0)
+    dk[...] = jnp.zeros_like(dk)
+    dv[...] = jnp.zeros_like(dv)
+    gacc[...] = jnp.zeros_like(gacc)
+    l_wo.wait()
+
+    def out_back(k):
+        g_dab.wait_chip(k)
+        two = pl.ds(2 * ((x + k) % AXIS), 2)
+        o = dot_nt(dab[two].reshape(2 * SPAN, WIDTH), wo_v[...]).astype(bf16)
+        for j in range(2):
+            blk = o[j * SPAN : (j + 1) * SPAN]
+            dob[2 * ((x + k) % AXIS) + j] = jnp.concatenate([blk[:, :128], blk[:, 128:]], axis=0)
+
+    out_back(0)
+    out_back(3)
+    out_back(1)
+    for n in range(4):
+        rs2.combine(n, False)
+    g_dab.last()
+    out_back(2)
+
+    def out_grad(m, _):
+        cols = pl.ds(pl.multiple_of(m * 512, 512), 512)
+        o = dot_tn(ob[...], dab[:, :, cols].reshape(LENGTH, 512)).astype(bf16)
+        for j in range(AXIS):
+            go[m, j] = o[:, j * 128 : j * 128 + 128]
+        return 0
+
+    lax.fori_loop(0, AXIS, out_grad, 0)
+    r_o = DpScatter(cm, go, o_acc, o_one, o_two, co, 0, 128)
+    r_o.start()
+
+    rs = SeqScatter(part, sib_recv, x_recv, rs_sems, co)
+    l_wq.wait()
+    wq2 = wq.reshape(WIDTH, QKV)
+    gain_q, gain_k = gains[2:3, 0:128], gains[3:4, 0:128]
+
+    def head_back(g, u, gain, co_t, si_t):
+        g = g * co_t - swap(g) * si_t
+        inv = rms(u)
+        unit = u * inv
+        return rms_back(g, gain, unit, inv), jnp.sum(g * unit, axis=0, keepdims=True)
+
+    def slot_of(chip):
+        k = (chip - x + AXIS) % AXIS
+        return jnp.where(k == 2, 0, jnp.where(k == 1, 1, jnp.where(k == 3, 2, 3)))
+
+    def chip_back(t, _):
+        chip = 3 - t
+
+        def block(j, _):
+            i = chip * 2 + 1 - j
+            q, do, p = qb[i], dob[i], pbuf[i]
+            dp = dot_nt(do, vb[...])
+            pf = p.astype(f32)
+            delta = jnp.sum(pf * dp, axis=-1, keepdims=True)
+            ds = (pf * (dp - delta)).astype(bf16)
+            dk[...] += dot_tn(ds, q)
+            dv[...] += dot_tn(p, do)
+            dq = dot(ds, kb[...]) * score_scale
+            cut = pl.ds(pl.multiple_of(i * SPAN, SPAN), SPAN)
+            u = jnp.concatenate([pre[cut, 0:128], pre[cut, 128:256]], axis=0)
+            co_t = jnp.concatenate([cos[cut, :]] * 2, axis=0)
+            si_t = jnp.concatenate([sin[cut, :]] * 2, axis=0)
+            dqp, gsum = head_back(dq, u, gain_q, co_t, si_t)
+            gacc[0:1, :] += gsum
+            dqp = dqp.astype(bf16)
+            dqkv[cut, 0:128] = dqp[:SPAN]
+            dqkv[cut, 128:256] = dqp[SPAN:]
+            return 0
+
+        lax.fori_loop(0, 2, block, 0)
+        cut = pl.ds(pl.multiple_of(chip * 256, 256), 256)
+        dkp, gsum = head_back(dk[cut, :] * score_scale, pre[cut, 256:384], gain_k, cos[cut, :], sin[cut, :])
+        gacc[1:2, :] += gsum
+        dqkv[cut, 256:384] = dkp.astype(bf16)
+        dqkv[cut, 384:512] = dv[cut, :].astype(bf16)
+        n = slot_of(chip)
+
+        def tile(m, _):
+            cols = pl.ds(pl.multiple_of(m * 512, 512), 512)
+            o = dot_nt(dqkv[cut, :], wq2[cols, :]).astype(bf16)
+            part[2 * n + 1 - c, :, cols] = o[:SPAN]
+            part[2 * n + c, :, cols] = o[SPAN:]
+            return 0
+
+        lax.fori_loop(0, WIDTH // 512, tile, 0)
+        rs.sib_copy(n).start()
+        rs.combine(n)
+        return 0
+
+    lax.fori_loop(0, 4, chip_back, 0)
+
+    for m in range(8):
+        l_h1[m].wait()
+        o = dot_tn(h1_v[m % 2].reshape(LENGTH, 256), dqkv[...]).astype(bf16)
+        gqk[m // 2, 2 * (m % 2)] = o[:SPAN]
+        gqk[m // 2, 2 * (m % 2) + 1] = o[SPAN:]
+        if m < 6:
+            l_h1.append(h1_load(m + 2))
+    r_q = DpScatter(cm, gqk, q_acc, q_one, q_two, co, 0, 64)
+    r_q.start()
+    for n in range(3):
+        rs2.x_copy(n).start()
+    r_m.mid()
+    r_d.mid()
+    r_o.mid()
+
+    rs.arrive()
+    gain_one = gains[0:1, :]
+
+    def input_back(i, acc):
+        cut = pl.ds(i * 32, 32)
+        v = tok[cut, :].astype(f32)
+        inv = rms(v)
+        unit = v * inv
+        dh1 = rs.rows(cut)
+        gt_o[cut, :] = dx1[cut, :] + rms_back(dh1, gain_one, unit, inv)
+        return acc + jnp.sum(dh1 * unit, axis=0, keepdims=True)
+
+    gain1 = lax.fori_loop(0, SPAN // 32, input_back, jnp.zeros((1, WIDTH), f32))
+
+    dev_i = lax.broadcasted_iota(jnp.int32, (ND * NS, WIDTH), 0)
+    col_j = lax.broadcasted_iota(jnp.int32, (ND * NS, WIDTH), 1)
+    mine = col_j // WR == dev_i
+    row_j = lax.broadcasted_iota(jnp.int32, (WIDTH, 128), 0)
+    lane = lax.broadcasted_iota(jnp.int32, (WIDTH, 128), 1)
+    rows = jnp.zeros((ND * NS, 128), f32)
+    for v, shift in ((gain1, 0), (gain2[0:1, :], WR)):
+        rows = rows + dot(
+            jnp.where(mine, v, 0.0).astype(bf16), (lane == row_j % WR + shift).astype(bf16)
+        )
+    eye_i = lax.broadcasted_iota(jnp.int32, (128, 128), 0)
+    eye_j = lax.broadcasted_iota(jnp.int32, (128, 128), 1)
+    for n in range(2):
+        rows = rows + dot(
+            jnp.where(eye_i == eye_j, gacc[n : n + 1, :], 0.0).astype(bf16),
+            (eye_j == 2 * WR + n).astype(bf16),
+        )
+    gg[...] = rows.reshape(AXIS, AXIS, NS, 128)
+    g_first = [cm.to(gg.at[(y + k) % AXIS], g_one.at[k - 1], yp[k - 1]) for k in (1, 2, 3)]
+    r_q.mid()
+    for copy in g_first:
+        copy.wait_recv()
+    gg[y] = gg[y] + g_one[0] + g_one[1] + g_one[2]
+    g_second = [cm.to(gg.at[y, (z + k) % AXIS], g_two.at[k - 1], zp[k - 1]) for k in (1, 2, 3)]
+
+    r_m.last(mo.reshape(NS * WR, 2 * FFS))
+    a2a = []
+    for k, j, p in peers:
+        t = ((x + k) % AXIS) * 2 + (c + j) % 2
+        a2a.append(cm.to(mo.at[t], gu_o.at[s], p))
+    l_mo = cm.here(mo.at[s], gu_o.at[s])
+    r_o.last(oo.reshape(2 * SPAN, SPAN))
+    o_three = []
+    for k, j, p in peers:
+        t = ((x + k) % AXIS) * 2 + (c + j) % 2
+        for h in range(2):
+            o_three.append(cm.to(oo.at[h, t], o2g.at[(s % 2) * 2 + h, s // 2], p))
+    l_three = [cm.here(oo.at[h, s], o2g.at[(s % 2) * 2 + h, s // 2]) for h in range(2)]
+    r_d.last(gwd_o)
+    rs2.arrive()
+
+    def out_rows(i, _):
+        cut = pl.ds(i * 32, 32)
+        block_o[cut, :] = (x1[cut, :] + rs2.rows(cut)).astype(bf16)
+        return 0
+
+    lax.fori_loop(0, SPAN // 32, out_rows, 0)
+    for copy in l_three:
+        copy.wait()
+    for copy in o_three:
+        copy.wait_recv()
+    o_two_c = [
+        cm.to(o2g.at[(z + k) % AXIS], o1g.at[:, :, pl.ds(pl.multiple_of(z * 128, 128), 128)], zp[k - 1])
+        for k in (1, 2, 3)
+    ]
+    l_two = cm.here(o2g.at[z], o1g.at[:, :, pl.ds(pl.multiple_of(z * 128, 128), 128)])
+    for copy in g_second:
+        copy.wait_recv()
+    g_all[s] = gg[y, z] + g_two[0] + g_two[1] + g_two[2]
+    g_third = [cm.to(g_all.at[s], g_all.at[s], p) for _, _, p in peers]
+    r_q.last(qo.reshape(NS * WR, QKV))
+    for k, j, p in peers:
+        t = ((x + k) % AXIS) * 2 + (c + j) % 2
+        a2a.append(cm.to(qo.at[t], gqkv_o.at[s], p))
+    l_qo = cm.here(qo.at[s], gqkv_o.at[s])
+    l_two.wait()
+    for copy in o_two_c:
+        copy.wait_recv()
+    o_one_c = [
+        cm.to(o1g.at[(y + k) % AXIS], ow.at[:, pl.ds(pl.multiple_of(y * 512, 512), 512)], yp[k - 1])
+        for k in (1, 2, 3)
+    ]
+    l_one = cm.here(o1g.at[y], ow.at[:, pl.ds(pl.multiple_of(y * 512, 512), 512)])
+    for copy in g_third:
+        copy.wait_recv()
+    total = g_all[0]
+    for t in range(1, NS):
+        total = total + g_all[t]
+    g_sum[...] = total
+    gg_o[...] = jnp.broadcast_to(g_sum[pl.ds(s, 1), :], (8, 128))
+    l_one.wait()
+    for copy in o_one_c:
+        copy.wait_recv()
+    gwo_o[...] = ow[...].astype(f32)
+    l_mo.wait()
+    l_qo.wait()
+    for copy in a2a:
+        copy.wait_recv()
+    rs.finish()
+    rs2.finish()
+    cm.finish()
+
+
+def attn_backward(dab_loc, pd, ggu, gwd, h1, gq, wo, *rest):
+    any_, vm = pl.BlockSpec(memory_space=pl.ANY), pl.BlockSpec(memory_space=pltpu.VMEM)
+    sds = jax.ShapeDtypeStruct
+    vmem = pltpu.VMEM
+    n_copies, n_local = 128, 32
+    return pl.pallas_call(
+        attn_backward_kernel,
+        name="attn_backward",
+        out_shape=[
+            sds((SPAN, WIDTH), f32), sds((SPAN, WIDTH), bf16), sds((NS, WR, 2 * FFS), bf16),
+            sds((FR, WIDTH), f32), sds((NS, WR, QKV), bf16), sds((WR, WIDTH), f32), sds((8, 128), f32),
+        ],
+        in_specs=[any_] * 7 + [vm] * len(rest),
+        out_specs=[vm, vm, any_, vm, any_, vm, vm],
+        scratch_shapes=[
+            vmem((8, SPAN, WIDTH), bf16), vmem((2, 8, SPAN, 256), bf16),
+            vmem((4, 4, 128, QKV), bf16), vmem((256, WIDTH), bf16),
+            vmem((8, 2 * SPAN, LENGTH), bf16), vmem((8, 2 * SPAN, 128), bf16),
+            vmem((LENGTH, 128), f32), vmem((LENGTH, 128), f32), vmem((LENGTH, QKV), bf16),
+            vmem((8, 128), f32),
+            *scatter_scratch(), vmem((4, SPAN, WIDTH), bf16), *scatter_scratch()[1:],
+            *dp_scatter_scratch(64, 2 * FFS), *dp_scatter_scratch(FR, WIDTH // 2),
+            *dp_scatter_scratch(SPAN, 128), *dp_scatter_scratch(64, QKV),
+            vmem((NS, WR, 2 * FFS), bf16), vmem((4, 4, 256, 128), bf16), vmem((2, NS, WR, 128), bf16),
+            vmem((4, 4, WR, 128), bf16), vmem((4, WR, 512), bf16), vmem((WR, WIDTH), bf16),
+            vmem((4, 4, SPAN, QKV), bf16), vmem((NS, WR, QKV), bf16),
+            vmem((4, 4, NS, 128), f32), vmem((3, 4, NS, 128), f32), vmem((3, NS, 128), f32),
+            vmem((NS, NS, 128), f32), vmem((NS, 128), f32),
+            pltpu.SemaphoreType.DMA((n_copies,)),
+            pltpu.SemaphoreType.DMA((n_copies,)),
+            pltpu.SemaphoreType.DMA((n_local,)),
+        ],
+        compiler_params=pltpu.CompilerParams(
+            collective_id=3, has_side_effects=True, vmem_limit_bytes=VMEM_LIMIT
+        ),
+    )(dab_loc, pd, ggu, gwd, h1, gq, wo, *rest)
+
+
 def shards(
     tokens, gain_attn, w_query, key_weight, value_weight, w_out, gain_query,
     key_norm_gain, gain_mlp, w_gate, w_up, w_down, cotangent,
@@ -576,113 +1135,21 @@
     (x1, h2_loc, h1, pre, qb, kb, vb, ob, lse, gains, gq, gm, gd, wo, dyb) = attn_forward(
         tokens[0], cotangent[0], pq, pm, w_down, w_out, cos, sin
     )
-    gain_one, gain_two = gains[0:1], gains[1:2]
-    gain_q, gain_k = gains[2:3, :128], gains[3:4, :128]
-    qkv_mat = gq.reshape(WIDTH, QKV + GCOL)[:, :QKV]
-    mlp_mat = gm.reshape(WIDTH, 2 * FFS)
-    gate_mat, up_mat = mlp_mat[:, :FFS], mlp_mat[:, FFS:]
-    down_mat = gd.reshape(FFS, WIDTH)
-    h1 = h1.reshape(LENGTH, WIDTH)
-    dyb = dyb.reshape(LENGTH, WIDTH)
-    x_loc = tokens[0].astype(f32)
-    heads = 2
-    length, ns, nd, wr, ff, fr, out_mat = LENGTH, NS, ND, WR, FFS, FR, wo
-    d2, cw = 2, 128
-    q_pre = pre[:, :qw].reshape(length, heads, HEAD_DIM)
-    k_pre = pre[:, qw:].reshape(length, 1, HEAD_DIM)
-    inv_q, inv_k = rms(q_pre), rms(k_pre)
-    unit_q, unit_k = q_pre * inv_q, k_pre * inv_k
-    qb = qb.reshape(8, 2, SPAN, HEAD_DIM).transpose(0, 2, 1, 3).reshape(length, heads, HEAD_DIM)
-    lse = lse[:, :, 0].reshape(8, 2, SPAN).transpose(1, 0, 2).reshape(2, length, 1)
-    cos_h, sin_h = jnp.asarray(cos[:, :64]), jnp.asarray(sin[:, 64:])
-
-    def unrotate(grads):
-        a, b = grads[..., :64], grads[..., 64:]
-        co, si = cos_h[:, None, :], sin_h[:, None, :]
-        return jnp.concatenate([a * co + b * si, b * co - a * si], axis=-1)
-
-    inv_two = rms(x1)
-    unit_two = x1 * inv_two
-    h2 = lax.all_gather(h2_loc, "seq", axis=0, tiled=True)
-    dy = cotangent[0].astype(f32)
-    gate = dot(h2, gate_mat)
-    up = dot(h2, up_mat)
-    sig = jax.nn.sigmoid(gate)
-    silu = gate * sig
-    hid = (silu * up).astype(bf16)
-    dhid = dot_nt(dyb, down_mat)
-    dgate = (dhid * up * (sig * (1.0 + gate * (1.0 - sig)))).astype(bf16)
-    dup = (dhid * silu).astype(bf16)
-    dh2 = (dot_nt(dgate, gate_mat) + dot_nt(dup, up_mat)).astype(bf16)
-    dh2 = lax.psum_scatter(dh2, "seq", scatter_dimension=0, tiled=True).astype(f32)
-    dx1 = dy + rms_back(dh2, gain_two, unit_two, inv_two)
-    g_gain_two = jnp.sum(dh2 * unit_two, axis=0)
-    part = dot(hid, down_mat).astype(bf16)
-    block = x1 + lax.psum_scatter(part, "seq", scatter_dimension=0, tiled=True).astype(f32)
-    block_out = block.astype(bf16)[None]
-    g_down = dot_tn(hid, dyb).astype(bf16)
-    g_mlp = jnp.concatenate([dot_tn(h2, dgate), dot_tn(h2, dup)], axis=1).astype(bf16)
-    g_down = lax.psum_scatter(g_down, "dp", scatter_dimension=0, tiled=True).astype(f32)
-    g_mlp = lax.psum_scatter(g_mlp, "dp", scatter_dimension=0, tiled=True)
-    g_mlp = lax.all_to_all(g_mlp.reshape(ns, wr, 2 * ff), "seq", 0, 0, tiled=True)
-    g_mlp = g_mlp.astype(f32).reshape(ns, wr, 2, nd, fr).transpose(2, 1, 3, 0, 4)
-    g_mlp = g_mlp.reshape(2, wr, nd * ns * fr)
-
-    allowed = (
-        jnp.arange(length, dtype=jnp.int32)[None, :]
-        <= jnp.arange(length, dtype=jnp.int32)[:, None]
+    dx1, dab_loc, gain2, ggu, gwd, pd = mlp(h2_loc, dyb, gm, gd, x1, cotangent[0], gains)
+    gt, block, g_gu, g_down, g_qkv, g_out, gg = attn_backward(
+        dab_loc, pd, ggu.reshape(4, 4, 128, 2 * FFS), gwd.reshape(4, 4, FR, WIDTH), h1, gq, wo,
+        dx1, tokens[0], x1, gain2, pre, qb, kb, vb, ob, lse, gains, cos, sin,
     )
-    score = jnp.einsum("qhd,kd->hqk", qb, kb, preferred_element_type=f32) * score_scale
-    prob = jnp.where(allowed, jnp.exp(score - lse), 0.0)
-    pb = prob.astype(bf16)
-    dab = lax.all_gather(dx1.astype(bf16), "seq", axis=0, tiled=True)
-    g_out = dot_tn(ob, dab).astype(bf16)
-    dob = dot_nt(dab, out_mat).astype(bf16).reshape(length, heads, HEAD_DIM)
-    dprob = jnp.einsum("qhd,kd->hqk", dob, vb, preferred_element_type=f32)
-    delta = jnp.sum(prob * dprob, axis=-1, keepdims=True)
-    dscore = (prob * (dprob - delta)).astype(bf16)
-    dq = jnp.einsum("hqk,kd->qhd", dscore, kb, preferred_element_type=f32) * score_scale
-    dk = jnp.einsum("hqk,qhd->kd", dscore, qb, preferred_element_type=f32) * score_scale
-    dv = jnp.einsum("hqk,qhd->kd", pb, dob, preferred_element_type=f32)
-    dq = unrotate(dq)
-    dk = unrotate(dk[:, None])
-    g_gain_q = jnp.sum(dq * unit_q, axis=(0, 1))
-    g_gain_k = jnp.sum(dk * unit_k, axis=(0, 1))
-    dqp = rms_back(dq, gain_q, unit_q, inv_q).reshape(length, qw)
-    dkp = rms_back(dk, gain_k, unit_k, inv_k).reshape(length, kw)
-    dqkv = jnp.concatenate([dqp, dkp, dv], axis=1).astype(bf16)
-    dh1 = dot_nt(dqkv, qkv_mat).astype(bf16)
-    dh1 = lax.psum_scatter(dh1, "seq", scatter_dimension=0, tiled=True).astype(f32)
-    inv_one = rms(x_loc)
-    unit_loc = x_loc * inv_one
-    grad_tokens = (dx1 + rms_back(dh1, gain_one, unit_loc, inv_one))[None]
-    g_gain_one = jnp.sum(dh1 * unit_loc, axis=0)
-    g_qkv = dot_tn(h1, dqkv).astype(bf16)
-    g_qkv = lax.psum_scatter(g_qkv, "dp", scatter_dimension=0, tiled=True)
-    g_qkv = lax.all_to_all(g_qkv.reshape(ns, wr, -1), "seq", 0, 0, tiled=True).astype(f32)
-    g_q = g_qkv[:, :, :qw].transpose(1, 0, 2).reshape(wr, -1)
-    g_k = g_qkv[:, :, qw : qw + kw].transpose(1, 0, 2).reshape(wr, -1)
-    g_v = g_qkv[:, :, qw + kw :].transpose(1, 0, 2).reshape(wr, -1)
-    g_out = lax.psum_scatter(g_out, "dp", scatter_dimension=1, tiled=True)
-    g_out = g_out.reshape(d2, ns, wr, cw).transpose(0, 2, 1, 3).reshape(d2 * wr, ns * cw)
-    g_out = lax.all_to_all(g_out, "seq", 1, 0, tiled=True)
-    g_out = lax.all_to_all(g_out, "dp", 0, 1, tiled=True).astype(f32)
-
-    gg = jnp.concatenate(
-        [
-            g_gain_one.reshape(nd * ns, wr),
-            g_gain_two.reshape(nd * ns, wr),
-            g_gain_q[:, None],
-            g_gain_k[:, None],
-        ],
-        axis=1,
-    )
-    gg = jnp.pad(gg, ((0, 0), (0, 128 - gg.shape[1])))
-    gg = lax.psum_scatter(gg, "dp", scatter_dimension=0, tiled=True)
-    gg = jnp.sum(lax.all_to_all(gg[:, None], "seq", 0, 1, tiled=True)[0], axis=0)
+    g_mlp = g_gu.astype(f32).reshape(NS, WR, 2, ND, FR).transpose(2, 1, 3, 0, 4)
+    g_mlp = g_mlp.reshape(2, WR, ND * NS * FR)
+    g_qkv = g_qkv.astype(f32)
+    g_q = g_qkv[:, :, :qw].transpose(1, 0, 2).reshape(WR, -1)
+    g_k = g_qkv[:, :, qw : qw + kw].transpose(1, 0, 2).reshape(WR, -1)
+    g_v = g_qkv[:, :, qw + kw :].transpose(1, 0, 2).reshape(WR, -1)
+    gg = gg[0]
     return (
-        block_out, grad_tokens, gg[:wr], g_q, g_k, g_v, g_out,
-        gg[2 * wr : 2 * wr + 1], gg[2 * wr + 1 : 2 * wr + 2], gg[wr : 2 * wr],
+        block[None], gt[None], gg[:WR], g_q, g_k, g_v, g_out,
+        gg[2 * WR : 2 * WR + 1], gg[2 * WR + 1 : 2 * WR + 2], gg[WR : 2 * WR],
         g_mlp[0], g_mlp[1], g_down,
     )
 

time: 788 us -> 323 us (0.41)
  waiting for transfers between devices: 454 us -> 0 us
  Pallas kernels: 114 us -> 297 us
  matrix products: 84.3 us -> 0 us
  local copies, waits for them, and re-layouts: 59.4 us -> 20.2 us
  other arithmetic: 28.2 us -> 3.13 us
  starting transfers between devices: 23.2 us -> 0 us
  between operations: 17.2 us -> 2.16 us
    reduce_scatter x6 -> x0, waiting for transfers between devices: 265 us -> none  [the longest x1 71.8 us: shards(): lax.psum_scatter(g_down, 'dp', scatter_dimension=0, tiled=True).astype(f32)]
    pallas_call x0 -> x2, Pallas kernels: none -> 183 us  [the longest x1 117 us: attn_backward(): pl.pallas_call(attn_backward_kernel, name='attn_backward', out_shape=[sds...]
    unnamed x12 -> x0, waiting for transfers between devices: 143 us -> none
    dot_general x18 -> x0, matrix products: 84.3 us -> none  [the longest x5 27.9 us: dot_tn(): lax.dot_general(a, b, (((0,), (0,)), ((), ())), preferred_element_type=f32)]
    all_gather x2 -> x0, waiting for transfers between devices: 39.7 us -> none  [the longest x1 30.3 us: shards(): h2 = lax.all_gather(h2_loc, 'seq', axis=0, tiled=True)]
    all_to_all x5 -> x0, starting transfers between devices: 21.9 us -> none  [the longest x1 4.82 us: shards(): g_out = lax.all_to_all(g_out, 'dp', 0, 1, tiled=True).astype(f32)]
    unnamed x83 -> x17, local copies, waits for them, and re-layouts: 16.5 us -> 4.4 us
  transfers between devices with their start and end apart: 15 -> 0, of which waited for: 10 -> 0; matrix products, arithmetic and copies ran while one was open for 13% -> 0% of each run, Pallas kernels for 0% -> 0%
where the time goes in v3:
time: 323 us; the launch traced here: 322 us
  Pallas kernels  297 us (92%)
  local copies, waits for them, and re-layouts  20.2 us (6%)
    pallas_call x1, Pallas kernels, attn_backward(): pl.pallas_call(attn_backward_kernel, name='attn_backward', out_shape=[sds...  117 us
    pallas_call x1, Pallas kernels, attn_forward(): pl.pallas_call(attn_forward_kernel, name='attn_forward', out_shape=[sds((...  114 us
    pallas_call x1, Pallas kernels, mlp(): pl.pallas_call(mlp_kernel, name='feed_forward', out_shape=[sds((SPAN, WID...  66.3 us

profile of v3, /device:TPU:0, one launch (start us, length us, event | category | flops | bytes accessed | tf_op | source)
XLA Modules:
  0.0 322.3 jit_solution(14742474394868287782)
XLA Ops:
  0.6 0.0 copy-start
  0.7 0.0 copy-start.3
  2.0 0.1 pad.13.clone
  2.1 0.1 pad.14.clone
  2.2 0.7 maximum_maximum_fusion
  2.9 0.1 copy.44
  3.0 0.8 copy.62
  3.9 0.0 copy-done
  3.9 0.8 copy_bitcast_fusion.5
  4.7 0.7 maximum_bitcast_fusion.pq
  5.3 1.4 reshape.85
  6.8 0.1 copy.59
  6.9 0.5 reshape.86
  7.3 0.0 copy-done.3
  7.3 0.5 reshape.87
  7.9 0.1 copy.58
  8.0 0.5 reshape.88
  8.4 0.8 pad_maximum_fusion.pm
  9.2 113.8 %attn_forward.1 = (f32[128,2048]{1,0:T(8,128)}, bf16[128,2048]{1,0:T(8,128)(2,1)}, bf16[8,128,2048]{2,1,0:T(8,128)(2,1)}, f32[1024,384]{1,0:T(8,128)}, bf16[8,25...) custom-call(bf16[128,2048]{1,0:T(8,128)(2,1)} %bitcast.66, ...), custom_call_target="tpu_custom_call" | custom-call | tf_op jit(solution)/shard_map/attn_forward/pallas_call | solution.py:516
  123.1 66.3 %feed_forward.1 = (f32[128,2048]{1,0:T(8,128)}, bf16[128,2048]{1,0:T(8,128)(2,1)}, f32[8,2048]{1,0:T(8,128)}, bf16[2048,1536]{1,0:T(8,128)(2,1)}, bf16[768,2048]...) custom-call(bf16[128,2048]{1,0:T(8,128)(2,1)} %get-tuple-element.41.h2_loc, bf16[8,128,2048]{2,1,0:T(8,128)(2,1)} %get-tuple-element.42.dyg, ...), custom_call_target="tpu_custom_call" | custom-call | tf_op jit(solution)/shard_map/feed_forward/pallas_call | solution.py:686
  189.4 116.6 %attn_backward.1 = (f32[128,2048]{1,0:T(8,128)}, bf16[128,2048]{1,0:T(8,128)(2,1)}, bf16[8,16,1536]{2,1,0:T(8,128)(2,1)}, f32[48,2048]{1,0:T(8,128)}, bf16[8,16,...) custom-call(bf16[128,2048]{1,0:T(8,128)(2,1)} %get-tuple-element.47.dab_loc, ...), custom_call_target="tpu_custom_call" | custom-call | tf_op jit(solution)/shard_map/attn_backward/pallas_call | solution.py:1070
  306.0 1.3 fusion.1
  307.3 1.3 slice_bitcast_fusion.3
  308.7 0.9 convert_element_type.6
  309.6 0.6 copy.60
  310.3 0.7 copy.48
  310.9 0.6 copy.61
  311.6 2.2 reshape.95
  313.8 0.1 fusion
  314.0 0.6 copy.43
  314.6 0.0 copy-start.1
  314.6 1.4 squeeze.18
  316.0 0.0 copy-start.4
  316.0 0.6 copy.42
  316.6 0.0 copy-start.2
  316.6 1.4 squeeze.17
  318.0 1.9 copy.69
  319.9 0.0 copy-done.1
  319.9 1.0 copy.70
  320.9 0.0 copy-done.4
  320.9 0.7 copy.71
  321.6 0.0 copy-done.2
  321.6 0.7 copy.72
  (4 shorter events, 0.0 us)
Async XLA Ops:
  0.6 3.2 %copy-start = (bf16[16,1024]{1,0:T(8,128)(2,1)S(1)}, bf16[16,1024]{1,0:T(8,128)(2,1)}, u32[]{:S(2)}) copy-start(bf16[16,1024]{1,0:T(8,128)(2,1)} %param.18) | copy-start | bytes 98308
  0.7 6.7 %copy-start.3 = (bf16[16,6144]{1,0:T(8,128)(2,1)S(1)}, bf16[16,6144]{1,0:T(8,128)(2,1)}, u32[]{:S(2)}) copy-start(bf16[16,6144]{1,0:T(8,128)(2,1)} %param.25) | copy-start | bytes 589828
  314.6 5.3 %copy-start.1 = (f32[128,2048]{1,0:T(8,128)S(1)}, f32[128,2048]{1,0:T(8,128)}, u32[]{:S(2)}) copy-start(f32[128,2048]{1,0:T(8,128)} %get-tuple-element.63) | copy-start | bytes 3145732
  316.0 4.9 %copy-start.4 = (f32[16,2048]{1,0:T(8,128)S(1)}, f32[16,2048]{1,0:T(8,128)}, u32[]{:S(2)}) copy-start(f32[16,2048]{1,0:T(8,128)} %get-tuple-element.98) | copy-start | bytes 393220
  316.6 4.9 %copy-start.2 = (f32[48,2048]{1,0:T(8,128)S(1)}, f32[48,2048]{1,0:T(8,128)}, u32[]{:S(2)}) copy-start(f32[48,2048]{1,0:T(8,128)} %get-tuple-element.104) | copy-start | bytes 1179652

commit v4 on v3

v4 whole, which is shorter than its diff:
```python
import functools
import math

import jax
import jax.numpy as jnp
import numpy as np
from jax import lax
from jax.experimental import pallas as pl
from jax.experimental.pallas import tpu as pltpu
from jax.sharding import PartitionSpec as P

QUERY_HEADS = 16
KEY_VALUE_HEADS = 8
HEAD_DIM = 128

eps_norm = 1e-06
rope_base = 1000000.0
score_scale = 1.0 / math.sqrt(HEAD_DIM)

f32 = jnp.float32
bf16 = jnp.bfloat16

AXIS = 4
ND, NS = 16, 8
SPAN = 128
WIDTH = 2048
LENGTH = SPAN * NS
WR = 16
FR = 48
FFS = ND * FR
QKV = 512
GCOL = 128
VMEM_LIMIT = 60 * 2**20
MESH = pl.DeviceIdType.MESH


def dot(a, b):
    return jnp.dot(a, b, preferred_element_type=f32)


def dot_tn(a, b):
    return lax.dot_general(a, b, (((0,), (0,)), ((), ())), preferred_element_type=f32)


def dot_nt(a, b):
    return lax.dot_general(a, b, (((1,), (1,)), ((), ())), preferred_element_type=f32)


def rms(values):
    return lax.rsqrt(jnp.mean(values * values, axis=-1, keepdims=True) + eps_norm)


def rms_back(grad_out, gain, unit, inv):
    grad_unit = grad_out * gain
    return inv * (grad_unit - unit * jnp.mean(grad_unit * unit, axis=-1, keepdims=True))


def rope_constants():
    half = HEAD_DIM // 2
    freqs = np.float32(rope_base) ** (
        -(np.arange(half, dtype=np.float32) * np.float32(2.0) / np.float32(2 * half))
    )
    angles = np.arange(LENGTH, dtype=np.float32)[:, None] * freqs.astype(np.float32)[None, :]
    cos, sin = np.cos(angles), np.sin(angles)
    return np.concatenate([cos, sin], axis=1).astype(np.float32)


def coords():
    dp, sq = lax.axis_index("dp"), lax.axis_index("seq")
    return dp // AXIS, dp % AXIS, sq // 2, sq % 2


def device(y, z, x, c):
    return (y * AXIS + z, x * 2 + c)


def seq_peers(y, z, x, c):
    return [
        (k, j, device(y, z, (x + k) % AXIS, (c + j) % 2))
        for k in range(AXIS)
        for j in range(2)
        if (k, j) != (0, 0)
    ]


def greet(peers):
    sem = pltpu.get_barrier_semaphore()
    for peer in peers:
        pl.semaphore_signal(sem, inc=1, device_id=peer, device_id_type=MESH)


def all_in(peers):
    pl.semaphore_wait(pltpu.get_barrier_semaphore(), len(peers))


def around(y, z, x, c):
    yp = [device((y + k) % AXIS, z, x, c) for k in (1, 2, 3)]
    zp = [device(y, (z + k) % AXIS, x, c) for k in (1, 2, 3)]
    return seq_peers(y, z, x, c), yp, zp


class Copies:
    def __init__(self, send, recv, local):
        self.send, self.recv, self.local = send, recv, local
        self.n, self.n_local = 0, 0
        self.sent = []

    def to(self, src, dst, dev):
        copy = pltpu.make_async_remote_copy(
            src_ref=src, dst_ref=dst, send_sem=self.send.at[self.n], recv_sem=self.recv.at[self.n],
            device_id=dev, device_id_type=MESH,
        )
        self.n += 1
        copy.start()
        self.sent.append(copy)
        return copy

    def here(self, src, dst):
        copy = pltpu.make_async_copy(src, dst, self.local.at[self.n_local])
        self.n_local += 1
        copy.start()
        return copy

    def finish(self):
        for copy in self.sent:
            copy.wait_send()
        self.sent = []

    def drain(self, copies):
        for copy in copies:
            copy.wait_send()
        done = {id(copy) for copy in copies}
        self.sent = [copy for copy in self.sent if id(copy) not in done]


class SeqGather:
    def __init__(self, cm, own, buf, co):
        self.cm, self.own, self.buf, self.co = cm, own, buf, co
        self.half = buf.shape[1] // 2

    def slot(self, k):
        y, z, x, c = self.co
        return self.buf.at[((x + k) % AXIS) * 2 + c]

    def start(self):
        y, z, x, c = self.co
        self.sib = device(y, z, x, 1 - c)
        self.plus, self.minus = device(y, z, (x + 1) % AXIS, c), device(y, z, (x + 3) % AXIS, c)
        self.a = self.cm.to(self.own, self.slot(0), self.plus)
        self.b = self.cm.to(self.own, self.slot(0), self.minus)
        self.s0 = self.cm.to(self.own, self.slot(0), self.sib)
        self.l = self.cm.here(self.own, self.slot(0))

    def forward(self):
        h = self.half
        lo, hi = pl.ds(0, h), pl.ds(h, h)
        self.a.wait_recv()
        left = self.slot(3)
        self.fa = self.cm.to(left.at[lo], left.at[lo], self.plus)
        self.s1 = self.cm.to(left, left, self.sib)
        self.b.wait_recv()
        right = self.slot(1)
        self.fb = self.cm.to(right.at[hi], right.at[hi], self.minus)
        self.s2 = self.cm.to(right, right, self.sib)

    def last(self):
        h = self.half
        lo, hi = pl.ds(0, h), pl.ds(h, h)
        opp = self.slot(2)
        self.fa.wait_recv()
        self.s3 = self.cm.to(opp.at[lo], opp.at[lo], self.sib)
        self.fb.wait_recv()
        self.s4 = self.cm.to(opp.at[hi], opp.at[hi], self.sib)

    def drain(self):
        self.cm.drain(
            [self.a, self.b, self.s0, self.fa, self.s1, self.fb, self.s2, self.s3, self.s4]
        )

    def wait_chip(self, k):
        if k == 0:
            self.l.wait()
            self.s0.wait_recv()
        elif k == 3:
            self.s1.wait_recv()
        elif k == 1:
            self.s2.wait_recv()
        else:
            self.s3.wait_recv()
            self.s4.wait_recv()


class DpGather:
    def __init__(self, cm, own, buf, co, axis):
        self.cm, self.own, self.buf, self.co, self.axis = cm, own, buf, co, axis
        n = own.shape[axis]
        self.h, self.q = n // 2, n // 4

    def part(self, ref, half, quarter=None):
        lo = half * self.h + (0 if quarter is None else quarter * self.q)
        size = self.h if quarter is None else self.q
        cut = pl.ds(lo, size)
        lead = len(ref.shape) - 2
        index = (slice(None),) * lead + ((cut, slice(None)) if self.axis == 0 else (slice(None), cut))
        return ref.at[index]

    def both(self, src_p, dst_p, src_m, dst_m, along):
        y, z, x, c = self.co
        if along == 0:
            plus, minus = device((y + 1) % AXIS, z, x, c), device((y + 3) % AXIS, z, x, c)
        else:
            plus, minus = device(y, (z + 1) % AXIS, x, c), device(y, (z + 3) % AXIS, x, c)
        return (self.cm.to(src_p, dst_p, plus), self.cm.to(src_m, dst_m, minus))

    def start(self):
        y, z, _, _ = self.co
        mine = self.buf.at[y, z]
        self.l = self.cm.here(self.own, mine)
        self.one = []
        for half in (0, 1):
            src, dst = self.part(self.own, half), self.part(mine, half)
            self.one.append(self.both(src, dst, src, dst, half))

    def spread(self):
        y, z, _, _ = self.co
        self.two = []
        for half in (0, 1):
            if half == 0:
                left, right = self.buf.at[(y + 3) % AXIS, z], self.buf.at[(y + 1) % AXIS, z]
            else:
                left, right = self.buf.at[y, (z + 3) % AXIS], self.buf.at[y, (z + 1) % AXIS]
            for copy in self.one[half]:
                copy.wait_recv()
            lp, rp = self.part(left, half, 0), self.part(right, half, 1)
            self.two.append(self.both(lp, lp, rp, rp, half))

    def line(self, half, k):
        y, z, _, _ = self.co
        if half == 0:
            return self.buf.at[:, (z + k) % AXIS]
        return self.buf.at[(y + k) % AXIS]

    def turn(self):
        self.l.wait()
        self.three = []
        for half in (0, 1):
            for copy in self.two[half]:
                copy.wait_recv()
            mine = self.part(self.line(half, 0), half)
            self.three.append(self.both(mine, mine, mine, mine, 1 - half))

    def last(self):
        self.four = []
        for half in (0, 1):
            for copy in self.three[half]:
                copy.wait_recv()
            lp = self.part(self.line(half, 3), half, 0)
            rp = self.part(self.line(half, 1), half, 1)
            self.four.append(self.both(lp, lp, rp, rp, 1 - half))

    def wait(self):
        for half in (0, 1):
            for copy in self.four[half]:
                copy.wait_recv()


def off(n):
    return jnp.where(n == 0, 2, jnp.where(n == 1, 1, jnp.where(n == 2, 3, 0)))


class SeqScatter:
    def __init__(self, part, sib_recv, x_recv, sems, co, kept=None):
        self.part, self.sib_recv, self.x_recv, self.sems, self.co = part, sib_recv, x_recv, sems, co
        self.kept = kept

    def ours(self, n):
        return self.part.at[2 * n + 1] if self.kept is None else self.kept.at[n]

    def sib_copy(self, n):
        y, z, x, c = self.co
        return pltpu.make_async_remote_copy(
            src_ref=self.part.at[2 * n], dst_ref=self.sib_recv.at[n],
            send_sem=self.sems.at[0, n], recv_sem=self.sems.at[1, n],
            device_id=device(y, z, x, 1 - c), device_id_type=MESH,
        )

    def x_copy(self, n):
        y, z, x, c = self.co
        return pltpu.make_async_remote_copy(
            src_ref=self.ours(n), dst_ref=self.x_recv.at[n],
            send_sem=self.sems.at[2, n], recv_sem=self.sems.at[3, n],
            device_id=device(y, z, (x + off(n)) % AXIS, c), device_id_type=MESH,
        )

    def combine(self, n, go=True):
        self.sib_copy(n).wait_recv()
        ours = self.ours(n)

        def add(i, _):
            cut = pl.ds(i * 32, 32)
            total = ours[cut, :].astype(f32) + self.sib_recv[n, cut, :].astype(f32)
            ours[cut, :] = total.astype(bf16)
            return 0

        lax.fori_loop(0, SPAN // 32, add, 0)
        if go:

            @pl.when(n < 3)
            def _():
                self.x_copy(n).start()

    def arrive(self):
        for n in range(3):
            self.x_copy(n).wait_recv()

    def rows(self, cut):
        total = self.ours(3)[cut, :].astype(f32)
        for n in range(3):
            total = total + self.x_recv[n, cut, :].astype(f32)
        return total

    def finish(self):
        for n in range(4):
            self.sib_copy(n).wait_send()
        for n in range(3):
            self.x_copy(n).wait_send()


def scatter_scratch():
    return [
        pltpu.VMEM((8, SPAN, WIDTH), bf16),
        pltpu.VMEM((4, SPAN, WIDTH), bf16),
        pltpu.VMEM((3, SPAN, WIDTH), bf16),
        pltpu.SemaphoreType.DMA((4, 4)),
    ]


def swap(u):
    return pltpu.roll(u, HEAD_DIM // 2, 1)


def rope_rows(table):
    low = lax.broadcasted_iota(jnp.int32, table.shape, 1) < HEAD_DIM // 2
    other = swap(table)
    return jnp.where(low, table, other), jnp.where(low, -other, table)


def peer_index(x, c, k, j):
    return ((x + k) % AXIS) * 2 + (c + j) % 2


class DpScatter:
    def __init__(self, cm, grad, acc, one, two, co, tile):
        self.cm, self.grad, self.acc, self.r1, self.r2 = cm, grad, acc, one, two
        self.co, self.tile = co, tile
        self.h = acc.shape[2]

    def part(self, ref, half):
        return ref.at[:, pl.ds(half * self.h, self.h)]

    def line(self, half, k):
        y, z, _, _ = self.co
        if half == 0:
            return self.part(self.grad.at[(y + k) % AXIS], half)
        return self.part(self.grad.at[:, (z + k) % AXIS], half)

    def away(self, along, k):
        y, z, x, c = self.co
        if along == 0:
            return device((y + k) % AXIS, z, x, c)
        return device(y, (z + k) % AXIS, x, c)

    def start(self):
        self.own = [self.cm.here(self.line(h, 0), self.acc.at[h]) for h in (0, 1)]
        self.first = [[], []]
        for k in (2, 1, 3):
            for h in (0, 1):
                self.first[h].append(
                    self.cm.to(self.line(h, k), self.r1.at[h, k - 1], self.away(h, k))
                )

    def add_first(self):
        rows = self.acc.shape[2]
        for h in (0, 1):
            self.own[h].wait()
            for copy in self.first[h]:
                copy.wait_recv()

            def add(t, _, h=h):
                q = t // (rows // self.tile)
                cut = pl.ds((t % (rows // self.tile)) * self.tile, self.tile)
                total = self.acc[h, q, cut, :].astype(f32)
                for k in range(3):
                    total = total + self.r1[h, k, q, cut, :].astype(f32)
                self.acc[h, q, cut, :] = total.astype(bf16)
                return 0

            lax.fori_loop(0, AXIS * (rows // self.tile), add, 0)

    def send_second(self):
        y, z, _, _ = self.co
        self.second = [[], []]
        for h in (0, 1):
            mine = z if h == 0 else y
            for k in (2, 1, 3):
                self.second[h].append(
                    self.cm.to(self.acc.at[h, (mine + k) % AXIS], self.r2.at[h, k - 1], self.away(1 - h, k))
                )

    def mid(self):
        self.add_first()
        self.send_second()

    def last(self, out):
        y, z, _, _ = self.co
        rows, cols = self.acc.shape[2:]
        for h in (0, 1):
            for copy in self.second[h]:
                copy.wait_recv()
            mine = z if h == 0 else y

            def add(t, _, h=h, mine=mine):
                cut = pl.ds(t * self.tile, self.tile)
                total = self.acc[h, mine, cut, :].astype(f32)
                for k in range(3):
                    total = total + self.r2[h, k, cut, :].astype(f32)
                out[pl.ds(h * self.h + t * self.tile, self.tile), :] = total.astype(out.dtype)
                return 0

            lax.fori_loop(0, rows // self.tile, add, 0)


def dp_scatter_scratch(rows, cols):
    return [
        pltpu.VMEM((2, AXIS, rows, cols), bf16),
        pltpu.VMEM((2, 3, AXIS, rows, cols), bf16),
        pltpu.VMEM((2, 3, rows, cols), bf16),
    ]


def front_kernel(
    tok, cot, extra, w_query, w_key, w_value, w_out, w_gate, w_up, w_down, table,
    x1_o, dx1_o, dab_o, gain2_o, h1_o, pre_o, qb, kb, vb, ob, gains, gq_o, wo_o, ggu_o, pd_o, dacc_o,
    xg, pq, pm, wod, a2a_q, a2a_m, wq, wo_b, wo_v, wd_b, wd_v, wgu, o1, o2, o3o, o3d, h2_loc,
    dy_v, hid, dgu, pdv, d_one,
    part, sib_recv, x_recv, rs_sems, rs_sems2, send, recv, local,
):
    co = y, z, x, c = coords()
    s = x * 2 + c
    peers, yp, zp = around(*co)
    everyone = [p for _, _, p in peers] + yp + zp
    greet(everyone)
    cm = Copies(send, recv, local)
    for t in range(NS):
        pq[t, :, 0:256] = w_query[:, t * 256 : t * 256 + 256]
        pq[t, :, 256:384] = w_key[:, t * 128 : t * 128 + 128]
        pq[t, :, 384:512] = w_value[:, t * 128 : t * 128 + 128]
        pq[t, :, 512:640] = extra[...]
        pm[t, :, 0:FFS] = w_gate[:, t * FFS : t * FFS + FFS]
        pm[t, :, FFS : 2 * FFS] = w_up[:, t * FFS : t * FFS + FFS]
    wod[0:WR, :] = w_out[...]
    wod[WR : WR + FR, :] = w_down[...]
    all_in(everyone)

    aq = [cm.to(pq.at[peer_index(x, c, k, j)], a2a_q.at[s], p) for k, j, p in peers]
    lq = cm.here(pq.at[s], a2a_q.at[s])
    g_tok = SeqGather(cm, tok, xg, co)
    g_tok.start()

    def quarter(i):
        return pl.ds(pl.multiple_of(i * 512, 512), 512)

    def chunk(i):
        return pl.ds(pl.multiple_of(i * 128, 128), 128)

    o_one = [cm.to(wod.at[:, quarter((y + k) % AXIS)], o1.at[y], yp[k - 1]) for k in (1, 2, 3)]
    l_one = cm.here(wod.at[:, quarter(y)], o1.at[y])
    am = [cm.to(pm.at[peer_index(x, c, k, j)], a2a_m.at[s], p) for k, j, p in peers]
    lm = cm.here(pm.at[s], a2a_m.at[s])
    lq.wait()
    for copy in aq:
        copy.wait_recv()
    g_q = DpGather(cm, a2a_q.reshape(NS * WR, QKV + GCOL), wq, co, 0)
    g_q.start()
    l_one.wait()
    for copy in o_one:
        copy.wait_recv()
    o_two = [cm.to(o1.at[:, :, chunk((z + k) % AXIS)], o2.at[z], zp[k - 1]) for k in (1, 2, 3)]
    l_two = cm.here(o1.at[:, :, chunk(z)], o2.at[z])
    g_q.spread()
    l_two.wait()
    for copy in o_two:
        copy.wait_recv()

    def rows_of(t, lo, n):
        return o2.at[pl.ds((t % 2) * 2, 2), t // 2, pl.ds(lo, n)]

    o_three = []
    for k, j, p in peers:
        t = peer_index(x, c, k, j)
        o_three.append(cm.to(rows_of(t, 0, WR), o3o.at[:, s], p))
        o_three.append(cm.to(rows_of(t, WR, FR), o3d.at[:, s], p))
    l_three = [
        cm.here(rows_of(s, 0, WR), o3o.at[:, s]),
        cm.here(rows_of(s, WR, FR), o3d.at[:, s]),
    ]
    g_q.turn()
    g_tok.forward()
    lm.wait()
    for copy in am:
        copy.wait_recv()
    g_m = DpGather(cm, a2a_m.reshape(NS * WR, 2 * FFS), wgu, co, 0)
    g_m.start()
    for copy in l_three:
        copy.wait()
    for copy in o_three:
        copy.wait_recv()
    g_o = DpGather(cm, o3o.reshape(2 * SPAN, SPAN), wo_b, co, 0)
    g_o.start()
    g_d = DpGather(cm, o3d.reshape(FFS, SPAN), wd_b, co, 0)
    g_d.start()
    g_q.last()
    g_o.spread()
    g_tok.last()
    g_cot = SeqGather(cm, cot, dy_v, co)
    g_cot.start()
    g_o.turn()
    g_m.spread()
    g_d.spread()
    g_q.wait()
    wq_out = cm.here(wq.at[:, :, :, pl.ds(0, QKV)], gq_o)
    g_o.last()
    g_m.turn()
    g_d.turn()

    wq2 = wq.reshape(WIDTH, QKV + GCOL)
    gcols = wq2[:, QKV:]
    flat = gcols.astype(f32).T
    gains[...] = flat[:8]
    gain_one = flat[0:1]
    rows = lax.broadcasted_iota(jnp.int32, (WIDTH, HEAD_DIM), 0)
    cols = lax.broadcasted_iota(jnp.int32, (WIDTH, HEAD_DIM), 1)
    pick = (rows == cols * WR).astype(bf16)
    head_gains = dot(flat[:8].astype(bf16), pick)
    gain_q, gain_k = head_gains[2:3], head_gains[3:4]
    gains[2:4, 0:HEAD_DIM] = head_gains[2:4]

    def normed(i, _):
        cut = pl.ds((i % 4) * 32, 32)
        v = xg[i // 4, cut, :].astype(f32)
        part[i // 4, cut, :] = (v * rms(v) * gain_one).astype(bf16)
        return 0

    for k in (0, 1, 3, 2):
        g_tok.wait_chip(k)
    lax.fori_loop(0, LENGTH // 32, normed, 0)
    h1_copy = cm.here(part, h1_o)
    g_cot.forward()

    def project(i, _):
        h = part[pl.ds(2 * i, 2)].reshape(2 * SPAN, WIDTH)
        p = dot(h, wq2[:, :QKV])
        cut = pl.ds(pl.multiple_of(i * 256, 256), 256)
        pre_o[cut, :] = p[:, :384]
        vb[cut, :] = p[:, 384:].astype(bf16)
        co_t, si_t = rope_rows(table[cut, :])
        for h_i in range(2):
            u = p[:, h_i * 128 : h_i * 128 + 128]
            u = u * rms(u) * gain_q
            u = (u * co_t + swap(u) * si_t).astype(bf16)
            qb[pl.ds(2 * i, 2), pl.ds(h_i * SPAN, SPAN), :] = u.reshape(2, SPAN, HEAD_DIM)
        u = p[:, 256:384]
        u = u * rms(u) * gain_k
        kb[cut, :] = (u * co_t + swap(u) * si_t).astype(bf16)
        return 0

    lax.fori_loop(0, 4, project, 0)
    h1_copy.wait()
    g_tok.drain()
    g_o.wait()
    wo_copy = [
        cm.here(wo_b.at[yy, zz], wo_v.at[:, pl.ds((yy * AXIS + zz) * 128, 128)])
        for yy in range(AXIS)
        for zz in range(AXIS)
    ]
    for copy in wo_copy:
        copy.wait()
    wo_out = cm.here(wo_v, wo_o)

    rs = SeqScatter(part, sib_recv, x_recv, rs_sems, co)

    def attend(i, slot):
        sc = dot_nt(qb[i], kb[...]) * score_scale
        r = lax.broadcasted_iota(jnp.int32, (2 * SPAN, LENGTH), 0) % SPAN + i * SPAN
        k = lax.broadcasted_iota(jnp.int32, (2 * SPAN, LENGTH), 1)
        sc = jnp.where(k <= r, sc, -1e30)
        top = jnp.max(sc, axis=-1, keepdims=True)
        ex = jnp.exp(sc - top)
        tot = jnp.sum(ex, axis=-1, keepdims=True)
        pb = (ex / tot).astype(bf16)
        o = dot(pb, vb[...]).astype(bf16)
        o = jnp.concatenate([o[:SPAN], o[SPAN:]], axis=1)
        ob[pl.ds(pl.multiple_of(i * SPAN, SPAN), SPAN), :] = o
        part[slot] = dot(o, wo_v[...]).astype(bf16)

    def pair(n, _):
        chip = (x + off(n)) % AXIS
        attend(chip * 2 + 1 - c, 2 * n)
        rs.sib_copy(n).start()
        attend(chip * 2 + c, 2 * n + 1)
        rs.combine(n)
        return 0

    lax.fori_loop(0, 4, pair, 0)
    g_cot.last()
    g_m.last()
    g_d.last()
    rs.arrive()

    def residual(i, _):
        cut = pl.ds(i * 32, 32)
        v = xg[s, cut, :].astype(f32) + rs.rows(cut)
        x1_o[cut, :] = v
        h2_loc[cut, :] = (v * rms(v) * gains[1:2, :]).astype(bf16)
        return 0

    lax.fori_loop(0, SPAN // 32, residual, 0)
    rs.finish()

    g_h2 = SeqGather(cm, h2_loc, xg, co)
    g_h2.start()
    for k in (0, 1, 3, 2):
        g_cot.wait_chip(k)
    g_d.wait()
    wd_copy = [
        cm.here(wd_b.at[yy, zz], wd_v.at[:, pl.ds((yy * AXIS + zz) * 128, 128)])
        for yy in range(AXIS)
        for zz in range(AXIS)
    ]
    g_m.wait()
    for copy in wd_copy:
        copy.wait()
    rs = SeqScatter(part, sib_recv, x_recv, rs_sems2, co)
    wgu2 = wgu.reshape(WIDTH, 2 * FFS)
    order = {2: 0, 1: 1, 3: 2, 0: 3}

    def chip_of(k):
        return (x + k) % AXIS

    def forward(k):
        chip = chip_of(k)
        rows = pl.ds(pl.multiple_of(chip * 256, 256), 256)
        two = pl.ds(2 * chip, 2)

        def tile(f, _):
            lo = pl.multiple_of(f * 256, 256)
            h = xg[two].reshape(256, WIDTH)
            gate = dot(h, wgu2[:, pl.ds(lo, 256)])
            up = dot(h, wgu2[:, pl.ds(pl.multiple_of(lo + FFS, 256), 256)])
            dh = dot_nt(dy_v[two].reshape(256, WIDTH), wd_v[pl.ds(lo, 256), :])
            sig = jax.nn.sigmoid(gate)
            silu = gate * sig
            hid[rows, pl.ds(lo, 256)] = (silu * up).astype(bf16)
            dgate = dh * up * (sig * (1.0 + gate * (1.0 - sig)))
            dgu[rows, pl.ds(lo, 256)] = dgate.astype(bf16)
            dgu[rows, pl.ds(pl.multiple_of(lo + FFS, 256), 256)] = (dh * silu).astype(bf16)
            return 0

        lax.fori_loop(0, FFS // 256, tile, 0)

    def put(ref, n, cols, o):
        ref[2 * n + 1 - c, :, cols] = o[:SPAN]
        ref[2 * n + c, :, cols] = o[SPAN:]

    def back(k):
        n = order[k]
        rows = pl.ds(pl.multiple_of(chip_of(k) * 256, 256), 256)

        def tile(m, _):
            cols = pl.ds(pl.multiple_of(m * 256, 256), 256)
            put(part, n, cols, dot_nt(dgu[rows, :], wgu2[cols, :]).astype(bf16))
            return 0

        lax.fori_loop(0, WIDTH // 256, tile, 0)
        rs.sib_copy(n).start()

    g_h2.wait_chip(0)
    forward(0)
    g_h2.forward()
    back(0)
    g_h2.wait_chip(3)
    forward(3)
    g_h2.last()
    back(3)
    g_h2.wait_chip(1)
    forward(1)
    rs.combine(order[3])
    back(1)
    g_h2.wait_chip(2)
    forward(2)
    rs.combine(order[1])
    back(2)
    rs.combine(order[0])
    cm.finish()

    def down_grad(m, _):
        cut = pl.ds(pl.multiple_of(m * 256, 256), 256)
        o = dot_tn(hid[:, cut], dy_v[...].reshape(LENGTH, WIDTH)).astype(bf16)
        for yy in range(AXIS):
            for zz in range(AXIS):
                lo = (yy * AXIS + zz) * 128
                wd_b[yy, zz, cut, :] = o[:, lo : lo + 128]
        return 0

    lax.fori_loop(0, 1, down_grad, 0)
    rs.combine(order[2])
    lax.fori_loop(1, FFS // 256, down_grad, 0)
    r_d = DpScatter(cm, wd_b, dacc_o, d_one, None, co, 128)
    r_d.start()

    for k in range(4):
        n = order[k]
        rows = pl.ds(pl.multiple_of(chip_of(k) * 256, 256), 256)

        def down(m, _):
            cols = pl.ds(pl.multiple_of(m * 512, 512), 512)
            put(pdv, n, cols, dot(hid[rows, :], wd_v[:, cols]).astype(bf16))
            return 0

        lax.fori_loop(0, WIDTH // 512, down, 0)
    outs = [cm.here(pdv, pd_o)]

    def gate_up(m, _):
        cols = pl.ds(pl.multiple_of(m * 256, 256), 256)
        wgu2[cols, :] = dot_tn(xg[:, :, cols].reshape(LENGTH, 256), dgu[...]).astype(bf16)
        return 0

    lax.fori_loop(0, WIDTH // 256, gate_up, 0)
    outs.append(cm.here(wgu, ggu_o))
    rs.arrive()
    gain_two = gains[1:2, :]

    def mlp_back(i, acc):
        cut = pl.ds(i * 32, 32)
        v = x1_o[cut, :]
        inv = rms(v)
        unit = v * inv
        dh2 = rs.rows(cut)
        dx1 = dy_v[s, cut, :].astype(f32) + rms_back(dh2, gain_two, unit, inv)
        dx1_o[cut, :] = dx1
        dab_o[cut, :] = dx1.astype(bf16)
        return acc + jnp.sum(dh2 * unit, axis=0, keepdims=True)

    acc = lax.fori_loop(0, SPAN // 32, mlp_back, jnp.zeros((1, WIDTH), f32))
    gain2_o[...] = jnp.broadcast_to(acc, (8, WIDTH))
    r_d.add_first()
    rs.finish()
    wo_out.wait()
    wq_out.wait()
    for copy in outs:
        copy.wait()
    cm.finish()


def front(*args):
    any_, vm = pl.BlockSpec(memory_space=pl.ANY), pl.BlockSpec(memory_space=pltpu.VMEM)
    sds = jax.ShapeDtypeStruct
    vmem = pltpu.VMEM
    n_copies, n_local = 160, 64
    return pl.pallas_call(
        front_kernel,
        name="attn_forward",
        out_shape=[
            sds((SPAN, WIDTH), f32), sds((SPAN, WIDTH), f32), sds((SPAN, WIDTH), bf16),
            sds((8, WIDTH), f32), sds((8, SPAN, WIDTH), bf16), sds((LENGTH, 384), f32),
            sds((8, 2 * SPAN, 128), bf16), sds((LENGTH, 128), bf16), sds((LENGTH, 128), bf16),
            sds((LENGTH, 256), bf16), sds((8, WIDTH), f32), sds((4, 4, 128, QKV), bf16),
            sds((256, WIDTH), bf16), sds((4, 4, 128, 2 * FFS), bf16), sds((8, SPAN, WIDTH), bf16),
            sds((2, 4, FFS // 2, 128), bf16),
        ],
        in_specs=[any_] * 2 + [vm] * 9,
        out_specs=[vm, vm, vm, vm, any_, vm, vm, vm, vm, vm, vm, any_, any_, any_, any_, vm],
        scratch_shapes=[
            vmem((8, SPAN, WIDTH), bf16),
            vmem((NS, WR, QKV + GCOL), bf16), vmem((NS, WR, 2 * FFS), bf16),
            vmem((WR + FR, WIDTH), bf16),
            vmem((NS, WR, QKV + GCOL), bf16), vmem((NS, WR, 2 * FFS), bf16),
            vmem((4, 4, 128, QKV + GCOL), bf16),
            vmem((4, 4, 256, 128), bf16), vmem((256, WIDTH), bf16),
            vmem((4, 4, FFS, 128), bf16), vmem((FFS, WIDTH), bf16),
            vmem((4, 4, 128, 2 * FFS), bf16),
            vmem((4, WR + FR, 512), bf16), vmem((4, 4, WR + FR, 128), bf16),
            vmem((2, NS, WR, 128), bf16), vmem((2, NS, FR, 128), bf16),
            vmem((SPAN, WIDTH), bf16),
            vmem((8, SPAN, WIDTH), bf16), vmem((LENGTH, FFS), bf16), vmem((LENGTH, 2 * FFS), bf16),
            vmem((8, SPAN, WIDTH), bf16), vmem((2, 3, AXIS, FFS // 2, 128), bf16),
            *scatter_scratch(),
            pltpu.SemaphoreType.DMA((4, 4)),
            pltpu.SemaphoreType.DMA((n_copies,)),
            pltpu.SemaphoreType.DMA((n_copies,)),
            pltpu.SemaphoreType.DMA((n_local,)),
        ],
        compiler_params=pltpu.CompilerParams(
            collective_id=1, has_side_effects=True, vmem_limit_bytes=VMEM_LIMIT
        ),
    )(*args)


class RowsHome:
    def __init__(self, cm, res, r2, r1, out, co):
        self.cm, self.res, self.r2, self.r1, self.out, self.co = cm, res, r2, r1, out, co
        self.peers, self.yp, self.zp = around(*co)

    def step(self, sends, here):
        self.wait()
        self.arriving = [self.cm.to(*a) for a in sends]
        self.local = self.cm.here(*here)

    def wait(self):
        if hasattr(self, "arriving"):
            self.local.wait()
            for copy in self.arriving:
                copy.wait_recv()

    def over_seq(self):
        y, z, x, c = self.co
        s = x * 2 + c
        dst = self.r2.at[pl.ds((s % 2) * 2, 2), s // 2]
        self.step(
            [(self.res.at[:, peer_index(x, c, k, j)], dst, p) for k, j, p in self.peers],
            (self.res.at[:, s], dst),
        )

    def over_z(self):
        y, z, x, c = self.co
        dst = self.r1.at[:, :, pl.ds(pl.multiple_of(z * 128, 128), 128)]
        self.step(
            [(self.r2.at[(z + k) % AXIS], dst, self.zp[k - 1]) for k in (1, 2, 3)],
            (self.r2.at[z], dst),
        )

    def over_y(self):
        y, z, x, c = self.co
        dst = self.out.at[:, pl.ds(pl.multiple_of(y * 512, 512), 512)]
        self.step(
            [(self.r1.at[(y + k) % AXIS], dst, self.yp[k - 1]) for k in (1, 2, 3)],
            (self.r1.at[y], dst),
        )


def back_kernel(
    dab_loc, pd, ggu, h1, gq, wo,
    dacc, dx1, tok, x1, gain2, pre, qb, kb, vb, ob, gains, table,
    gt_o, block_o, gwq_o, gwk_o, gwv_o, gwo_o, gwg_o, gwu_o, gwd_o, gg_o,
    dab, h1_v, wq, wo_v, pbuf, dob, dk, dv, dqkv, gacc,
    part, sib_recv, x_recv, rs_sems, kept, sib2, x2, rs2_sems,
    m_acc, m_one, m_two, o_acc, o_one, o_two, q_acc, q_one, q_two, d_two,
    mo, mr, qo, qr, go, gqk, oo, o2g, o1g, ow, od, d2g, d1g, dw,
    gg, g_one, g_two, g_all, g_sum,
    send, recv, local,
):
    co = y, z, x, c = coords()
    s = x * 2 + c
    peers, yp, zp = around(*co)
    everyone = [p for _, _, p in peers] + yp + zp
    greet(everyone)
    cm = Copies(send, recv, local)
    l_pd = [cm.here(pd.at[2 * n + 1], kept.at[n]) for n in range(4)]
    l_wo = cm.here(wo, wo_v)
    l_wq = cm.here(gq, wq)

    def h1_load(m):
        return cm.here(h1.at[:, :, pl.ds(m * 256, 256)], h1_v.at[m % 2])

    l_h1 = [h1_load(0), h1_load(1)]
    all_in(everyone)
    g_dab = SeqGather(cm, dab_loc, dab, co)
    g_dab.start()
    r_d = DpScatter(cm, None, dacc, None, d_two, co, 128)
    r_d.send_second()
    r_m = DpScatter(cm, ggu, m_acc, m_one, m_two, co, 16)
    r_m.start()
    rs2 = SeqScatter(pd, sib2, x2, rs2_sems, co, kept)
    for n in range(4):
        l_pd[n].wait()
        rs2.sib_copy(n).start()

    def probs(i, _):
        sc = dot_nt(qb[i], kb[...]) * score_scale
        r = lax.broadcasted_iota(jnp.int32, (2 * SPAN, LENGTH), 0) % SPAN + i * SPAN
        k = lax.broadcasted_iota(jnp.int32, (2 * SPAN, LENGTH), 1)
        sc = jnp.where(k <= r, sc, -1e30)
        ex = jnp.exp(sc - jnp.max(sc, axis=-1, keepdims=True))
        pbuf[i] = (ex / jnp.sum(ex, axis=-1, keepdims=True)).astype(bf16)
        return 0

    lax.fori_loop(0, 4, probs, 0)
    g_dab.forward()
    lax.fori_loop(4, 8, probs, 0)
    dk[...] = jnp.zeros_like(dk)
    dv[...] = jnp.zeros_like(dv)
    gacc[...] = jnp.zeros_like(gacc)
    l_wo.wait()

    def out_back(k):
        g_dab.wait_chip(k)
        two = pl.ds(2 * ((x + k) % AXIS), 2)
        o = dot_nt(dab[two].reshape(2 * SPAN, WIDTH), wo_v[...]).astype(bf16)
        for j in range(2):
            blk = o[j * SPAN : (j + 1) * SPAN]
            dob[2 * ((x + k) % AXIS) + j] = jnp.concatenate([blk[:, :128], blk[:, 128:]], axis=0)

    out_back(0)
    out_back(3)
    out_back(1)
    for n in range(4):
        rs2.combine(n, False)
    g_dab.last()
    rs2.x_copy(0).start()
    out_back(2)

    def out_grad(m, _):
        cols = pl.ds(pl.multiple_of(m * 512, 512), 512)
        o = dot_tn(ob[...], dab[:, :, cols].reshape(LENGTH, 512)).astype(bf16)
        for j in range(AXIS):
            go[m, j] = o[:, j * 128 : j * 128 + 128]
        return 0

    lax.fori_loop(0, AXIS, out_grad, 0)
    r_o = DpScatter(cm, go, o_acc, o_one, o_two, co, 128)
    r_o.start()

    rs = SeqScatter(part, sib_recv, x_recv, rs_sems, co)
    l_wq.wait()
    wq2 = wq.reshape(WIDTH, QKV)
    gain_q, gain_k = gains[2:3, 0:128], gains[3:4, 0:128]

    def head_back(g, u, gain, co_t, si_t):
        g = g * co_t - swap(g) * si_t
        inv = rms(u)
        unit = u * inv
        return rms_back(g, gain, unit, inv), jnp.sum(g * unit, axis=0, keepdims=True)

    def slot_of(chip):
        k = (chip - x + AXIS) % AXIS
        return jnp.where(k == 2, 0, jnp.where(k == 1, 1, jnp.where(k == 3, 2, 3)))

    def chip_back(t, _):
        chip = 3 - t

        def block(j, _):
            i = chip * 2 + 1 - j
            q, do, p = qb[i], dob[i], pbuf[i]
            dp = dot_nt(do, vb[...])
            pf = p.astype(f32)
            delta = jnp.sum(pf * dp, axis=-1, keepdims=True)
            ds = (pf * (dp - delta)).astype(bf16)
            dk[...] += dot_tn(ds, q)
            dv[...] += dot_tn(p, do)
            dq = dot(ds, kb[...]) * score_scale
            cut = pl.ds(pl.multiple_of(i * SPAN, SPAN), SPAN)
            u = jnp.concatenate([pre[cut, 0:128], pre[cut, 128:256]], axis=0)
            co_t, si_t = rope_rows(table[cut, :])
            co_t = jnp.concatenate([co_t] * 2, axis=0)
            si_t = jnp.concatenate([si_t] * 2, axis=0)
            dqp, gsum = head_back(dq, u, gain_q, co_t, si_t)
            gacc[0:1, :] += gsum
            dqp = dqp.astype(bf16)
            dqkv[cut, 0:128] = dqp[:SPAN]
            dqkv[cut, 128:256] = dqp[SPAN:]
            return 0

        lax.fori_loop(0, 2, block, 0)
        cut = pl.ds(pl.multiple_of(chip * 256, 256), 256)
        co_t, si_t = rope_rows(table[cut, :])
        dkp, gsum = head_back(dk[cut, :] * score_scale, pre[cut, 256:384], gain_k, co_t, si_t)
        gacc[1:2, :] += gsum
        dqkv[cut, 256:384] = dkp.astype(bf16)
        dqkv[cut, 384:512] = dv[cut, :].astype(bf16)
        n = slot_of(chip)

        def tile(m, _):
            cols = pl.ds(pl.multiple_of(m * 512, 512), 512)
            o = dot_nt(dqkv[cut, :], wq2[cols, :]).astype(bf16)
            part[2 * n + 1 - c, :, cols] = o[:SPAN]
            part[2 * n + c, :, cols] = o[SPAN:]
            return 0

        lax.fori_loop(0, WIDTH // 512, tile, 0)
        rs.sib_copy(n).start()
        rs.combine(n)
        return 0

    lax.fori_loop(0, 2, chip_back, 0)
    r_m.mid()
    lax.fori_loop(2, 4, chip_back, 0)
    for n in (1, 2):
        rs2.x_copy(n).start()

    for m in range(8):
        l_h1[m].wait()
        o = dot_tn(h1_v[m % 2].reshape(LENGTH, 256), dqkv[...]).astype(bf16)
        gqk[m // 2, 2 * (m % 2)] = o[:SPAN]
        gqk[m // 2, 2 * (m % 2) + 1] = o[SPAN:]
        if m < 6:
            l_h1.append(h1_load(m + 2))
    r_q = DpScatter(cm, gqk, q_acc, q_one, q_two, co, 64)
    r_q.start()
    r_o.mid()
    r_d.last(od.reshape(FFS, SPAN))
    h_d = RowsHome(cm, od, d2g, d1g, dw, co)
    h_d.over_seq()
    r_m.last(mo.reshape(NS * WR, 2 * FFS))
    a_m = [cm.to(mo.at[peer_index(x, c, k, j)], mr.at[s], p) for k, j, p in peers]
    l_mo = cm.here(mo.at[s], mr.at[s])

    rs.arrive()
    gain_one = gains[0:1, :]

    def input_back(i, acc):
        cut = pl.ds(i * 32, 32)
        v = tok[cut, :].astype(f32)
        inv = rms(v)
        unit = v * inv
        dh1 = rs.rows(cut)
        gt_o[cut, :] = dx1[cut, :] + rms_back(dh1, gain_one, unit, inv)
        return acc + jnp.sum(dh1 * unit, axis=0, keepdims=True)

    gain1 = lax.fori_loop(0, SPAN // 32, input_back, jnp.zeros((1, WIDTH), f32))

    dev_i = lax.broadcasted_iota(jnp.int32, (ND * NS, WIDTH), 0)
    col_j = lax.broadcasted_iota(jnp.int32, (ND * NS, WIDTH), 1)
    mine = col_j // WR == dev_i
    row_j = lax.broadcasted_iota(jnp.int32, (WIDTH, 128), 0)
    lane = lax.broadcasted_iota(jnp.int32, (WIDTH, 128), 1)
    rows = jnp.zeros((ND * NS, 128), f32)
    for v, shift in ((gain1, 0), (gain2[0:1, :], WR)):
        rows = rows + dot(
            jnp.where(mine, v, 0.0).astype(bf16), (lane == row_j % WR + shift).astype(bf16)
        )
    eye_i = lax.broadcasted_iota(jnp.int32, (128, 128), 0)
    eye_j = lax.broadcasted_iota(jnp.int32, (128, 128), 1)
    for n in range(2):
        rows = rows + dot(
            jnp.where(eye_i == eye_j, gacc[n : n + 1, :], 0.0).astype(bf16),
            (eye_j == 2 * WR + n).astype(bf16),
        )
    gg[...] = rows.reshape(AXIS, AXIS, NS, 128)
    g_first = [cm.to(gg.at[(y + k) % AXIS], g_one.at[k - 1], yp[k - 1]) for k in (1, 2, 3)]
    h_d.over_z()
    r_q.mid()
    r_o.last(oo.reshape(2 * SPAN, SPAN))
    h_o = RowsHome(cm, oo, o2g, o1g, ow, co)
    h_o.over_seq()
    for copy in g_first:
        copy.wait_recv()
    gg[y] = gg[y] + g_one[0] + g_one[1] + g_one[2]
    g_second = [cm.to(gg.at[y, (z + k) % AXIS], g_two.at[k - 1], zp[k - 1]) for k in (1, 2, 3)]
    l_mo.wait()
    for copy in a_m:
        copy.wait_recv()
    for t in range(NS):
        gwg_o[:, t * FFS : t * FFS + FFS] = mr[t, :, 0:FFS].astype(f32)
        gwu_o[:, t * FFS : t * FFS + FFS] = mr[t, :, FFS : 2 * FFS].astype(f32)
    h_d.over_y()
    h_o.over_z()
    for copy in g_second:
        copy.wait_recv()
    g_all[s] = gg[y, z] + g_two[0] + g_two[1] + g_two[2]
    g_third = [cm.to(g_all.at[s], g_all.at[s], p) for _, _, p in peers]
    r_q.last(qo.reshape(NS * WR, QKV))
    a_q = [cm.to(qo.at[peer_index(x, c, k, j)], qr.at[s], p) for k, j, p in peers]
    l_qo = cm.here(qo.at[s], qr.at[s])
    h_d.wait()
    gwd_o[...] = dw[...].astype(f32)
    h_o.over_y()
    rs2.arrive()

    def out_rows(i, _):
        cut = pl.ds(i * 32, 32)
        block_o[cut, :] = (x1[cut, :] + rs2.rows(cut)).astype(bf16)
        return 0

    lax.fori_loop(0, SPAN // 32, out_rows, 0)
    for copy in g_third:
        copy.wait_recv()
    total = g_all[0]
    for t in range(1, NS):
        total = total + g_all[t]
    g_sum[...] = total
    gg_o[...] = jnp.broadcast_to(g_sum[pl.ds(s, 1), :], (8, 128))
    h_o.wait()
    gwo_o[...] = ow[...].astype(f32)
    l_qo.wait()
    for copy in a_q:
        copy.wait_recv()
    for t in range(NS):
        gwq_o[:, t * 256 : t * 256 + 256] = qr[t, :, 0:256].astype(f32)
        gwk_o[:, t * 128 : t * 128 + 128] = qr[t, :, 256:384].astype(f32)
        gwv_o[:, t * 128 : t * 128 + 128] = qr[t, :, 384:512].astype(f32)
    rs.finish()
    rs2.finish()
    cm.finish()


def back(*args):
    any_, vm = pl.BlockSpec(memory_space=pl.ANY), pl.BlockSpec(memory_space=pltpu.VMEM)
    sds = jax.ShapeDtypeStruct
    vmem = pltpu.VMEM
    n_copies, n_local = 128, 32
    return pl.pallas_call(
        back_kernel,
        name="attn_backward",
        out_shape=[
            sds((SPAN, WIDTH), f32), sds((SPAN, WIDTH), bf16),
            sds((WR, 2048), f32), sds((WR, 1024), f32), sds((WR, 1024), f32), sds((WR, WIDTH), f32),
            sds((WR, NS * FFS), f32), sds((WR, NS * FFS), f32), sds((FR, WIDTH), f32),
            sds((8, 128), f32),
        ],
        in_specs=[any_] * 6 + [vm] * (len(args) - 6),
        out_specs=[vm] * 10,
        scratch_shapes=[
            vmem((8, SPAN, WIDTH), bf16), vmem((2, 8, SPAN, 256), bf16),
            vmem((4, 4, 128, QKV), bf16), vmem((256, WIDTH), bf16),
            vmem((8, 2 * SPAN, LENGTH), bf16), vmem((8, 2 * SPAN, 128), bf16),
            vmem((LENGTH, 128), f32), vmem((LENGTH, 128), f32), vmem((LENGTH, QKV), bf16),
            vmem((8, 128), f32),
            *scatter_scratch(), vmem((4, SPAN, WIDTH), bf16), *scatter_scratch()[1:],
            *dp_scatter_scratch(64, 2 * FFS), *dp_scatter_scratch(SPAN, 128),
            *dp_scatter_scratch(64, QKV), vmem((2, 3, FFS // 2, 128), bf16),
            vmem((NS, WR, 2 * FFS), bf16), vmem((NS, WR, 2 * FFS), bf16),
            vmem((NS, WR, QKV), bf16), vmem((NS, WR, QKV), bf16),
            vmem((4, 4, 256, 128), bf16), vmem((4, 4, SPAN, QKV), bf16),
            vmem((2, NS, WR, 128), bf16), vmem((4, 4, WR, 128), bf16), vmem((4, WR, 512), bf16),
            vmem((WR, WIDTH), bf16),
            vmem((2, NS, FR, 128), bf16), vmem((4, 4, FR, 128), bf16), vmem((4, FR, 512), bf16),
            vmem((FR, WIDTH), bf16),
            vmem((4, 4, NS, 128), f32), vmem((3, 4, NS, 128), f32), vmem((3, NS, 128), f32),
            vmem((NS, NS, 128), f32), vmem((NS, 128), f32),
            pltpu.SemaphoreType.DMA((n_copies,)),
            pltpu.SemaphoreType.DMA((n_copies,)),
            pltpu.SemaphoreType.DMA((n_local,)),
        ],
        compiler_params=pltpu.CompilerParams(
            collective_id=2, has_side_effects=True, vmem_limit_bytes=VMEM_LIMIT
        ),
    )(*args)


def shards(
    tokens, gain_attn, w_query, key_weight, value_weight, w_out, gain_query,
    key_norm_gain, gain_mlp, w_gate, w_up, w_down, cotangent,
):
    extra = jnp.stack(
        [
            gain_attn,
            gain_mlp,
            jnp.broadcast_to(gain_query, (WR,)),
            jnp.broadcast_to(key_norm_gain, (WR,)),
        ],
        axis=1,
    )
    extra = jnp.pad(extra, ((0, 0), (0, GCOL - 4)))
    table = rope_constants()
    (x1, dx1, dab, gain2, h1, pre, qb, kb, vb, ob, gains, gq, wo, ggu, pd, dacc) = front(
        tokens[0], cotangent[0], extra, w_query, key_weight, value_weight, w_out, w_gate, w_up,
        w_down, table,
    )
    gt, block, g_q, g_k, g_v, g_out, g_gate, g_up, g_down, gg = back(
        dab, pd, ggu, h1, gq, wo,
        dacc, dx1, tokens[0], x1, gain2, pre, qb, kb, vb, ob, gains, table,
    )
    gg = gg[0]
    return (
        block[None], gt[None], gg[:WR], g_q, g_k, g_v, g_out,
        gg[2 * WR : 2 * WR + 1], gg[2 * WR + 1 : 2 * WR + 2], gg[WR : 2 * WR],
        g_gate, g_up, g_down,
    )


def solution(mesh):
    both = P(("dp", "seq"))
    rows = P(("dp", "seq"), None)
    act = P("dp", "seq", None)
    in_specs = (act, both, rows, rows, rows, rows, both, both, both, rows, rows, rows, act)
    out_specs = (act, act, both, rows, rows, rows, rows, both, both, both, rows, rows, rows)
    return jax.shard_map(
        shards, mesh=mesh, in_specs=in_specs, out_specs=out_specs, check_vma=False
    )
```

time: 323 us -> 294 us (0.910)
  Pallas kernels: 297 us -> 275 us
  local copies, waits for them, and re-layouts: 20.2 us -> 16 us
    pallas_call x3 -> x2, Pallas kernels: 297 us -> 275 us  [the longest x1 157 us: front(): pl.pallas_call(front_kernel, name='attn_forward', out_shape=[sds((SPAN, W...]
    unnamed x17 -> x15, local copies, waits for them, and re-layouts: 4.4 us -> 12.5 us
    reshape x11 -> x0, local copies, waits for them, and re-layouts: 6.59 us -> none  [the longest x6 3.04 us: shards(): w.reshape(WR, ND, NS, FR).transpose(2, 0, 1, 3).reshape(NS, WR, FFS)]
where the time goes in v4:
time: 294 us
  Pallas kernels  275 us (94%)
  local copies, waits for them, and re-layouts  16 us (5%)
    pallas_call x1, Pallas kernels, front(): pl.pallas_call(front_kernel, name='attn_forward', out_shape=[sds((SPAN, W...  157 us
    pallas_call x1, Pallas kernels, back(): pl.pallas_call(back_kernel, name='attn_backward', out_shape=[sds((SPAN, W...  118 us
    unnamed x15, local copies, waits for them, and re-layouts  12.5 us

profile of v4, /device:TPU:0, one launch (start us, length us, event | category | flops | bytes accessed | tf_op | source)
XLA Modules:
  0.0 293.6 jit_solution(15576861597196367827)
XLA Ops:
  2.0 0.1 pad.7.clone
  2.0 0.1 pad.8.clone
  2.1 0.7 maximum_maximum_fusion
  2.8 0.1 copy.29
  2.9 0.6 pad.4.extra
  3.5 156.6 %attn_forward.1 = (f32[128,2048]{1,0:T(8,128)}, f32[128,2048]{1,0:T(8,128)}, bf16[128,2048]{1,0:T(8,128)(2,1)}, f32[8,2048]{1,0:T(8,128)}, bf16[8,128,2048]{2,1,...) custom-call(bf16[128,2048]{1,0:T(8,128)(2,1)} %bitcast.14, ...), custom_call_target="tpu_custom_call" | custom-call | tf_op jit(solution)/shard_map/attn_forward/pallas_call | solution.py:770
  160.1 118.2 %attn_backward.1 = (f32[128,2048]{1,0:T(8,128)}, bf16[128,2048]{1,0:T(8,128)(2,1)}, f32[16,2048]{1,0:T(8,128)}, f32[16,1024]{1,0:T(8,128)}, f32[16,1024]{1,0:T(8...) custom-call(bf16[128,2048]{1,0:T(8,128)(2,1)} %get-tuple-element.39., ...), custom_call_target="tpu_custom_call" | custom-call | tf_op jit(solution)/shard_map/attn_backward/pallas_call | solution.py:1111
  278.4 0.0 copy-start.2
  278.4 0.0 copy-start.1
  278.4 0.0 copy-start
  278.4 1.4 fusion
  279.8 1.3 slice_bitcast_fusion
  281.1 1.9 copy.41
  283.0 2.3 copy.42
  285.3 1.6 copy.43
  286.8 1.5 copy.44
  288.3 1.5 copy.45
  289.8 1.6 copy.46
  291.3 0.0 copy-done.2
  291.3 0.7 copy.47
  292.1 0.0 copy-done.1
  292.1 0.7 copy.48
  292.8 0.0 copy-done
  292.8 0.7 copy.49
Async XLA Ops:
  278.4 13.0 %copy-start.2 = (f32[16,6144]{1,0:T(8,128)S(1)}, f32[16,6144]{1,0:T(8,128)}, u32[]{:S(2)}) copy-start(f32[16,6144]{1,0:T(8,128)} %get-tuple-element.92) | copy-start | bytes 1179652
  278.4 13.7 %copy-start.1 = (f32[16,6144]{1,0:T(8,128)S(1)}, f32[16,6144]{1,0:T(8,128)}, u32[]{:S(2)}) copy-start(f32[16,6144]{1,0:T(8,128)} %get-tuple-element.93) | copy-start | bytes 1179652
  278.4 14.5 %copy-start = (f32[48,2048]{1,0:T(8,128)S(1)}, f32[48,2048]{1,0:T(8,128)}, u32[]{:S(2)}) copy-start(f32[48,2048]{1,0:T(8,128)} %get-tuple-element.94) | copy-start | bytes 1179652

commit v5 on v4

--- a/solution.py
+++ b/solution.py
@@ -240,14 +240,18 @@
             return self.buf.at[:, (z + k) % AXIS]
         return self.buf.at[(y + k) % AXIS]
 
-    def turn(self):
+    def turn(self, far=False):
+        y, z, xx, c = self.co
         self.l.wait()
-        self.three = []
+        self.three, self.four = [], [[], []]
         for half in (0, 1):
             for copy in self.two[half]:
                 copy.wait_recv()
             mine = self.part(self.line(half, 0), half)
             self.three.append(self.both(mine, mine, mine, mine, 1 - half))
+            if far:
+                there = device(y, (z + 2) % AXIS, xx, c) if half == 0 else device((y + 2) % AXIS, z, xx, c)
+                self.four[half] = [self.cm.to(mine, mine, there), *self.three[half]]
 
     def last(self):
         self.four = []
@@ -440,9 +444,9 @@
 
 def front_kernel(
     tok, cot, extra, w_query, w_key, w_value, w_out, w_gate, w_up, w_down, table,
-    x1_o, dx1_o, dab_o, gain2_o, h1_o, pre_o, qb, kb, vb, ob, gains, gq_o, wo_o, ggu_o, pd_o, dacc_o,
+    x1_o, dx1_o, dab_o, gain2_o, h1_o, pre_o, qb_o, kb_o, vb_o, ob_o, gains, gq_o, wo_o, ggu_o, pd_o, dacc_o,
     xg, pq, pm, wod, a2a_q, a2a_m, wq, wo_b, wo_v, wd_b, wd_v, wgu, o1, o2, o3o, o3d, h2_loc,
-    dy_v, hid, dgu, pdv, d_one,
+    dy_v, hid, dgu, pdv, d_one, x1_v, pre, qb, kb, vb, ob, d_acc,
     part, sib_recv, x_recv, rs_sems, rs_sems2, send, recv, local,
 ):
     co = y, z, x, c = coords()
@@ -456,16 +460,17 @@
         pq[t, :, 256:384] = w_key[:, t * 128 : t * 128 + 128]
         pq[t, :, 384:512] = w_value[:, t * 128 : t * 128 + 128]
         pq[t, :, 512:640] = extra[...]
+    all_in(everyone)
+
+    aq = [cm.to(pq.at[peer_index(x, c, k, j)], a2a_q.at[s], p) for k, j, p in peers]
+    lq = cm.here(pq.at[s], a2a_q.at[s])
+    g_tok = SeqGather(cm, tok, xg, co)
+    g_tok.start()
+    for t in range(NS):
         pm[t, :, 0:FFS] = w_gate[:, t * FFS : t * FFS + FFS]
         pm[t, :, FFS : 2 * FFS] = w_up[:, t * FFS : t * FFS + FFS]
     wod[0:WR, :] = w_out[...]
     wod[WR : WR + FR, :] = w_down[...]
-    all_in(everyone)
-
-    aq = [cm.to(pq.at[peer_index(x, c, k, j)], a2a_q.at[s], p) for k, j, p in peers]
-    lq = cm.here(pq.at[s], a2a_q.at[s])
-    g_tok = SeqGather(cm, tok, xg, co)
-    g_tok.start()
 
     def quarter(i):
         return pl.ds(pl.multiple_of(i * 512, 512), 512)
@@ -506,6 +511,7 @@
     ]
     g_q.turn()
     g_tok.forward()
+    g_q.last()
     lm.wait()
     for copy in am:
         copy.wait_recv()
@@ -519,19 +525,14 @@
     g_o.start()
     g_d = DpGather(cm, o3d.reshape(FFS, SPAN), wd_b, co, 0)
     g_d.start()
-    g_q.last()
+    g_m.spread()
     g_o.spread()
-    g_tok.last()
-    g_cot = SeqGather(cm, cot, dy_v, co)
-    g_cot.start()
-    g_o.turn()
-    g_m.spread()
     g_d.spread()
+    g_o.turn(True)
+    g_m.turn()
+    g_d.turn()
     g_q.wait()
     wq_out = cm.here(wq.at[:, :, :, pl.ds(0, QKV)], gq_o)
-    g_o.last()
-    g_m.turn()
-    g_d.turn()
 
     wq2 = wq.reshape(WIDTH, QKV + GCOL)
     gcols = wq2[:, QKV:]
@@ -551,17 +552,19 @@
         part[i // 4, cut, :] = (v * rms(v) * gain_one).astype(bf16)
         return 0
 
+    g_tok.last()
+    g_cot = SeqGather(cm, cot, dy_v, co)
+    g_cot.start()
     for k in (0, 1, 3, 2):
         g_tok.wait_chip(k)
     lax.fori_loop(0, LENGTH // 32, normed, 0)
     h1_copy = cm.here(part, h1_o)
-    g_cot.forward()
 
     def project(i, _):
         h = part[pl.ds(2 * i, 2)].reshape(2 * SPAN, WIDTH)
         p = dot(h, wq2[:, :QKV])
         cut = pl.ds(pl.multiple_of(i * 256, 256), 256)
-        pre_o[cut, :] = p[:, :384]
+        pre[cut, :] = p[:, :384]
         vb[cut, :] = p[:, 384:].astype(bf16)
         co_t, si_t = rope_rows(table[cut, :])
         for h_i in range(2):
@@ -575,6 +578,7 @@
         return 0
 
     lax.fori_loop(0, 4, project, 0)
+    outs = [cm.here(pre, pre_o), cm.here(qb, qb_o), cm.here(kb, kb_o), cm.here(vb, vb_o)]
     h1_copy.wait()
     g_tok.drain()
     g_o.wait()
@@ -586,6 +590,7 @@
     for copy in wo_copy:
         copy.wait()
     wo_out = cm.here(wo_v, wo_o)
+    g_cot.forward()
 
     rs = SeqScatter(part, sib_recv, x_recv, rs_sems, co)
 
@@ -607,11 +612,16 @@
         chip = (x + off(n)) % AXIS
         attend(chip * 2 + 1 - c, 2 * n)
         rs.sib_copy(n).start()
+
+        @pl.when(n > 0)
+        def _():
+            rs.combine(n - 1)
+
         attend(chip * 2 + c, 2 * n + 1)
-        rs.combine(n)
         return 0
 
     lax.fori_loop(0, 4, pair, 0)
+    rs.combine(3)
     g_cot.last()
     g_m.last()
     g_d.last()
@@ -620,17 +630,16 @@
     def residual(i, _):
         cut = pl.ds(i * 32, 32)
         v = xg[s, cut, :].astype(f32) + rs.rows(cut)
-        x1_o[cut, :] = v
+        x1_v[cut, :] = v
         h2_loc[cut, :] = (v * rms(v) * gains[1:2, :]).astype(bf16)
         return 0
 
     lax.fori_loop(0, SPAN // 32, residual, 0)
     rs.finish()
+    outs += [cm.here(x1_v, x1_o), cm.here(ob, ob_o)]
 
     g_h2 = SeqGather(cm, h2_loc, xg, co)
     g_h2.start()
-    for k in (0, 1, 3, 2):
-        g_cot.wait_chip(k)
     g_d.wait()
     wd_copy = [
         cm.here(wd_b.at[yy, zz], wd_v.at[:, pl.ds((yy * AXIS + zz) * 128, 128)])
@@ -685,18 +694,22 @@
         rs.sib_copy(n).start()
 
     g_h2.wait_chip(0)
+    g_cot.wait_chip(0)
     forward(0)
     g_h2.forward()
     back(0)
     g_h2.wait_chip(3)
+    g_cot.wait_chip(3)
     forward(3)
     g_h2.last()
     back(3)
     g_h2.wait_chip(1)
+    g_cot.wait_chip(1)
     forward(1)
     rs.combine(order[3])
     back(1)
     g_h2.wait_chip(2)
+    g_cot.wait_chip(2)
     forward(2)
     rs.combine(order[1])
     back(2)
@@ -715,7 +728,7 @@
     lax.fori_loop(0, 1, down_grad, 0)
     rs.combine(order[2])
     lax.fori_loop(1, FFS // 256, down_grad, 0)
-    r_d = DpScatter(cm, wd_b, dacc_o, d_one, None, co, 128)
+    r_d = DpScatter(cm, wd_b, d_acc, d_one, None, co, 128)
     r_d.start()
 
     for k in range(4):
@@ -728,7 +741,7 @@
             return 0
 
         lax.fori_loop(0, WIDTH // 512, down, 0)
-    outs = [cm.here(pdv, pd_o)]
+    outs.append(cm.here(pdv, pd_o))
 
     def gate_up(m, _):
         cols = pl.ds(pl.multiple_of(m * 256, 256), 256)
@@ -742,7 +755,7 @@
 
     def mlp_back(i, acc):
         cut = pl.ds(i * 32, 32)
-        v = x1_o[cut, :]
+        v = x1_v[cut, :]
         inv = rms(v)
         unit = v * inv
         dh2 = rs.rows(cut)
@@ -754,6 +767,7 @@
     acc = lax.fori_loop(0, SPAN // 32, mlp_back, jnp.zeros((1, WIDTH), f32))
     gain2_o[...] = jnp.broadcast_to(acc, (8, WIDTH))
     r_d.add_first()
+    outs.append(cm.here(d_acc, dacc_o))
     rs.finish()
     wo_out.wait()
     wq_out.wait()
@@ -766,7 +780,7 @@
     any_, vm = pl.BlockSpec(memory_space=pl.ANY), pl.BlockSpec(memory_space=pltpu.VMEM)
     sds = jax.ShapeDtypeStruct
     vmem = pltpu.VMEM
-    n_copies, n_local = 160, 64
+    n_copies, n_local = 160, 72
     return pl.pallas_call(
         front_kernel,
         name="attn_forward",
@@ -779,7 +793,7 @@
             sds((2, 4, FFS // 2, 128), bf16),
         ],
         in_specs=[any_] * 2 + [vm] * 9,
-        out_specs=[vm, vm, vm, vm, any_, vm, vm, vm, vm, vm, vm, any_, any_, any_, any_, vm],
+        out_specs=[any_, vm, vm, vm, any_, any_, any_, any_, any_, any_, vm, any_, any_, any_, any_, any_],
         scratch_shapes=[
             vmem((8, SPAN, WIDTH), bf16),
             vmem((NS, WR, QKV + GCOL), bf16), vmem((NS, WR, 2 * FFS), bf16),
@@ -794,6 +808,9 @@
             vmem((SPAN, WIDTH), bf16),
             vmem((8, SPAN, WIDTH), bf16), vmem((LENGTH, FFS), bf16), vmem((LENGTH, 2 * FFS), bf16),
             vmem((8, SPAN, WIDTH), bf16), vmem((2, 3, AXIS, FFS // 2, 128), bf16),
+            vmem((SPAN, WIDTH), f32), vmem((LENGTH, 384), f32), vmem((8, 2 * SPAN, 128), bf16),
+            vmem((LENGTH, 128), bf16), vmem((LENGTH, 128), bf16), vmem((LENGTH, 256), bf16),
+            vmem((2, 4, FFS // 2, 128), bf16),
             *scatter_scratch(),
             pltpu.SemaphoreType.DMA((4, 4)),
             pltpu.SemaphoreType.DMA((n_copies,)),
@@ -849,14 +866,14 @@
 
 
 def back_kernel(
-    dab_loc, pd, ggu, h1, gq, wo,
-    dacc, dx1, tok, x1, gain2, pre, qb, kb, vb, ob, gains, table,
+    dab_loc, pd, ggu, h1, gq, wo, dacc, dx1, tok, x1, pre_i, qb_i, kb_i, vb_i, ob_i,
+    gain2, gains, table,
     gt_o, block_o, gwq_o, gwk_o, gwv_o, gwo_o, gwg_o, gwu_o, gwd_o, gg_o,
     dab, h1_v, wq, wo_v, pbuf, dob, dk, dv, dqkv, gacc,
     part, sib_recv, x_recv, rs_sems, kept, sib2, x2, rs2_sems,
     m_acc, m_one, m_two, o_acc, o_one, o_two, q_acc, q_one, q_two, d_two,
     mo, mr, qo, qr, go, gqk, oo, o2g, o1g, ow, od, d2g, d1g, dw,
-    gg, g_one, g_two, g_all, g_sum,
+    gg, g_one, g_two, g_all, g_sum, d_acc, tok_v, x1_v, pre, qb, kb, vb, ob,
     send, recv, local,
 ):
     co = y, z, x, c = coords()
@@ -865,6 +882,7 @@
     everyone = [p for _, _, p in peers] + yp + zp
     greet(everyone)
     cm = Copies(send, recv, local)
+    l_qk = [cm.here(qb_i, qb), cm.here(kb_i, kb)]
     l_pd = [cm.here(pd.at[2 * n + 1], kept.at[n]) for n in range(4)]
     l_wo = cm.here(wo, wo_v)
     l_wq = cm.here(gq, wq)
@@ -873,10 +891,16 @@
         return cm.here(h1.at[:, :, pl.ds(m * 256, 256)], h1_v.at[m % 2])
 
     l_h1 = [h1_load(0), h1_load(1)]
+    l_in = [
+        cm.here(vb_i, vb), cm.here(ob_i, ob), cm.here(pre_i, pre), cm.here(dacc, d_acc),
+        cm.here(dx1, gt_o), cm.here(tok, tok_v), cm.here(x1, x1_v),
+    ]
     all_in(everyone)
     g_dab = SeqGather(cm, dab_loc, dab, co)
     g_dab.start()
-    r_d = DpScatter(cm, None, dacc, None, d_two, co, 128)
+    r_d = DpScatter(cm, None, d_acc, None, d_two, co, 128)
+    for copy in l_in:
+        copy.wait()
     r_d.send_second()
     r_m = DpScatter(cm, ggu, m_acc, m_one, m_two, co, 16)
     r_m.start()
@@ -894,6 +918,8 @@
         pbuf[i] = (ex / jnp.sum(ex, axis=-1, keepdims=True)).astype(bf16)
         return 0
 
+    for copy in l_qk:
+        copy.wait()
     lax.fori_loop(0, 4, probs, 0)
     g_dab.forward()
     lax.fori_loop(4, 8, probs, 0)
@@ -916,7 +942,8 @@
     for n in range(4):
         rs2.combine(n, False)
     g_dab.last()
-    rs2.x_copy(0).start()
+    for n in range(3):
+        rs2.x_copy(n).start()
     out_back(2)
 
     def out_grad(m, _):
@@ -979,6 +1006,10 @@
         dqkv[cut, 384:512] = dv[cut, :].astype(bf16)
         n = slot_of(chip)
 
+        @pl.when(t % 2 == 1)
+        def _():
+            rs.combine(slot_of(chip + 1))
+
         def tile(m, _):
             cols = pl.ds(pl.multiple_of(m * 512, 512), 512)
             o = dot_nt(dqkv[cut, :], wq2[cols, :]).astype(bf16)
@@ -988,14 +1019,13 @@
 
         lax.fori_loop(0, WIDTH // 512, tile, 0)
         rs.sib_copy(n).start()
-        rs.combine(n)
         return 0
 
     lax.fori_loop(0, 2, chip_back, 0)
+    rs.combine(slot_of(2))
     r_m.mid()
     lax.fori_loop(2, 4, chip_back, 0)
-    for n in (1, 2):
-        rs2.x_copy(n).start()
+    rs.combine(slot_of(0))
 
     for m in range(8):
         l_h1[m].wait()
@@ -1019,11 +1049,11 @@
 
     def input_back(i, acc):
         cut = pl.ds(i * 32, 32)
-        v = tok[cut, :].astype(f32)
+        v = tok_v[cut, :].astype(f32)
         inv = rms(v)
         unit = v * inv
         dh1 = rs.rows(cut)
-        gt_o[cut, :] = dx1[cut, :] + rms_back(dh1, gain_one, unit, inv)
+        gt_o[cut, :] = gt_o[cut, :] + rms_back(dh1, gain_one, unit, inv)
         return acc + jnp.sum(dh1 * unit, axis=0, keepdims=True)
 
     gain1 = lax.fori_loop(0, SPAN // 32, input_back, jnp.zeros((1, WIDTH), f32))
@@ -1078,7 +1108,7 @@
 
     def out_rows(i, _):
         cut = pl.ds(i * 32, 32)
-        block_o[cut, :] = (x1[cut, :] + rs2.rows(cut)).astype(bf16)
+        block_o[cut, :] = (x1_v[cut, :] + rs2.rows(cut)).astype(bf16)
         return 0
 
     lax.fori_loop(0, SPAN // 32, out_rows, 0)
@@ -1107,7 +1137,7 @@
     any_, vm = pl.BlockSpec(memory_space=pl.ANY), pl.BlockSpec(memory_space=pltpu.VMEM)
     sds = jax.ShapeDtypeStruct
     vmem = pltpu.VMEM
-    n_copies, n_local = 128, 32
+    n_copies, n_local = 128, 48
     return pl.pallas_call(
         back_kernel,
         name="attn_backward",
@@ -1117,7 +1147,7 @@
             sds((WR, NS * FFS), f32), sds((WR, NS * FFS), f32), sds((FR, WIDTH), f32),
             sds((8, 128), f32),
         ],
-        in_specs=[any_] * 6 + [vm] * (len(args) - 6),
+        in_specs=[any_] * 15 + [vm] * (len(args) - 15),
         out_specs=[vm] * 10,
         scratch_shapes=[
             vmem((8, SPAN, WIDTH), bf16), vmem((2, 8, SPAN, 256), bf16),
@@ -1137,6 +1167,9 @@
             vmem((FR, WIDTH), bf16),
             vmem((4, 4, NS, 128), f32), vmem((3, 4, NS, 128), f32), vmem((3, NS, 128), f32),
             vmem((NS, NS, 128), f32), vmem((NS, 128), f32),
+            vmem((2, 4, FFS // 2, 128), bf16), vmem((SPAN, WIDTH), bf16), vmem((SPAN, WIDTH), f32),
+            vmem((LENGTH, 384), f32), vmem((8, 2 * SPAN, 128), bf16),
+            vmem((LENGTH, 128), bf16), vmem((LENGTH, 128), bf16), vmem((LENGTH, 256), bf16),
             pltpu.SemaphoreType.DMA((n_copies,)),
             pltpu.SemaphoreType.DMA((n_copies,)),
             pltpu.SemaphoreType.DMA((n_local,)),
@@ -1145,6 +1178,28 @@
             collective_id=2, has_side_effects=True, vmem_limit_bytes=VMEM_LIMIT
         ),
     )(*args)
+
+
+def hand_over_kernel(*refs):
+    n = len(refs) // 2
+    sems = refs[-1]
+    copies = [pltpu.make_async_copy(refs[i], refs[n + i], sems.at[i]) for i in range(n)]
+    for copy in copies:
+        copy.start()
+    for copy in copies:
+        copy.wait()
+
+
+def hand_over(*arrays):
+    any_ = pl.BlockSpec(memory_space=pl.ANY)
+    return pl.pallas_call(
+        hand_over_kernel,
+        name="hand_over",
+        out_shape=[jax.ShapeDtypeStruct(a.shape, a.dtype) for a in arrays],
+        in_specs=[pl.BlockSpec(memory_space=pltpu.VMEM)] * len(arrays),
+        out_specs=[any_] * len(arrays),
+        scratch_shapes=[pltpu.SemaphoreType.DMA((len(arrays),))],
+    )(*arrays)
 
 
 def shards(
@@ -1167,8 +1222,10 @@
         w_down, table,
     )
     gt, block, g_q, g_k, g_v, g_out, g_gate, g_up, g_down, gg = back(
-        dab, pd, ggu, h1, gq, wo,
-        dacc, dx1, tokens[0], x1, gain2, pre, qb, kb, vb, ob, gains, table,
+        dab, pd, ggu, h1, gq, wo, dacc, dx1, tokens[0], x1, pre, qb, kb, vb, ob, gain2, gains, table,
+    )
+    block, gt, g_q, g_k, g_v, g_out, g_gate, g_up, g_down = hand_over(
+        block, gt, g_q, g_k, g_v, g_out, g_gate, g_up, g_down
     )
     gg = gg[0]
     return (

time: 294 us -> 277 us (0.942)
  local copies, waits for them, and re-layouts: 16 us -> 3.53 us
  Pallas kernels: 275 us -> 271 us
    unnamed x15 -> x0, local copies, waits for them, and re-layouts: 12.5 us -> none
    pallas_call x1, Pallas kernels: 118 us -> 108 us  [back(): pl.pallas_call(back_kernel, name='attn_backward', out_shape=[sds((SPAN, W...]
    pallas_call x0 -> x1, Pallas kernels: none -> 3.58 us  [hand_over(): pl.pallas_call(hand_over_kernel, name='hand_over', out_shape=[jax.ShapeDt...]
where the time goes in v5:
time: 277 us
  Pallas kernels  271 us (98%)
  local copies, waits for them, and re-layouts  3.53 us (1%)
    pallas_call x1, Pallas kernels, front(): pl.pallas_call(front_kernel, name='attn_forward', out_shape=[sds((SPAN, W...  159 us
    pallas_call x1, Pallas kernels, back(): pl.pallas_call(back_kernel, name='attn_backward', out_shape=[sds((SPAN, W...  108 us

profile of v5, /device:TPU:0, one launch (start us, length us, event | category | flops | bytes accessed | tf_op | source)
XLA Modules:
  0.0 276.8 jit_solution(15003812363681925656)
XLA Ops:
  2.0 0.1 pad.7.clone
  2.0 0.1 pad.8.clone
  2.1 0.7 maximum_maximum_fusion
  2.8 0.1 copy.29
  2.9 0.6 pad.4.extra
  3.5 158.5 %attn_forward.1 = (f32[128,2048]{1,0:T(8,128)}, f32[128,2048]{1,0:T(8,128)}, bf16[128,2048]{1,0:T(8,128)(2,1)}, f32[8,2048]{1,0:T(8,128)}, bf16[8,128,2048]{2,1,...) custom-call(bf16[128,2048]{1,0:T(8,128)(2,1)} %bitcast.14, ...), custom_call_target="tpu_custom_call" | custom-call | tf_op jit(solution)/shard_map/attn_forward/pallas_call | solution.py:784
  162.1 108.4 %attn_backward.1 = (f32[128,2048]{1,0:T(8,128)}, bf16[128,2048]{1,0:T(8,128)(2,1)}, f32[16,2048]{1,0:T(8,128)}, f32[16,1024]{1,0:T(8,128)}, f32[16,1024]{1,0:T(8...) custom-call(bf16[128,2048]{1,0:T(8,128)(2,1)} %get-tuple-element.48., ...), custom_call_target="tpu_custom_call" | custom-call | tf_op jit(solution)/shard_map/attn_backward/pallas_call | solution.py:1141
  270.5 3.6 %hand_over.1 = (bf16[128,2048]{1,0:T(8,128)(2,1)}, f32[128,2048]{1,0:T(8,128)}, f32[16,2048]{1,0:T(8,128)}, f32[16,1024]{1,0:T(8,128)}, f32[16,1024]{1,0:T(8,128...) custom-call(bf16[128,2048]{1,0:T(8,128)(2,1)} %get-tuple-element.64.refs_0_, ...), custom_call_target="tpu_custom_call" | custom-call | tf_op jit(solution)/shard_map/hand_over/pallas_call | solution.py:1195
  274.1 1.3 fusion
  275.4 1.3 slice_bitcast_fusion

commit v6 on v5

--- a/solution.py
+++ b/solution.py
@@ -712,8 +712,6 @@
     g_cot.wait_chip(2)
     forward(2)
     rs.combine(order[1])
-    back(2)
-    rs.combine(order[0])
     cm.finish()
 
     def down_grad(m, _):
@@ -725,13 +723,13 @@
                 wd_b[yy, zz, cut, :] = o[:, lo : lo + 128]
         return 0
 
-    lax.fori_loop(0, 1, down_grad, 0)
-    rs.combine(order[2])
-    lax.fori_loop(1, FFS // 256, down_grad, 0)
+    lax.fori_loop(0, FFS // 256, down_grad, 0)
     r_d = DpScatter(cm, wd_b, d_acc, d_one, None, co, 128)
     r_d.start()
-
-    for k in range(4):
+    back(2)
+    rs.combine(order[0])
+
+    for k in (0, 3, 1, 2):
         n = order[k]
         rows = pl.ds(pl.multiple_of(chip_of(k) * 256, 256), 256)
 
@@ -741,6 +739,8 @@
             return 0
 
         lax.fori_loop(0, WIDTH // 512, down, 0)
+        if k == 3:
+            rs.combine(order[2])
     outs.append(cm.here(pdv, pd_o))
 
     def gate_up(m, _):
@@ -899,8 +899,7 @@
     g_dab = SeqGather(cm, dab_loc, dab, co)
     g_dab.start()
     r_d = DpScatter(cm, None, d_acc, None, d_two, co, 128)
-    for copy in l_in:
-        copy.wait()
+    l_in[3].wait()
     r_d.send_second()
     r_m = DpScatter(cm, ggu, m_acc, m_one, m_two, co, 16)
     r_m.start()
@@ -926,6 +925,8 @@
     dk[...] = jnp.zeros_like(dk)
     dv[...] = jnp.zeros_like(dv)
     gacc[...] = jnp.zeros_like(gacc)
+    for n in (0, 1, 2, 4, 5, 6):
+        l_in[n].wait()
     l_wo.wait()
 
     def out_back(k):
@@ -1023,9 +1024,9 @@
 
     lax.fori_loop(0, 2, chip_back, 0)
     rs.combine(slot_of(2))
-    r_m.mid()
     lax.fori_loop(2, 4, chip_back, 0)
     rs.combine(slot_of(0))
+    r_m.mid()
 
     for m in range(8):
         l_h1[m].wait()

time: 277 us -> 264 us (0.953)
  Pallas kernels: 271 us -> 258 us
    pallas_call x1, Pallas kernels: 108 us -> 96.3 us  [back(): pl.pallas_call(back_kernel, name='attn_backward', out_shape=[sds((SPAN, W...]
where the time goes in v6:
time: 264 us
  Pallas kernels  258 us (98%)
  local copies, waits for them, and re-layouts  3.53 us (1%)
    pallas_call x1, Pallas kernels, front(): pl.pallas_call(front_kernel, name='attn_forward', out_shape=[sds((SPAN, W...  158 us
    pallas_call x1, Pallas kernels, back(): pl.pallas_call(back_kernel, name='attn_backward', out_shape=[sds((SPAN, W...  96.3 us

profile of v6, /device:TPU:0, one launch (start us, length us, event | category | flops | bytes accessed | tf_op | source)
XLA Modules:
  0.0 263.9 jit_solution(560534422955441154)
XLA Ops:
  2.0 0.1 pad.7.clone
  2.0 0.1 pad.8.clone
  2.1 0.7 maximum_maximum_fusion
  2.8 0.1 copy.29
  2.9 0.6 pad.4.extra
  3.5 157.7 %attn_forward.1 = (f32[128,2048]{1,0:T(8,128)}, f32[128,2048]{1,0:T(8,128)}, bf16[128,2048]{1,0:T(8,128)(2,1)}, f32[8,2048]{1,0:T(8,128)}, bf16[8,128,2048]{2,1,...) custom-call(bf16[128,2048]{1,0:T(8,128)(2,1)} %bitcast.14, ...), custom_call_target="tpu_custom_call" | custom-call | tf_op jit(solution)/shard_map/attn_forward/pallas_call | solution.py:784
  161.3 96.3 %attn_backward.1 = (f32[128,2048]{1,0:T(8,128)}, bf16[128,2048]{1,0:T(8,128)(2,1)}, f32[16,2048]{1,0:T(8,128)}, f32[16,1024]{1,0:T(8,128)}, f32[16,1024]{1,0:T(8...) custom-call(bf16[128,2048]{1,0:T(8,128)(2,1)} %get-tuple-element.48., ...), custom_call_target="tpu_custom_call" | custom-call | tf_op jit(solution)/shard_map/attn_backward/pallas_call | solution.py:1142
  257.6 3.6 %hand_over.1 = (bf16[128,2048]{1,0:T(8,128)(2,1)}, f32[128,2048]{1,0:T(8,128)}, f32[16,2048]{1,0:T(8,128)}, f32[16,1024]{1,0:T(8,128)}, f32[16,1024]{1,0:T(8,128...) custom-call(bf16[128,2048]{1,0:T(8,128)(2,1)} %get-tuple-element.64.refs_0_, ...), custom_call_target="tpu_custom_call" | custom-call | tf_op jit(solution)/shard_map/hand_over/pallas_call | solution.py:1196
  261.2 1.3 fusion
  262.5 1.3 slice_bitcast_fusion
